TPU v7x, 512 devices: a whole 4x4x16 slice. The times are simulated.
512 devices in a mesh: group: 16 (over x, z_lo), sample: 32 (over y, z_hi, core).
Axes of the slice: x: 4, y: 4, z: 16 (z_hi: 4, z_lo: 4; z = z_hi * 4 + z_lo), core: 2. Of those that a mesh axis runs over, the one named last changes fastest.
Arguments:
- response_rows: bfloat16 [65536, 4096], P(('group', 'sample')), may hold values from -6 to 6
- prompt_rows: bfloat16 [8192, 4096], P(('group', 'sample')), may hold values from -6 to 6
- queries: bfloat16 [65536, 4096], P(('group', 'sample')), may hold values from -4.5 to 4.5
- response_keys: bfloat16 [65536, 512], P(('group', 'sample')), may hold values from -6 to 6
- prompt_keys: bfloat16 [8192, 512], P(('group', 'sample')), may hold values from -5 to 5
- cotangent: bfloat16 [65536, 4096], P(('group', 'sample')), may hold values from -96 to 96
- segment_index: int32 [512, 128], P(('group', 'sample')), may hold values from 0 to 7, never falling along the last dimension, each value on 1 to 32 neighbouring positions
- prompt_choice: int32 [512, 8], P(('group', 'sample')), may hold values from 0 to 3
- frozen_value_weight: bfloat16 [4096, 512], P('sample'), may hold values from -0.09375 to 0.09375
- value_adapter_down: bfloat16 [4096, 16], P('sample'), may hold values from -0.09375 to 0.09375
- value_adapter_up: bfloat16 [16, 512], replicated, may hold values from -1.5 to 1.5
Outputs:
- response_grad: bfloat16 [65536, 4096], P(('group', 'sample'))
- prompt_grad: bfloat16 [8192, 4096], P(('group', 'sample'))
- response_key_grad: bfloat16 [65536, 512], P(('group', 'sample'))
- prompt_key_grad: bfloat16 [8192, 512], P(('group', 'sample'))
- first_grad: float32 [4096, 16], P('sample')
- second_grad: float32 [16, 512], replicated
Inputs may be any that keep to these rules, and one draw needn't show every extreme that they name: `segment_index`: within the 128 tokens of one device the response number never falls; each of the 8 responses has 1 to 32 tokens, and one has exactly 32.
All inputs are finite; a program needn't handle non-finite values.
Results may differ from a plain program's by a relative error of at most 0.015.
Values may be sent and summed in bfloat16 or wider, within the bound.
No kernel may reach another device: no remote copies, remote signals or barrier semaphores. Data moves between devices by JAX's collectives and lax.ppermute only.
A program may use at most 128 MiB of HBM per device.

v0:
```python
import jax
import jax.numpy as jnp
from jax import lax
from jax.sharding import PartitionSpec as P

HEADS = 32
KV_HEADS = 4
HEAD_DIM = 128
PROMPT_LEN = 128


adapter_scale = 2.0


def contract_final_axis(left, right):
    return lax.dot_general(
        left, right, (((1,), (1,)), ((), ())), preferred_element_type=jnp.float32
    )


def contract_first(left, right):
    return lax.dot_general(
        left, right, (((0,), (0,)), ((), ())), preferred_element_type=jnp.float32
    )


def visibility(segments, choices, prompt_total):
    tokens_here = segments.shape[0]
    onehot = (segments[:, None] == jnp.arange(choices.shape[0], dtype=jnp.int32)[None, :]).astype(
        jnp.int32
    )
    token_prompt = jnp.sum(onehot * choices[None, :], axis=1)
    key_prompt = jnp.arange(prompt_total, dtype=jnp.int32) // PROMPT_LEN
    prompt_seen = token_prompt[:, None] == key_prompt[None, :]
    position = jnp.arange(tokens_here, dtype=jnp.int32)
    own_seen = (segments[:, None] == segments[None, :]) & (position[None, :] <= position[:, None])
    return jnp.concatenate([prompt_seen, own_seen], axis=1)


def head_parts(query_rows, cotangent_rows, head_index):
    tokens_here = query_rows.shape[0]
    group_size = HEADS // KV_HEADS
    block_width = group_size * HEAD_DIM
    query_block = query_rows[:, head_index * block_width : (head_index + 1) * block_width].reshape(
        tokens_here, group_size, HEAD_DIM
    )
    cotangent_block = cotangent_rows[
        :, head_index * block_width : (head_index + 1) * block_width
    ].reshape(tokens_here, group_size, HEAD_DIM)
    return (query_block, cotangent_block)


def attend(query_rows, cotangent_rows, key_rows, value_rows, visible):
    score_scale = HEAD_DIM ** (-0.5)
    key_list = []
    value_list = []
    for head_index in range(KV_HEADS):
        query_block, cotangent_block = head_parts(query_rows, cotangent_rows, head_index)
        key_block = key_rows[:, head_index * HEAD_DIM : (head_index + 1) * HEAD_DIM]
        value_block = value_rows[:, head_index * HEAD_DIM : (head_index + 1) * HEAD_DIM]
        scores = (
            jnp.einsum("tgd,sd->gts", query_block, key_block, preferred_element_type=jnp.float32)
            * score_scale
        )
        scores = jnp.where(visible[None], scores, -1e30)
        row_top = jnp.max(scores, axis=-1, keepdims=True)
        powers = jnp.exp(scores - row_top)
        softmax_full = powers / jnp.sum(powers, axis=-1, keepdims=True)
        softmax_low = softmax_full.astype(jnp.bfloat16)
        mixture = jnp.einsum(
            "gts,sd->gtd", softmax_low, value_block, preferred_element_type=jnp.float32
        )
        row_delta = jnp.einsum("tgd,gtd->gt", cotangent_block.astype(jnp.float32), mixture)
        grad_softmax = jnp.einsum(
            "tgd,sd->gts", cotangent_block, value_block, preferred_element_type=jnp.float32
        )
        grad_scores = (softmax_full * (grad_softmax - row_delta[..., None])).astype(jnp.bfloat16)
        key_list.append(
            jnp.einsum("gts,tgd->sd", grad_scores, query_block, preferred_element_type=jnp.float32)
            * score_scale
        )
        value_list.append(
            jnp.einsum(
                "gts,tgd->sd", softmax_low, cotangent_block, preferred_element_type=jnp.float32
            )
        )
    return (jnp.concatenate(key_list, axis=1), jnp.concatenate(value_list, axis=1))


def on_device(
    response_rows,
    prompt_rows,
    queries,
    response_keys,
    prompt_keys,
    cotangent,
    segment_index,
    prompt_choice,
    frozen_value_weight,
    value_adapter_down,
    value_adapter_up,
):
    tokens_here = response_rows.shape[0]
    prompt_here = prompt_rows.shape[0]
    local_rows = jnp.concatenate([response_rows, prompt_rows], axis=0)
    weight_piece = lax.all_gather(frozen_value_weight, "sample", axis=0, tiled=True)
    down_factor_piece = lax.all_gather(value_adapter_down, "sample", axis=0, tiled=True)
    base_run = jnp.dot(local_rows, weight_piece, preferred_element_type=jnp.float32)
    low_run = jnp.dot(local_rows, down_factor_piece, preferred_element_type=jnp.float32)
    down_projection = low_run.astype(jnp.bfloat16)
    value_inputs = (
        base_run
        + adapter_scale
        * jnp.dot(down_projection, value_adapter_up, preferred_element_type=jnp.float32)
    ).astype(jnp.bfloat16)
    key_prefix, value_prefix = (
        lax.all_gather(prompt_keys, "sample", axis=0, tiled=True),
        lax.all_gather(value_inputs[tokens_here:], "sample", axis=0, tiled=True),
    )
    prompt_total = key_prefix.shape[0]
    visible = visibility(segment_index.reshape(-1), prompt_choice.reshape(-1), prompt_total)
    key_rows = jnp.concatenate([key_prefix, response_keys], axis=0)
    value_rows = jnp.concatenate([value_prefix, value_inputs[:tokens_here]], axis=0)
    key_grads, value_grads = attend(queries, cotangent, key_rows, value_rows, visible)
    own_key_grads = key_grads[prompt_total:]
    own_value_grads = value_grads[prompt_total:]
    prompt_key_part, prompt_value_part = (
        lax.psum_scatter(key_grads[:prompt_total], "sample", scatter_dimension=0, tiled=True),
        lax.psum_scatter(value_grads[:prompt_total], "sample", scatter_dimension=0, tiled=True),
    )
    value_low_rank = jnp.concatenate(
        [own_value_grads.astype(jnp.bfloat16), prompt_value_part.astype(jnp.bfloat16)], axis=0
    )
    low_rank_backward = contract_final_axis(value_low_rank, value_adapter_up).astype(jnp.bfloat16)
    adapter_backward = adapter_scale * contract_final_axis(low_rank_backward, down_factor_piece)
    frozen_backward = contract_final_axis(
        value_low_rank, lax.all_gather(frozen_value_weight, "sample", axis=0, tiled=True)
    )
    output_gradient = (frozen_backward + adapter_backward).astype(jnp.bfloat16)
    first_part = contract_first(local_rows, low_rank_backward)
    second_part = contract_first(down_projection, value_low_rank)
    adapter_factor = adapter_scale * float(
        (tokens_here + prompt_here) * lax.axis_size("group") * lax.axis_size("sample")
    ) ** (-0.5)
    slice_rows = value_adapter_down.shape[0]
    first_sum, second_sum = lax.psum((first_part, second_part), ("group", "sample"))
    first_slice = lax.dynamic_slice_in_dim(
        first_sum, lax.axis_index("sample") * slice_rows, slice_rows, 0
    )
    return (
        output_gradient[:tokens_here],
        output_gradient[tokens_here:],
        own_key_grads.astype(jnp.bfloat16),
        prompt_key_part.astype(jnp.bfloat16),
        first_slice * adapter_factor,
        second_sum * adapter_factor,
    )


def solution(mesh):
    in_specs = (
        P(("group", "sample"), None),
        P(("group", "sample"), None),
        P(("group", "sample"), None),
        P(("group", "sample"), None),
        P(("group", "sample"), None),
        P(("group", "sample"), None),
        P(("group", "sample"), None),
        P(("group", "sample"), None),
        P("sample", None),
        P("sample", None),
        P(),
    )
    out_specs = (
        P(("group", "sample"), None),
        P(("group", "sample"), None),
        P(("group", "sample"), None),
        P(("group", "sample"), None),
        P("sample", None),
        P(),
    )
    return jax.shard_map(
        on_device, mesh=mesh, in_specs=in_specs, out_specs=out_specs, check_vma=False
    )
```

profile of v0, /device:TPU:1, one launch (start us, length us, event | category | flops | bytes accessed | tf_op | source)
XLA Modules:
  0.0 880.2 jit_solution(14177063164198225989)
XLA Ops:
  8.8 62.9 %all_gather.13 = bf16[512,512]{1,0:T(8,128)(2,1)S(1)} all-gather(bf16[16,512]{1,0:T(8,128)(2,1)} %param.15), channel_id=1, replica_groups=mesh['group'=16,'sample'=32] {'sample'}, dimensions={0}, use_global_device_ids=true | all-gather | bytes 540672 | tf_op jit(solution)/shard_map/all_gather | solution.py:117
  72.6 1.3 fusion.108
  77.6 1.6 constant_dynamic-update-slice_fusion
  79.2 3.4 fusion.109
  82.5 3.3 fusion.111
  85.9 2.1 fusion.110
  88.0 3.9 fusion.112
  91.9 2.1 fusion.53
  97.2 1.4 copy-done.8
  99.5 1.1 slice.103
  100.6 2.6 copy.161
  104.1 47.1 %all_gather.15 = bf16[4096,16]{0,1:T(8,128)(2,1)S(1)} all-gather(bf16[128,16]{0,1:T(8,128)(2,1)S(1)} %copy-done.40), channel_id=1, replica_groups=mesh['group'=16,'sample'=32] {'sample'}, dimensions={0}, use_global_device_ids=true | all-gather | bytes 135168 | tf_op jit(solution)/shard_map/all_gather | solution.py:107
  151.1 1.3 constant_dynamic-update-slice_fusion.3
  153.6 52.3 %reduce-scatter.7.cloned.1.call-done = f32[16,512]{1,0:T(8,128)} async-done(((f32[512,512]{1,0:T(8,128)}), f32[16,512]{1,0:T(8,128)}) %reduce-scatter.7.cloned.1.call-update) | async-done | bytes 32784
  208.0 94.3 %all-gather.2.cloned.1.call-done = bf16[4096,512]{1,0:T(8,128)(2,1)} async-done(((bf16[128,512]{1,0:T(8,128)(2,1)}), bf16[4096,512]{1,0:T(8,128)(2,1)}) %all-gather.2.cloned.1.call-update) | async-done | bytes 4194320 | tf_op jit(solution)/shard_map/all_gather | solution.py:137
  302.3 3.1 fusion.49
  305.4 51.6 %all_gather.16 = bf16[512,512]{1,0:T(8,128)(2,1)S(1)} all-gather(bf16[16,512]{1,0:T(8,128)(2,1)S(1)} %slice.106), channel_id=1, replica_groups=mesh['group'=16,'sample'=32] {'sample'}, dimensions={0}, use_global_device_ids=true | all-gather | bytes 540672 | tf_op jit(solution)/shard_map/all_gather | solution.py:118
  357.7 1.0 fusion.48
  358.7 3.6 fusion.38
  362.3 2.0 fusion.46
  364.3 3.5 fusion.42
  367.8 2.0 fusion.47
  369.8 2.7 fusion.40
  373.0 2.6 fusion.44
  375.7 1.1 copy-done.7
  377.0 1.3 copy.163
  378.5 101.0 %psum.15 = f32[16,512]{1,0:T(8,128)S(1)} all-reduce(f32[16,512]{1,0:T(8,128)S(1)} %fusion.73), channel_id=1, replica_groups=mesh['group'=16,'sample'=32] {'group','sample'}, use_global_device_ids=true, to_apply=%region_12.13 | all-reduce | flops 8192 | bytes 65536 | tf_op jit(solution)/shard_map/psum | solution.py:146
  480.6 278.7 %all-reduce.2.cloned.1.call-done = f32[4096,16]{0,1:T(8,128)} async-done(((f32[4096,16]{0,1:T(8,128)}), f32[4096,16]{0,1:T(8,128)}) %all-reduce.2.cloned.1.call-update) | async-done | bytes 262160 | tf_op jit(solution)/shard_map/psum | solution.py:146
  759.3 1.3 dynamic-slice_multiply_fusion
  761.5 3.7 fusion.4
  765.9 1.1 slice.104
  767.8 104.3 %reduce-scatter.9.cloned.1.call-done = f32[16,512]{1,0:T(8,128)} async-done(((f32[512,512]{1,0:T(8,128)}), f32[16,512]{1,0:T(8,128)}) %reduce-scatter.9.cloned.1.call-update) | async-done | bytes 32784
  (132 shorter events, 20.6 us)
Async XLA Ops:
  7.2 145.8 %copy-start = (bf16[16,512]{1,0:T(8,128)(2,1)S(1)}, bf16[16,512]{1,0:T(8,128)(2,1)}, u32[]{:S(2)}) copy-start(bf16[16,512]{1,0:T(8,128)(2,1)} %param.21) | copy-start | bytes 49156
  7.2 198.6 %reduce-scatter.7.cloned.1.call-start = ((), (), s32[]{:S(2)}) async-start(), calls=%async_computation.4 | async-start | bytes 1081344
  71.7 4.1 copy-start.15
  75.7 6.8 copy-start.25
  75.9 6.7 copy-start.26
  76.3 19.0 %copy-start.12 = (bf16[128,1024]{0,1:T(8,128)(2,1)}, bf16[128,1024]{0,1:T(8,128)(2,1)S(1)}, u32[]{:S(2)}) copy-start(bf16[128,1024]{0,1:T(8,128)(2,1)S(1)} %copy.93) | copy-start | bytes 786436
  77.4 19.3 %copy-start.11 = (bf16[128,1024]{0,1:T(8,128)(2,1)}, bf16[128,1024]{0,1:T(8,128)(2,1)S(1)}, u32[]{:S(2)}) copy-start(bf16[128,1024]{0,1:T(8,128)(2,1)S(1)} %copy.97) | copy-start | bytes 786436
  77.6 8.3 copy-start.29
  82.5 9.4 %copy-start.39 = (f32[8,128]{1,0:T(8,128)}, f32[8,128]{1,0:T(8,128)S(1)}, u32[]{:S(2)}) copy-start(f32[8,128]{1,0:T(8,128)S(1)} %get-tuple-element.38) | copy-start | bytes 12292
  85.9 9.2 %copy-start.38 = (f32[8,128]{1,0:T(8,128)}, f32[8,128]{1,0:T(8,128)S(1)}, u32[]{:S(2)}) copy-start(f32[8,128]{1,0:T(8,128)S(1)} %get-tuple-element.42) | copy-start | bytes 12292
  87.9 8.5 copy-start.9
  87.9 8.5 copy-start.37
  91.9 5.3 copy-start.35
  91.9 3.2 copy-start.10
  96.6 2.2 copy-start.1
  99.5 4.6 copy-start.40
  100.6 51.9 %copy-start.28 = (bf16[16,4096]{1,0:T(8,128)(2,1)S(1)}, bf16[16,4096]{1,0:T(8,128)(2,1)}, u32[]{:S(2)}) copy-start(bf16[16,4096]{1,0:T(8,128)(2,1)} %param.12) | copy-start | bytes 393220
  103.2 199.0 %all-gather.2.cloned.1.call-start = ((), (), s32[]{:S(2)}) async-start(), calls=%async_computation.2 | async-start | bytes 4325376 | tf_op jit(solution)/shard_map/all_gather | solution.py:137
  104.0 655.3 %all-reduce.2.cloned.1.call-start = ((), (), s32[]{:S(2)}) async-start(), calls=%async_computation.3 | async-start | bytes 524288 | tf_op jit(solution)/shard_map/psum | solution.py:146
  104.1 103.8 %copy-start.20 = (bf16[128,512]{0,1:T(8,128)(2,1)}, bf16[128,512]{0,1:T(8,128)(2,1)S(1)}, u32[]{:S(2)}) copy-start(bf16[128,512]{0,1:T(8,128)(2,1)S(1)} %slice.185) | copy-start | bytes 393220
  206.9 95.4 %copy-start.31 = (bf16[144,16]{0,1:T(8,128)(2,1)}, bf16[144,16]{0,1:T(8,128)(2,1)S(1)}, u32[]{:S(2)}) copy-start(bf16[144,16]{0,1:T(8,128)(2,1)S(1)} %convolution_convert_fusion) | copy-start | bytes 13828
  207.9 149.8 %copy-start.17 = (bf16[128,1024]{0,1:T(8,128)(2,1)S(1)}, bf16[128,1024]{0,1:T(8,128)(2,1)}, u32[]{:S(2)}) copy-start(bf16[128,1024]{0,1:T(8,128)(2,1)} %copy.101) | copy-start | bytes 786436
  207.9 664.2 %reduce-scatter.9.cloned.1.call-start = ((), (), s32[]{:S(2)}) async-start(), calls=%async_computation.5 | async-start | bytes 1081344
  302.3 55.4 %copy-start.6 = (bf16[8,128,640]{1,2,0:T(8,128)(2,1)S(1)}, bf16[8,128,640]{1,2,0:T(8,128)(2,1)}, u32[]{:S(2)}) copy-start(bf16[8,128,640]{1,2,0:T(8,128)(2,1)} %copy-done.5) | copy-start | bytes 3932164
  358.7 3.6 copy-start.4
  364.3 3.5 copy-start.2
  369.8 3.2 copy-start.24
  369.8 3.2 copy-start.36
  372.9 2.7 copy-start.22
  373.0 2.7 copy-start.23
  376.8 103.3 %copy-start.14 = (bf16[4096,16]{0,1:T(8,128)(2,1)S(1)}, bf16[4096,16]{0,1:T(8,128)(2,1)}, u32[]{:S(2)}) copy-start(bf16[4096,16]{0,1:T(8,128)(2,1)} %copy-done.13) | copy-start | bytes 393220
  376.8 103.3 %copy-start.32 = (bf16[144,16]{0,1:T(8,128)(2,1)S(1)}, bf16[144,16]{0,1:T(8,128)(2,1)}, u32[]{:S(2)}) copy-start(bf16[144,16]{0,1:T(8,128)(2,1)} %copy-done.31) | copy-start | bytes 13828
  (13 other events, 18.1 us)
Sparse Core Ops, SparseCore 0:
  103.3 102.4 reduce-scatter.6
  209.4 92.7 all-gather.1
  308.6 450.6 all-reduce.1
  763.5 108.5 reduce-scatter.8
where the time goes:
time: 882 us; the launch traced here: 880 us
  waiting for transfers between devices  530 us (60%)
  blocking collectives  263 us (30%)
  matrix products  41.9 us (5%)
  local copies, waits for them, and re-layouts  24.3 us (3%)
  between operations  14.4 us (2%)
    psum x1, waiting for transfers between devices, on_device(): lax.psum((first_part, second_part), ('group', 'sample'))  279 us
    unnamed x6, waiting for transfers between devices  157 us
    psum x1, blocking collectives, on_device(): lax.psum((first_part, second_part), ('group', 'sample'))  101 us
    all_gather x1, waiting for transfers between devices, on_device(): lax.all_gather(frozen_value_weight, 'sample', axis=0, tiled=True)  94.3 us
    all_gather x1, blocking collectives, on_device(): lax.all_gather(prompt_keys, 'sample', axis=0, tiled=True)  62.9 us
    all_gather x1, blocking collectives, on_device(): lax.all_gather(value_inputs[tokens_here:], 'sample', axis=0, tiled=True)  51.6 us
    all_gather x1, blocking collectives, on_device(): lax.all_gather(value_adapter_down, 'sample', axis=0, tiled=True)  47.1 us
  transfers between devices with their start and end apart: 4, of which 4 were waited for; matrix products, arithmetic and copies ran while one was open for 4% of the time, Pallas kernels for 0%

commit v1 on v0

v1 whole, which is shorter than its diff:
```python
import jax
import jax.numpy as jnp
import numpy as np
from jax import lax
from jax.experimental import pallas as pl
from jax.experimental.pallas import tpu as pltpu
from jax.sharding import Mesh, PartitionSpec as P

HEADS = 32
KV_HEADS = 4
HEAD_DIM = 128
GROUP_SIZE = HEADS // KV_HEADS
PROMPT_LEN = 128
PROMPTS = 4
RANK = 16
TOKENS = 128
D = 4096
SCALE = HEAD_DIM**-0.5
ADAPTER_SCALE = 2.0
AXES = ("x", "zl", "y", "zh", "c")
SAMPLE = ("y", "zh", "c")
GROUP = ("x", "zl")
PAIR = 2 * TOKENS
F32 = jnp.float32
BF16 = jnp.bfloat16


def swap(array, axis):
    return lax.all_to_all(array, axis, 0, 0, tiled=True)


def gather(array, axis):
    n = lax.axis_size(axis)
    return swap(jnp.broadcast_to(array[None], (n,) + array.shape), axis)


def nt(left, right):
    return lax.dot_general(left, right, (((1,), (1,)), ((), ())), preferred_element_type=F32)


def tn(left, right):
    return lax.dot_general(left, right, (((0,), (0,)), ((), ())), preferred_element_type=F32)


def nn(left, right):
    return jnp.dot(left, right, preferred_element_type=F32)


def expand(rows, chosen):
    zero = jnp.zeros_like(rows)
    return jnp.concatenate([jnp.where(chosen == p, rows, zero) for p in range(PROMPTS)], axis=1)


def pair_rows(ref, pair):
    first = 2 * pair * HEAD_DIM
    return jnp.concatenate(
        [ref[:, first : first + HEAD_DIM], ref[:, first + HEAD_DIM : first + 2 * HEAD_DIM]], axis=0
    )


def prompt_block(ref):
    return jnp.concatenate(
        [
            jnp.concatenate([ref[c, p, zh] for zh in range(4) for c in range(2)], axis=0)
            for p in range(PROMPTS)
        ],
        axis=1,
    )


def spread(ref, row, block):
    for p in range(PROMPTS):
        for zh in range(4):
            for c in range(2):
                s = (zh * 2 + c) * 16
                ref[c, p, zh, pl.ds(row, 16), :] = block[
                    s : s + 16, p * HEAD_DIM : (p + 1) * HEAD_DIM
                ].astype(ref.dtype)


def softmax_pair(key_cat, own_key, expanded, rows, bias):
    seen = nt(key_cat, expanded) * SCALE
    own = nt(own_key, rows) * SCALE + bias
    top = jnp.maximum(jnp.max(seen, axis=0, keepdims=True), jnp.max(own, axis=0, keepdims=True))
    seen, own = jnp.exp(seen - top), jnp.exp(own - top)
    total = jnp.sum(seen, axis=0, keepdims=True) + jnp.sum(own, axis=0, keepdims=True)
    return seen / total, own / total


def forward_kernel(
    q_ref, cot_ref, key_ref, own_key_ref, chosen_ref, bias_ref, x_ref, up_ref,
    send_ref, low_ref, back_ref,
    probs, own_probs, cots, back,
):
    k = pl.program_id(0)
    key_cat = prompt_block(key_ref)
    own_key = own_key_ref[...]
    chosen = chosen_ref[...]
    bias = bias_ref[...]
    for pair in range(GROUP_SIZE // 2):
        rows = pair_rows(q_ref, pair)
        seen, own = softmax_pair(key_cat, own_key, expand(rows, chosen), rows, bias)
        at = pl.ds(pair * PAIR, PAIR)
        probs[:, at] = seen.astype(BF16)
        own_probs[:, at] = own.astype(BF16)
        cot = pair_rows(cot_ref, pair)
        cots[at, : PROMPTS * HEAD_DIM] = expand(cot, chosen)
        cots[at, PROMPTS * HEAD_DIM :] = cot
    spread(send_ref, pl.multiple_of(k * 16, 16), nn(probs[...], cots[:, : PROMPTS * HEAD_DIM]))
    low = nn(own_probs[...], cots[:, PROMPTS * HEAD_DIM :]).astype(BF16)
    low_ref[...] = low

    @pl.when(k == 0)
    def _():
        back[...] = jnp.zeros_like(back)

    back[...] += nt(up_ref[...], low)

    @pl.when(k == KV_HEADS - 1)
    def _():
        back_low = back[...].astype(BF16)
        back_ref[...] = back_low
        first = nn(back_low, x_ref[...])
        for y in range(4):
            for zh in range(4):
                for c in range(2):
                    at = ((y * 4 + zh) * 2 + c) * 128
                    send_ref[c, y, zh, KV_HEADS * 16 :, :] = first[:, at : at + 128].astype(BF16)


def backward_kernel(
    q_ref, cot_ref, key_ref, value_ref, own_key_ref, own_value_ref, chosen_ref, bias_ref,
    send_ref, own_ref,
    grads, own_grads, queries,
):
    k = pl.program_id(0)
    key_cat, value_cat = prompt_block(key_ref), prompt_block(value_ref)
    own_key, own_value = own_key_ref[...], own_value_ref[...]
    chosen = chosen_ref[...]
    bias = bias_ref[...]
    for pair in range(GROUP_SIZE // 2):
        rows = pair_rows(q_ref, pair)
        expanded = expand(rows, chosen)
        at = pl.ds(pair * PAIR, PAIR)
        queries[at, : PROMPTS * HEAD_DIM] = expanded
        queries[at, PROMPTS * HEAD_DIM :] = rows
        seen, own = softmax_pair(key_cat, own_key, expanded, rows, bias)
        cot = pair_rows(cot_ref, pair)
        seen_grad = nt(value_cat, expand(cot, chosen))
        own_grad = nt(own_value, cot)
        delta = jnp.sum(seen.astype(BF16).astype(F32) * seen_grad, axis=0, keepdims=True) + jnp.sum(
            own.astype(BF16).astype(F32) * own_grad, axis=0, keepdims=True
        )
        grads[:, at] = (seen * (seen_grad - delta)).astype(BF16)
        own_grads[:, at] = (own * (own_grad - delta)).astype(BF16)
    spread(
        send_ref,
        pl.multiple_of(k * 16, 16),
        nn(grads[...], queries[:, : PROMPTS * HEAD_DIM]) * SCALE,
    )
    own_ref[...] = (nn(own_grads[...], queries[:, PROMPTS * HEAD_DIM :]) * SCALE).astype(BF16)


def whole(shape):
    return pl.BlockSpec(shape, lambda k: (0,) * len(shape))


def heads_of(rows, width):
    return pl.BlockSpec((rows, width), lambda k: (0, k))


PROMPT_SPEC = pl.BlockSpec((2, 4, 4, 16, HEAD_DIM), lambda k: (0, 0, 0, k, 0))
WIDE = GROUP_SIZE * HEAD_DIM
ROWS = GROUP_SIZE * TOKENS


def attend_forward(queries, cotangent, keys, own_keys, chosen, bias, rows, up):
    return pl.pallas_call(
        forward_kernel,
        grid=(KV_HEADS,),
        in_specs=[
            heads_of(TOKENS, WIDE),
            heads_of(TOKENS, WIDE),
            PROMPT_SPEC,
            heads_of(TOKENS, HEAD_DIM),
            whole((PAIR, HEAD_DIM)),
            whole((TOKENS, PAIR)),
            whole((TOKENS, D)),
            heads_of(RANK, HEAD_DIM),
        ],
        out_specs=[
            whole((2, 4, 4, KV_HEADS * 16 + RANK, HEAD_DIM)),
            heads_of(TOKENS, HEAD_DIM),
            whole((RANK, TOKENS)),
        ],
        out_shape=[
            jax.ShapeDtypeStruct((2, 4, 4, KV_HEADS * 16 + RANK, HEAD_DIM), BF16),
            jax.ShapeDtypeStruct((TOKENS, KV_HEADS * HEAD_DIM), BF16),
            jax.ShapeDtypeStruct((RANK, TOKENS), BF16),
        ],
        scratch_shapes=[
            pltpu.VMEM((TOKENS, ROWS), BF16),
            pltpu.VMEM((TOKENS, ROWS), BF16),
            pltpu.VMEM((ROWS, (PROMPTS + 1) * HEAD_DIM), BF16),
            pltpu.VMEM((RANK, TOKENS), F32),
        ],
        compiler_params=pltpu.CompilerParams(
            vmem_limit_bytes=40 << 20, dimension_semantics=("arbitrary",)
        ),
        cost_estimate=pl.CostEstimate(
            flops=2_000_000_000, bytes_accessed=5 << 20, transcendentals=1 << 20
        ),
        name="attend_forward",
    )(queries, cotangent, keys, own_keys, chosen, bias, rows, up)


def attend_backward(queries, cotangent, keys, values, own_keys, own_values, chosen, bias):
    return pl.pallas_call(
        backward_kernel,
        grid=(KV_HEADS,),
        in_specs=[
            heads_of(TOKENS, WIDE),
            heads_of(TOKENS, WIDE),
            PROMPT_SPEC,
            PROMPT_SPEC,
            heads_of(TOKENS, HEAD_DIM),
            heads_of(TOKENS, HEAD_DIM),
            whole((PAIR, HEAD_DIM)),
            whole((TOKENS, PAIR)),
        ],
        out_specs=[
            whole((2, 4, 4, KV_HEADS * 16, HEAD_DIM)),
            heads_of(TOKENS, HEAD_DIM),
        ],
        out_shape=[
            jax.ShapeDtypeStruct((2, 4, 4, KV_HEADS * 16, HEAD_DIM), BF16),
            jax.ShapeDtypeStruct((TOKENS, KV_HEADS * HEAD_DIM), BF16),
        ],
        scratch_shapes=[
            pltpu.VMEM((TOKENS, ROWS), BF16),
            pltpu.VMEM((TOKENS, ROWS), BF16),
            pltpu.VMEM((ROWS, (PROMPTS + 1) * HEAD_DIM), BF16),
        ],
        compiler_params=pltpu.CompilerParams(
            vmem_limit_bytes=40 << 20, dimension_semantics=("arbitrary",)
        ),
        cost_estimate=pl.CostEstimate(
            flops=3_000_000_000, bytes_accessed=5 << 20, transcendentals=1 << 20
        ),
        name="attend_backward",
    )(queries, cotangent, keys, values, own_keys, own_values, chosen, bias)


def reduce_parts(parts):
    shape = parts.shape[3:]
    got = swap(parts, "c").astype(F32)
    part = (got[0] + got[1]).astype(BF16)
    part = jnp.sum(swap(part, "y").astype(F32), axis=0).astype(BF16)
    part = jnp.sum(swap(part, "zh").astype(F32), axis=0)
    return part.reshape(shape)


def gather_parts(part):
    return gather(gather(gather(part, "zh"), "y"), "c")


def heads_first(rows):
    return rows.reshape(16, KV_HEADS, HEAD_DIM).transpose(1, 0, 2).reshape(KV_HEADS * 16, HEAD_DIM)


def heads_last(parts):
    return parts.reshape(KV_HEADS, 16, HEAD_DIM).transpose(1, 0, 2).reshape(16, KV_HEADS * HEAD_DIM)


def on_device(
    response_rows,
    prompt_rows,
    queries,
    response_keys,
    prompt_keys,
    cotangent,
    segment_index,
    prompt_choice,
    frozen_value_weight,
    value_adapter_down,
    value_adapter_up,
):
    segments = segment_index.reshape(TOKENS)
    onehot = (segments[:, None] == jnp.arange(8, dtype=jnp.int32)[None, :]).astype(jnp.int32)
    token_prompt = jnp.sum(onehot * prompt_choice.reshape(1, 8), axis=1)
    chosen = jnp.broadcast_to(jnp.tile(token_prompt, 2)[:, None], (PAIR, HEAD_DIM))
    position = jnp.arange(TOKENS, dtype=jnp.int32)
    own_seen = (segments[:, None] == segments[None, :]) & (position[:, None] <= position[None, :])
    bias = jnp.tile(jnp.where(own_seen, 0.0, -1e30).astype(F32), (1, 2))

    down_t = value_adapter_down.T
    key_part = jnp.concatenate([heads_first(prompt_keys), down_t], axis=0)
    key_all = gather_parts(key_part)
    own_columns = lax.dynamic_slice_in_dim(
        frozen_value_weight, lax.axis_index("x") * HEAD_DIM, HEAD_DIM, 1
    )
    weight = gather(gather(gather(gather(own_columns, "zh"), "x"), "y"), "c")
    weight = weight.transpose(1, 3, 0, 4, 2, 5).reshape(D, KV_HEADS * HEAD_DIM)
    prompt_columns = swap(prompt_rows.reshape(16, 32, 128).transpose(1, 0, 2), SAMPLE)

    send, low, back_t = attend_forward(
        queries, cotangent, key_all, response_keys, chosen, bias, response_rows, value_adapter_up
    )
    got = reduce_parts(send)
    prompt_low = heads_last(got[: KV_HEADS * 16].astype(BF16))
    first_sum = got[KV_HEADS * 16 :]

    down_full = key_all[:, :, :, KV_HEADS * 16 :].transpose(3, 1, 2, 0, 4).reshape(RANK, D)
    local_rows = jnp.concatenate([response_rows, prompt_rows], axis=0)
    first_proj = nt(local_rows, down_full).astype(BF16)
    value_low = jnp.concatenate([low, prompt_low], axis=0)
    prompt_back = nt(prompt_low, value_adapter_up).astype(BF16)
    back_low = jnp.concatenate([back_t.T, prompt_back], axis=0)

    second_part = tn(first_proj, value_low)
    packed = jnp.concatenate(
        [
            second_part.reshape(RANK, 32, 16).transpose(1, 0, 2),
            jnp.broadcast_to(prompt_back.astype(F32)[None], (32, 16, RANK)),
            jnp.zeros((32, 16, 96), F32),
        ],
        axis=2,
    )
    packed = swap(packed, SAMPLE)
    second_sum = jnp.sum(packed[:, :, :16], axis=0)
    first_sum = first_sum + tn(
        packed[:, :, 16:32].reshape(512, RANK).astype(BF16), prompt_columns.reshape(512, 128)
    )
    both = jnp.concatenate([first_sum, second_sum, jnp.zeros((RANK, 112), F32)], axis=1)
    both = jnp.sum(gather(both, GROUP), axis=0)
    factor = ADAPTER_SCALE * float(73728) ** (-0.5)
    first_grad = both[:, :128].T * factor
    second_grad = gather(both[:, 128:] * factor, SAMPLE)[:, :, :16]
    second_grad = second_grad.transpose(1, 0, 2).reshape(RANK, KV_HEADS * HEAD_DIM)

    values = (nn(local_rows, weight) + ADAPTER_SCALE * nn(first_proj, value_adapter_up)).astype(BF16)
    value_all = gather_parts(heads_first(values[TOKENS:]))
    key_send, own_key_grad = attend_backward(
        queries, cotangent, key_all, value_all, response_keys, values[:TOKENS], chosen, bias
    )
    prompt_key_grad = heads_last(reduce_parts(key_send).astype(BF16))
    grads = (nt(value_low, weight) + ADAPTER_SCALE * nn(back_low, down_full)).astype(BF16)
    return (
        grads[:TOKENS],
        grads[TOKENS:],
        own_key_grad,
        prompt_key_grad,
        first_grad,
        second_grad,
    )


def solution(mesh):
    fine = Mesh(np.asarray(mesh.devices).reshape(4, 4, 4, 4, 2), AXES)
    rows = P(AXES, None)
    in_specs = (rows,) * 8 + (P(SAMPLE, None), P(SAMPLE, None), P())
    out_specs = (rows,) * 4 + (P(SAMPLE, None), P())
    return jax.shard_map(
        on_device, mesh=fine, in_specs=in_specs, out_specs=out_specs, check_vma=False
    )
```

time: 882 us -> 323 us (0.37)
  waiting for transfers between devices: 530 us -> 135 us
  blocking collectives: 263 us -> 63.6 us
  starting transfers between devices: 0.16 us -> 64 us
  matrix products: 41.9 us -> 7.38 us
  between operations: 14.4 us -> 1.09 us
  Pallas kernels: 0 us -> 11.6 us
    psum x1 -> x0, waiting for transfers between devices: 279 us -> none  [on_device(): lax.psum((first_part, second_part), ('group', 'sample'))]
    all_gather x3 -> x0, blocking collectives: 162 us -> none  [the longest x1 62.9 us: on_device(): lax.all_gather(prompt_keys, 'sample', axis=0, tiled=True)]
    unnamed x6 -> x0, waiting for transfers between devices: 157 us -> none
    all_to_all x0 -> x14, waiting for transfers between devices: none -> 135 us  [swap(): return lax.all_to_all(array, axis, 0, 0, tiled=True)]
    psum x1 -> x0, blocking collectives: 101 us -> none  [on_device(): lax.psum((first_part, second_part), ('group', 'sample'))]
    all_gather x1 -> x0, waiting for transfers between devices: 94.3 us -> none  [on_device(): lax.all_gather(frozen_value_weight, 'sample', axis=0, tiled=True)]
    all_to_all x0 -> x14, starting transfers between devices: none -> 64 us  [swap(): return lax.all_to_all(array, axis, 0, 0, tiled=True)]
    all_to_all x0 -> x6, blocking collectives: none -> 63.6 us  [swap(): return lax.all_to_all(array, axis, 0, 0, tiled=True)]
  transfers between devices with their start and end apart: 4 -> 14, of which waited for: 4 -> 14; matrix products, arithmetic and copies ran while one was open for 4% -> 8% of each run, Pallas kernels for 0% -> 2%
where the time goes in v1:
time: 323 us; the launch traced here: 320 us
  waiting for transfers between devices  135 us (42%)
  starting transfers between devices  64 us (20%)
  blocking collectives  63.6 us (20%)
  local copies, waits for them, and re-layouts  29.6 us (9%)
  Pallas kernels  11.6 us (4%)
  matrix products  7.38 us (2%)
  other arithmetic  7.35 us (2%)
    all_to_all x14, waiting for transfers between devices, swap(): return lax.all_to_all(array, axis, 0, 0, tiled=True)  135 us
    all_to_all x14, starting transfers between devices, swap(): return lax.all_to_all(array, axis, 0, 0, tiled=True)  64 us
    all_to_all x6, blocking collectives, swap(): return lax.all_to_all(array, axis, 0, 0, tiled=True)  63.6 us
    broadcast_in_dim x12, local copies, waits for them, and re-layouts, gather(): return swap(jnp.broadcast_to(array[None], (n,) + array.shape), axis)  11.1 us
    unnamed x28, local copies, waits for them, and re-layouts  6.85 us
    pallas_call x1, Pallas kernels, attend_backward(): pl.pallas_call(backward_kernel, grid=(KV_HEADS,), in_specs=[heads_of(TOKE...  6.47 us
  transfers between devices with their start and end apart: 14, of which 14 were waited for; matrix products, arithmetic and copies ran while one was open for 8% of the time, Pallas kernels for 2%

profile of v1, /device:TPU:1, one launch (start us, length us, event | category | flops | bytes accessed | tf_op | source)
XLA Modules:
  0.0 319.8 jit_solution(3117268583229450967)
XLA Ops:
  2.2 27.9 %all_to_all.100 = bf16[4,80,128]{2,1,0:T(8,128)(2,1)S(1)} all-to-all(bf16[4,80,128]{2,1,0:T(8,128)(2,1)S(1)} %broadcast_in_dim.44), channel_id=1, replica_groups=mesh['x'=4,'zl'=4,'y'=4,'zh'=4,'c'=2] {'zh'}, dimensions={0} | all-to-all | bytes 163840 | tf_op jit(solution)/shard_map/all_to_all | solution.py:29
  30.9 4.3 %all-to-all-start.1 = ((bf16[4,4,80,128]{3,2,1,0:T(8,128)(2,1)}), bf16[4,4,80,128]{3,2,1,0:T(8,128)(2,1)S(1)}, u32[]{:S(2)}, u32[]{:S(2)}) async-start(bf16[4,4,80,128]{3,2,1,0:T(8,128)(2,1)} %broadcast_in_dim.45), calls=%async_computation.1 | async-start | bytes 655360 | tf_op jit(solution)/shard_map/all_to_all | solution.py:29
  41.2 7.6 %all_to_all.101.key_ref = bf16[2,4,4,80,128]{4,3,2,1,0:T(8,128)(2,1)S(1)} all-to-all(bf16[2,4,4,80,128]{4,3,2,1,0:T(8,128)(2,1)S(1)} %broadcast_in_dim.46), channel_id=1, replica_groups=mesh['x'=4,'zl'=4,'y'=4,'zh'=4,'c'=2] {'c'}, dimensions={0} | all-to-all | bytes 1310720 | tf_op jit(solution)/shard_map/all_to_all | solution.py:29
  55.4 5.1 %attend_forward.1 = (bf16[2,4,4,80,128]{4,3,2,1,0:T(8,128)(2,1)S(1)}, bf16[128,512]{1,0:T(8,128)(2,1)S(1)}, bf16[16,128]{1,0:T(8,128)(2,1)S(1)}) custom-call(bf16[128,4096]{1,0:T(8,128)(2,1)S(1)} %copy-done.3, bf16[128,4096]{1,0:T(8,128)(2,1)S(1)} %copy-done.5, bf16[2,4,4,80,128]{4,3,2,1,0:T(8,128)(2,1)S(1)} %all_to_all.101.key_ref, ...), custom_call_target="tpu_custom_call" | custom-call | flops 2000000000 | bytes 5242880 | tf_op jit(solution)/shard_map/attend_forward/pallas_call | solution.py:178
  60.5 5.0 %all-to-all-done.6 = bf16[4,128,128]{2,1,0:T(8,128)(2,1)S(1)} async-done(((bf16[4,128,128]{2,1,0:T(8,128)(2,1)}), bf16[4,128,128]{2,1,0:T(8,128)(2,1)S(1)}, u32[]{:S(2)}, u32[]{:S(2)}) %all-to-all-start.6) | async-done | bytes 131104 | tf_op jit(solution)/shard_map/all_to_all | solution.py:29
  65.5 7.0 %all_to_all.102 = bf16[2,4,4,80,128]{4,3,2,1,0:T(8,128)(2,1)} all-to-all(bf16[2,4,4,80,128]{4,3,2,1,0:T(8,128)(2,1)S(1)} %get-tuple-element.12), channel_id=1, replica_groups=mesh['x'=4,'zl'=4,'y'=4,'zh'=4,'c'=2] {'c'}, dimensions={0} | all-to-all | bytes 1310720 | tf_op jit(solution)/shard_map/all_to_all | solution.py:29
  72.6 6.1 %all-to-all-start.17 = ((bf16[32,16,128]{2,1,0:T(8,128)(2,1)}), bf16[32,16,128]{2,1,0:T(8,128)(2,1)S(1)}, u32[]{:S(2)}, u32[]{:S(2)}) async-start(bf16[32,16,128]{2,1,0:T(8,128)(2,1)} %copy.79), calls=%async_computation.17 | async-start | bytes 262144 | tf_op jit(solution)/shard_map/all_to_all | solution.py:29
  80.6 15.1 %all-to-all-done.17 = bf16[32,16,128]{2,1,0:T(8,128)(2,1)S(1)} async-done(((bf16[32,16,128]{2,1,0:T(8,128)(2,1)}), bf16[32,16,128]{2,1,0:T(8,128)(2,1)S(1)}, u32[]{:S(2)}, u32[]{:S(2)}) %all-to-all-start.17) | async-done | bytes 131104 | tf_op jit(solution)/shard_map/all_to_all | solution.py:29
  99.3 7.0 %all-to-all-done.4 = bf16[4,4,80,128]{3,2,1,0:T(8,128)(2,1)S(1)} async-done(((bf16[4,4,80,128]{3,2,1,0:T(8,128)(2,1)}), bf16[4,4,80,128]{3,2,1,0:T(8,128)(2,1)S(1)}, u32[]{:S(2)}, u32[]{:S(2)}) %all-to-all-start.4) | async-done | bytes 327712 | tf_op jit(solution)/shard_map/all_to_all | solution.py:29
  107.1 4.0 %all-to-all-start.7 = ((bf16[4,4,128,128]{3,2,1,0:T(8,128)(2,1)}), bf16[4,4,128,128]{3,2,1,0:T(8,128)(2,1)S(1)}, u32[]{:S(2)}, u32[]{:S(2)}) async-start(bf16[4,4,128,128]{3,2,1,0:T(8,128)(2,1)} %broadcast_in_dim.52), calls=%async_computation.7 | async-start | bytes 1048576 | tf_op jit(solution)/shard_map/all_to_all | solution.py:29
  112.9 6.0 %all-to-all-done.7 = bf16[4,4,128,128]{3,2,1,0:T(8,128)(2,1)S(1)} async-done(((bf16[4,4,128,128]{3,2,1,0:T(8,128)(2,1)}), bf16[4,4,128,128]{3,2,1,0:T(8,128)(2,1)S(1)}, u32[]{:S(2)}, u32[]{:S(2)}) %all-to-all-start.7) | async-done | bytes 524320 | tf_op jit(solution)/shard_map/all_to_all | solution.py:29
  124.2 9.8 %all-to-all-done.5 = bf16[4,80,128]{2,1,0:T(8,128)(2,1)S(1)} async-done(((bf16[4,80,128]{2,1,0:T(8,128)(2,1)}), bf16[4,80,128]{2,1,0:T(8,128)(2,1)S(1)}, u32[]{:S(2)}, u32[]{:S(2)}) %all-to-all-start.5) | async-done | bytes 81952 | tf_op jit(solution)/shard_map/all_to_all | solution.py:29
  136.1 4.5 %all-to-all-start.8 = ((bf16[4,4,4,128,128]{4,1,3,2,0:T(4,128)(2,1)}), bf16[4,4,4,128,128]{4,1,3,2,0:T(4,128)(2,1)}, u32[]{:S(2)}, u32[]{:S(2)}) async-start(bf16[4,4,4,128,128]{4,1,3,2,0:T(4,128)(2,1)} %broadcast_in_dim.53), calls=%async_computation.8 | async-start | bytes 4194304 | tf_op jit(solution)/shard_map/all_to_all | solution.py:29
  144.1 18.9 %all-to-all-done.8 = bf16[4,4,4,128,128]{4,1,3,2,0:T(4,128)(2,1)} async-done(((bf16[4,4,4,128,128]{4,1,3,2,0:T(4,128)(2,1)}), bf16[4,4,4,128,128]{4,1,3,2,0:T(4,128)(2,1)}, u32[]{:S(2)}, u32[]{:S(2)}) %all-to-all-start.8) | async-done | bytes 2097184 | tf_op jit(solution)/shard_map/all_to_all | solution.py:29
  166.5 12.7 %all_to_all.103 = bf16[2,4,4,4,128,128]{5,2,4,3,1,0:T(4,128)(2,1)} all-to-all(bf16[2,4,4,4,128,128]{5,2,4,3,1,0:T(4,128)(2,1)S(1)} %broadcast_in_dim.54), channel_id=1, replica_groups=mesh['x'=4,'zl'=4,'y'=4,'zh'=4,'c'=2] {'c'}, dimensions={0} | all-to-all | bytes 8388608 | tf_op jit(solution)/shard_map/all_to_all | solution.py:29
  179.2 3.9 %all-to-all-start.16 = ((f32[32,16,128]{2,1,0:T(8,128)}), f32[32,16,128]{2,1,0:T(8,128)S(1)}, u32[]{:S(2)}, u32[]{:S(2)}) async-start(f32[32,16,128]{2,1,0:T(8,128)} %maximum_maximum_fusion), calls=%async_computation.16 | async-start | bytes 524288 | tf_op jit(solution)/shard_map/all_to_all | solution.py:29
  183.1 4.0 %copy.73 = bf16[4,4,2,128,4,128]{5,4,3,2,1,0:T(4,128)(2,1)S(1)} copy(bf16[4,4,2,128,4,128]{5,4,3,1,0,2:T(4,128)(2,1)} %bitcast.75) | data formatting | bytes 8388608 | tf_op jit(solution)/shard_map/transpose | solution.py:303
  189.3 12.5 %all-to-all-done.16 = f32[32,16,128]{2,1,0:T(8,128)S(1)} async-done(((f32[32,16,128]{2,1,0:T(8,128)}), f32[32,16,128]{2,1,0:T(8,128)S(1)}, u32[]{:S(2)}, u32[]{:S(2)}) %all-to-all-start.16) | async-done | bytes 262176 | tf_op jit(solution)/shard_map/all_to_all | solution.py:29
  202.4 4.2 %all-to-all-start.10 = ((bf16[4,64,128]{2,1,0:T(8,128)(2,1)}), bf16[4,64,128]{2,1,0:T(8,128)(2,1)S(1)}, u32[]{:S(2)}, u32[]{:S(2)}) async-start(bf16[4,64,128]{2,1,0:T(8,128)(2,1)} %broadcast_in_dim.56), calls=%async_computation.10 | async-start | bytes 131072 | tf_op jit(solution)/shard_map/all_to_all | solution.py:29
  206.7 12.6 %all-to-all-done.10 = bf16[4,64,128]{2,1,0:T(8,128)(2,1)S(1)} async-done(((bf16[4,64,128]{2,1,0:T(8,128)(2,1)}), bf16[4,64,128]{2,1,0:T(8,128)(2,1)S(1)}, u32[]{:S(2)}, u32[]{:S(2)}) %all-to-all-start.10) | async-done | bytes 65568 | tf_op jit(solution)/shard_map/all_to_all | solution.py:29
  220.1 4.6 %all-to-all-start.11 = ((bf16[4,4,64,128]{3,2,1,0:T(8,128)(2,1)}), bf16[4,4,64,128]{3,2,1,0:T(8,128)(2,1)S(1)}, u32[]{:S(2)}, u32[]{:S(2)}) async-start(bf16[4,4,64,128]{3,2,1,0:T(8,128)(2,1)} %broadcast_in_dim.57), calls=%async_computation.11 | async-start | bytes 524288 | tf_op jit(solution)/shard_map/all_to_all | solution.py:29
  224.9 6.3 %all-to-all-done.11 = bf16[4,4,64,128]{3,2,1,0:T(8,128)(2,1)S(1)} async-done(((bf16[4,4,64,128]{3,2,1,0:T(8,128)(2,1)}), bf16[4,4,64,128]{3,2,1,0:T(8,128)(2,1)S(1)}, u32[]{:S(2)}, u32[]{:S(2)}) %all-to-all-start.11) | async-done | bytes 262176 | tf_op jit(solution)/shard_map/all_to_all | solution.py:29
  231.4 4.1 %all_to_all.104.value_ref = bf16[2,4,4,64,128]{4,3,2,1,0:T(8,128)(2,1)S(1)} all-to-all(bf16[2,4,4,64,128]{4,3,2,1,0:T(8,128)(2,1)S(1)} %broadcast_in_dim.58), channel_id=1, replica_groups=mesh['x'=4,'zl'=4,'y'=4,'zh'=4,'c'=2] {'c'}, dimensions={0} | all-to-all | bytes 1048576 | tf_op jit(solution)/shard_map/all_to_all | solution.py:29
  236.8 6.5 %attend_backward.1 = (bf16[2,4,4,64,128]{4,3,2,1,0:T(8,128)(2,1)S(1)}, bf16[128,512]{1,0:T(8,128)(2,1)}) custom-call(bf16[128,4096]{1,0:T(8,128)(2,1)S(1)} %copy-done.4, bf16[128,4096]{1,0:T(8,128)(2,1)S(1)} %copy-done.6, bf16[2,4,4,80,128]{4,3,2,1,0:T(8,128)(2,1)S(1)} %all_to_all.101.key_ref, bf16[2,4,4,64,128]{4,3,2,1,0:T(8,128)(2,1)S(1)} %all_to_all.104.value_ref, ...), custom_call_target="tpu_custom_call" | custom-call | flops 3000000000 | bytes 5242880 | tf_op jit(solution)/shard_map/attend_backward/pallas_call | solution.py:218
  243.2 4.2 %all_to_all.105 = bf16[2,4,4,64,128]{4,3,2,1,0:T(8,128)(2,1)S(1)} all-to-all(bf16[2,4,4,64,128]{4,3,2,1,0:T(8,128)(2,1)S(1)} %get-tuple-element.15), channel_id=1, replica_groups=mesh['x'=4,'zl'=4,'y'=4,'zh'=4,'c'=2] {'c'}, dimensions={0} | all-to-all | bytes 1048576 | tf_op jit(solution)/shard_map/all_to_all | solution.py:29
  251.7 6.1 %all-to-all-done.14 = bf16[4,4,64,128]{3,2,1,0:T(8,128)(2,1)S(1)} async-done(((bf16[4,4,64,128]{3,2,1,0:T(8,128)(2,1)}), bf16[4,4,64,128]{3,2,1,0:T(8,128)(2,1)S(1)}, u32[]{:S(2)}, u32[]{:S(2)}) %all-to-all-start.14) | async-done | bytes 262176 | tf_op jit(solution)/shard_map/all_to_all | solution.py:29
  258.6 7.6 %all-to-all-start.18 = ((f32[16,16,256]{2,1,0:T(8,128)}), f32[16,16,256]{2,1,0:T(8,128)S(1)}, u32[]{:S(2)}, u32[]{:S(2)}) async-start(f32[16,16,256]{2,1,0:T(8,128)} %broadcast_in_dim.62), calls=%async_computation.18 | async-start | bytes 524288 | tf_op jit(solution)/shard_map/all_to_all | solution.py:29
  266.9 7.9 %all-to-all-done.18 = f32[16,16,256]{2,1,0:T(8,128)S(1)} async-done(((f32[16,16,256]{2,1,0:T(8,128)}), f32[16,16,256]{2,1,0:T(8,128)S(1)}, u32[]{:S(2)}, u32[]{:S(2)}) %all-to-all-start.18) | async-done | bytes 262176 | tf_op jit(solution)/shard_map/all_to_all | solution.py:29
  278.7 11.0 %all-to-all-done.15 = bf16[4,64,128]{2,1,0:T(8,128)(2,1)S(1)} async-done(((bf16[4,64,128]{2,1,0:T(8,128)(2,1)}), bf16[4,64,128]{2,1,0:T(8,128)(2,1)S(1)}, u32[]{:S(2)}, u32[]{:S(2)}) %all-to-all-start.15) | async-done | bytes 65568 | tf_op jit(solution)/shard_map/all_to_all | solution.py:29
  290.4 8.1 %all-to-all-start.19 = ((f32[32,16,128]{2,1,0:T(8,128)}), f32[32,16,128]{2,1,0:T(8,128)S(1)}, u32[]{:S(2)}, u32[]{:S(2)}) async-start(f32[32,16,128]{2,1,0:T(8,128)} %broadcast_in_dim.122), calls=%async_computation.19 | async-start | bytes 524288 | tf_op jit(solution)/shard_map/all_to_all | solution.py:29
  299.0 3.7 %fusion = bf16[144,4096]{1,0:T(8,128)(2,1)S(1)} fusion(f32[144,4096]{1,0:T(8,128)S(1)} %convolution_multiply_fusion, bf16[144,512]{1,0:T(8,128)(2,1)S(1)} %bitcast_dynamic-update-slice_fusion, bf16[512,8,4,128]{3,2,1,0:T(4,128)(2,1)} %bitcast.77), kind=kOutput, calls=%fused_computation.2 | convolution fusion | flops 605159424 | bytes 7880704 | tf_op jit(solution)/shard_map/dot_general | solution.py:38
  305.1 13.8 %all-to-all-done.19 = f32[32,16,128]{2,1,0:T(8,128)S(1)} async-done(((f32[32,16,128]{2,1,0:T(8,128)}), f32[32,16,128]{2,1,0:T(8,128)S(1)}, u32[]{:S(2)}, u32[]{:S(2)}) %all-to-all-start.19) | async-done | bytes 262176 | tf_op jit(solution)/shard_map/all_to_all | solution.py:29
  (100 shorter events, 56.6 us)
Async XLA Ops:
  0.6 37.1 %copy-start = (bf16[128,512]{1,0:T(8,128)(2,1)S(1)}, bf16[128,512]{1,0:T(8,128)(2,1)}, u32[]{:S(2)}) copy-start(bf16[128,512]{1,0:T(8,128)(2,1)} %param.19) | copy-start | bytes 393220
  0.6 37.1 %copy-start.10 = (s32[1,128]{1,0:T(1,128)S(1)}, s32[1,128]{1,0:T(1,128)}, u32[]{:S(2)}) copy-start(s32[1,128]{1,0:T(1,128)} %param.17) | copy-start | bytes 1540
  0.7 37.1 %copy-start.11 = (s32[1,8]{1,0:T(1,128)S(1)}, s32[1,8]{1,0:T(1,128)}, u32[]{:S(2)}) copy-start(s32[1,8]{1,0:T(1,128)} %param.18) | copy-start | bytes 100
  30.9 22.0 %copy-start.1 = (bf16[128,4096]{1,0:T(8,128)(2,1)S(1)}, bf16[128,4096]{1,0:T(8,128)(2,1)}, u32[]{:S(2)}) copy-start(bf16[128,4096]{1,0:T(8,128)(2,1)} %x_ref.1) | copy-start | bytes 3145732
  30.9 22.0 %copy-start.2 = (bf16[16,512]{1,0:T(8,128)(2,1)S(1)}, bf16[16,512]{1,0:T(8,128)(2,1)}, u32[]{:S(2)}) copy-start(bf16[16,512]{1,0:T(8,128)(2,1)} %up_ref.1) | copy-start | bytes 49156
  30.9 22.1 %copy-start.7 = (bf16[128,512]{1,0:T(8,128)(2,1)S(1)}, bf16[128,512]{1,0:T(8,128)(2,1)}, u32[]{:S(2)}) copy-start(bf16[128,512]{1,0:T(8,128)(2,1)} %own_key_ref.3) | copy-start | bytes 393220
  30.9 10.2 %all-to-all-start.1 = ((bf16[4,4,80,128]{3,2,1,0:T(8,128)(2,1)}), bf16[4,4,80,128]{3,2,1,0:T(8,128)(2,1)S(1)}, u32[]{:S(2)}, u32[]{:S(2)}) async-start(bf16[4,4,80,128]{3,2,1,0:T(8,128)(2,1)} %broadcast_in_dim.45), calls=%async_computation.1 | async-start | bytes 655360 | tf_op jit(solution)/shard_map/all_to_all | solution.py:29
  49.5 16.1 %all-to-all-start.6 = ((bf16[4,128,128]{2,1,0:T(8,128)(2,1)}), bf16[4,128,128]{2,1,0:T(8,128)(2,1)S(1)}, u32[]{:S(2)}, u32[]{:S(2)}) async-start(bf16[4,128,128]{2,1,0:T(8,128)(2,1)} %broadcast_in_dim.51), calls=%async_computation.6 | async-start | bytes 262144 | tf_op jit(solution)/shard_map/all_to_all | solution.py:29
  52.9 1.2 copy-start.3
  54.2 1.2 copy-start.5
  72.6 23.1 %all-to-all-start.17 = ((bf16[32,16,128]{2,1,0:T(8,128)(2,1)}), bf16[32,16,128]{2,1,0:T(8,128)(2,1)S(1)}, u32[]{:S(2)}, u32[]{:S(2)}) async-start(bf16[32,16,128]{2,1,0:T(8,128)(2,1)} %copy.79), calls=%async_computation.17 | async-start | bytes 262144 | tf_op jit(solution)/shard_map/all_to_all | solution.py:29
  95.7 10.5 %all-to-all-start.4 = ((bf16[4,4,80,128]{3,2,1,0:T(8,128)(2,1)}), bf16[4,4,80,128]{3,2,1,0:T(8,128)(2,1)S(1)}, u32[]{:S(2)}, u32[]{:S(2)}) async-start(bf16[4,4,80,128]{3,2,1,0:T(8,128)(2,1)} %fusion.11), calls=%async_computation.4 | async-start | bytes 655360 | tf_op jit(solution)/shard_map/all_to_all | solution.py:29
  107.1 11.7 %all-to-all-start.7 = ((bf16[4,4,128,128]{3,2,1,0:T(8,128)(2,1)}), bf16[4,4,128,128]{3,2,1,0:T(8,128)(2,1)S(1)}, u32[]{:S(2)}, u32[]{:S(2)}) async-start(bf16[4,4,128,128]{3,2,1,0:T(8,128)(2,1)} %broadcast_in_dim.52), calls=%async_computation.7 | async-start | bytes 1048576 | tf_op jit(solution)/shard_map/all_to_all | solution.py:29
  118.9 15.1 %all-to-all-start.5 = ((bf16[4,80,128]{2,1,0:T(8,128)(2,1)}), bf16[4,80,128]{2,1,0:T(8,128)(2,1)S(1)}, u32[]{:S(2)}, u32[]{:S(2)}) async-start(bf16[4,80,128]{2,1,0:T(8,128)(2,1)} %reduce_sum.73), calls=%async_computation.5 | async-start | bytes 163840 | tf_op jit(solution)/shard_map/all_to_all | solution.py:29
  136.1 26.9 %all-to-all-start.8 = ((bf16[4,4,4,128,128]{4,1,3,2,0:T(4,128)(2,1)}), bf16[4,4,4,128,128]{4,1,3,2,0:T(4,128)(2,1)}, u32[]{:S(2)}, u32[]{:S(2)}) async-start(bf16[4,4,4,128,128]{4,1,3,2,0:T(4,128)(2,1)} %broadcast_in_dim.53), calls=%async_computation.8 | async-start | bytes 4194304 | tf_op jit(solution)/shard_map/all_to_all | solution.py:29
  179.2 22.6 %all-to-all-start.16 = ((f32[32,16,128]{2,1,0:T(8,128)}), f32[32,16,128]{2,1,0:T(8,128)S(1)}, u32[]{:S(2)}, u32[]{:S(2)}) async-start(f32[32,16,128]{2,1,0:T(8,128)} %maximum_maximum_fusion), calls=%async_computation.16 | async-start | bytes 524288 | tf_op jit(solution)/shard_map/all_to_all | solution.py:29
  183.1 4.0 %copy-start.9 = (bf16[144,4096]{1,0:T(8,128)(2,1)S(1)}, bf16[144,4096]{1,0:T(8,128)(2,1)}, u32[]{:S(2)}) copy-start(bf16[144,4096]{1,0:T(8,128)(2,1)} %constant_dynamic-update-slice_fusion.1) | copy-start | bytes 3538948
  187.1 1.9 copy-start.8
  189.0 46.5 %copy-start.4 = (bf16[128,4096]{1,0:T(8,128)(2,1)S(1)}, bf16[128,4096]{1,0:T(8,128)(2,1)}, u32[]{:S(2)}) copy-start(bf16[128,4096]{1,0:T(8,128)(2,1)} %q_ref.3) | copy-start | bytes 3145732
  202.4 16.9 %all-to-all-start.10 = ((bf16[4,64,128]{2,1,0:T(8,128)(2,1)}), bf16[4,64,128]{2,1,0:T(8,128)(2,1)S(1)}, u32[]{:S(2)}, u32[]{:S(2)}) async-start(bf16[4,64,128]{2,1,0:T(8,128)(2,1)} %broadcast_in_dim.56), calls=%async_computation.10 | async-start | bytes 131072 | tf_op jit(solution)/shard_map/all_to_all | solution.py:29
  220.1 11.2 %all-to-all-start.11 = ((bf16[4,4,64,128]{3,2,1,0:T(8,128)(2,1)}), bf16[4,4,64,128]{3,2,1,0:T(8,128)(2,1)S(1)}, u32[]{:S(2)}, u32[]{:S(2)}) async-start(bf16[4,4,64,128]{3,2,1,0:T(8,128)(2,1)} %broadcast_in_dim.57), calls=%async_computation.11 | async-start | bytes 524288 | tf_op jit(solution)/shard_map/all_to_all | solution.py:29
  235.5 1.2 copy-start.6
  248.3 9.6 %all-to-all-start.14 = ((bf16[4,4,64,128]{3,2,1,0:T(8,128)(2,1)}), bf16[4,4,64,128]{3,2,1,0:T(8,128)(2,1)S(1)}, u32[]{:S(2)}, u32[]{:S(2)}) async-start(bf16[4,4,64,128]{3,2,1,0:T(8,128)(2,1)} %fusion.12), calls=%async_computation.14 | async-start | bytes 524288 | tf_op jit(solution)/shard_map/all_to_all | solution.py:29
  258.6 16.1 %all-to-all-start.18 = ((f32[16,16,256]{2,1,0:T(8,128)}), f32[16,16,256]{2,1,0:T(8,128)S(1)}, u32[]{:S(2)}, u32[]{:S(2)}) async-start(f32[16,16,256]{2,1,0:T(8,128)} %broadcast_in_dim.62), calls=%async_computation.18 | async-start | bytes 524288 | tf_op jit(solution)/shard_map/all_to_all | solution.py:29
  274.7 15.0 %all-to-all-start.15 = ((bf16[4,64,128]{2,1,0:T(8,128)(2,1)}), bf16[4,64,128]{2,1,0:T(8,128)(2,1)S(1)}, u32[]{:S(2)}, u32[]{:S(2)}) async-start(bf16[4,64,128]{2,1,0:T(8,128)(2,1)} %reduce_sum.75), calls=%async_computation.15 | async-start | bytes 131072 | tf_op jit(solution)/shard_map/all_to_all | solution.py:29
  290.4 28.5 %all-to-all-start.19 = ((f32[32,16,128]{2,1,0:T(8,128)}), f32[32,16,128]{2,1,0:T(8,128)S(1)}, u32[]{:S(2)}, u32[]{:S(2)}) async-start(f32[32,16,128]{2,1,0:T(8,128)} %broadcast_in_dim.122), calls=%async_computation.19 | async-start | bytes 524288 | tf_op jit(solution)/shard_map/all_to_all | solution.py:29

commit v2 on v1

--- a/solution.py
+++ b/solution.py
@@ -68,6 +68,19 @@
     )
 
 
+def value_block(ref, k):
+    def part(c, p, zh):
+        return ref[c, pl.ds(pl.multiple_of((p * 4 + zh) * 64 + k * 16, 16), 16), :]
+
+    return jnp.concatenate(
+        [
+            jnp.concatenate([part(c, p, zh) for zh in range(4) for c in range(2)], axis=0)
+            for p in range(PROMPTS)
+        ],
+        axis=1,
+    )
+
+
 def spread(ref, row, block):
     for p in range(PROMPTS):
         for zh in range(4):
@@ -87,9 +100,14 @@
     return seen / total, own / total
 
 
+BLOCKS = [
+    (((y * 4 + zh) * 2 + c) * 128, y, zh, c) for y in range(4) for zh in range(4) for c in range(2)
+]
+
+
 def forward_kernel(
-    q_ref, cot_ref, key_ref, own_key_ref, chosen_ref, bias_ref, x_ref, up_ref,
-    send_ref, low_ref, back_ref,
+    q_ref, cot_ref, key_ref, down_ref, own_key_ref, chosen_ref, bias_ref, x_ref, prompt_ref, up_ref,
+    send_ref, low_ref, back_ref, first_ref, down_out_ref,
     probs, own_probs, cots, back,
 ):
     k = pl.program_id(0)
@@ -113,19 +131,103 @@
     @pl.when(k == 0)
     def _():
         back[...] = jnp.zeros_like(back)
+        for at, y, zh, c in BLOCKS:
+            down_out_ref[:, at : at + 128] = down_ref[c, y, zh]
+        down = down_out_ref[...]
+        first_ref[:TOKENS, :] = nt(x_ref[...], down).astype(BF16)
+        first_ref[TOKENS:, :] = nt(prompt_ref[...], down).astype(BF16)
 
     back[...] += nt(up_ref[...], low)
 
     @pl.when(k == KV_HEADS - 1)
     def _():
-        back_low = back[...].astype(BF16)
-        back_ref[...] = back_low
-        first = nn(back_low, x_ref[...])
+        back_ref[...] = back[...].astype(BF16)
+
+
+def adapter_kernel(
+    low_ref, back_ref, got_ref, first_ref, up_ref, x_ref, prompt_ref,
+    prompt_low_ref, prompt_back_ref, send_ref,
+):
+    got = got_ref[...].astype(F32)
+    total = ((got[0] + got[1]) + (got[2] + got[3])).astype(BF16)
+    up = up_ref[...]
+    first = first_ref[...]
+    prompt_back = jnp.zeros((RANK, 16), F32)
+    for k in range(KV_HEADS):
+        at = slice(k * HEAD_DIM, (k + 1) * HEAD_DIM)
+        low = total[k * 16 : (k + 1) * 16]
+        prompt_low_ref[:, at] = low
+        prompt_back = prompt_back + nt(up[:, at], low)
+        second = (tn(first[:TOKENS], low_ref[:, at]) + tn(first[TOKENS:], low)).astype(BF16)
+        for zh in range(4):
+            send_ref[zh, 128 + k * 16 : 128 + (k + 1) * 16, :] = second
+    prompt_back = prompt_back.astype(BF16)
+    prompt_back_ref[...] = prompt_back
+    grad = (nn(back_ref[...], x_ref[...]) + nn(prompt_back, prompt_ref[...])).astype(BF16)
+    for at, y, zh, c in BLOCKS:
+        row = (y * 2 + c) * 16
+        send_ref[zh, row : row + 16, :] = grad[:, at : at + 128]
+
+
+def project_kernel(
+    x_ref, prompt_ref, weight_ref, first_ref, up_ref, adapter_ref,
+    values_ref, send_ref, weight_out_ref,
+    rows,
+):
+    k = pl.program_id(0)
+
+    @pl.when(k == 0)
+    def _():
+        rows[:TOKENS, :] = x_ref[...]
+        rows[TOKENS:, :] = prompt_ref[...]
+        send_ref[:, KV_HEADS * 16 :, :] = adapter_ref[...]
+
+    for at, y, zh, c in BLOCKS:
+        weight_out_ref[at : at + 128, :] = weight_ref[0, y, c, zh]
+    values = nn(rows[...], weight_out_ref[...]) + ADAPTER_SCALE * nn(first_ref[...], up_ref[...])
+    values = values.astype(BF16)
+    values_ref[...] = values[:TOKENS]
+    for zh in range(4):
+        send_ref[zh, pl.ds(pl.multiple_of(k * 16, 16), 16), :] = values[TOKENS:]
+
+
+def total_of(parts):
+    parts = parts.astype(F32)
+    total = parts[0]
+    for i in range(1, parts.shape[0]):
+        total = total + parts[i]
+    return total
+
+
+def after_zh_kernel(got_ref, send_ref):
+    second = total_of(got_ref[:, 192:, :]).astype(BF16)
+    for y in range(4):
+        for zh in range(4):
+            send_ref[y, zh * 64 : (zh + 1) * 64, :] = got_ref[zh, :64, :]
+        first = total_of(got_ref[:, 64 + y * 32 : 64 + (y + 1) * 32, :])
+        send_ref[y, 256:288, :] = first.astype(BF16)
+        send_ref[y, 288:, :] = second
+
+
+def after_y_kernel(got_ref, send_ref):
+    second = total_of(got_ref[:, 288:, :]).astype(BF16)
+    for c in range(2):
         for y in range(4):
-            for zh in range(4):
-                for c in range(2):
-                    at = ((y * 4 + zh) * 2 + c) * 128
-                    send_ref[c, y, zh, KV_HEADS * 16 :, :] = first[:, at : at + 128].astype(BF16)
+            send_ref[c, y * 256 : (y + 1) * 256, :] = got_ref[y, :256, :]
+        first = total_of(got_ref[:, 256 + c * 16 : 256 + (c + 1) * 16, :])
+        send_ref[c, 1024:1040, :] = first.astype(BF16)
+        send_ref[c, 1040:, :] = second
+
+
+def in_vmem(kernel, shape, name):
+    return pl.pallas_call(
+        kernel,
+        in_specs=[pl.BlockSpec(memory_space=pltpu.VMEM)],
+        out_specs=pl.BlockSpec(memory_space=pltpu.VMEM),
+        out_shape=jax.ShapeDtypeStruct(shape, BF16),
+        compiler_params=pltpu.CompilerParams(vmem_limit_bytes=16 << 20),
+        name=name,
+    )
 
 
 def backward_kernel(
@@ -134,7 +236,7 @@
     grads, own_grads, queries,
 ):
     k = pl.program_id(0)
-    key_cat, value_cat = prompt_block(key_ref), prompt_block(value_ref)
+    key_cat, value_cat = prompt_block(key_ref), value_block(value_ref, k)
     own_key, own_value = own_key_ref[...], own_value_ref[...]
     chosen = chosen_ref[...]
     bias = bias_ref[...]
@@ -174,7 +276,11 @@
 ROWS = GROUP_SIZE * TOKENS
 
 
-def attend_forward(queries, cotangent, keys, own_keys, chosen, bias, rows, up):
+DOWN_SPEC = pl.BlockSpec((2, 4, 4, 16, HEAD_DIM), lambda k: (0, 0, 0, KV_HEADS, 0))
+PARAMS = pltpu.CompilerParams(vmem_limit_bytes=40 << 20, dimension_semantics=("arbitrary",))
+
+
+def attend_forward(queries, cotangent, keys, own_keys, chosen, bias, rows, prompt_rows, up):
     return pl.pallas_call(
         forward_kernel,
         grid=(KV_HEADS,),
@@ -182,21 +288,27 @@
             heads_of(TOKENS, WIDE),
             heads_of(TOKENS, WIDE),
             PROMPT_SPEC,
+            DOWN_SPEC,
             heads_of(TOKENS, HEAD_DIM),
             whole((PAIR, HEAD_DIM)),
             whole((TOKENS, PAIR)),
             whole((TOKENS, D)),
+            whole((16, D)),
             heads_of(RANK, HEAD_DIM),
         ],
         out_specs=[
-            whole((2, 4, 4, KV_HEADS * 16 + RANK, HEAD_DIM)),
+            whole((2, 4, 4, KV_HEADS * 16, HEAD_DIM)),
             heads_of(TOKENS, HEAD_DIM),
             whole((RANK, TOKENS)),
+            whole((TOKENS + 16, RANK)),
+            whole((RANK, D)),
         ],
         out_shape=[
-            jax.ShapeDtypeStruct((2, 4, 4, KV_HEADS * 16 + RANK, HEAD_DIM), BF16),
+            jax.ShapeDtypeStruct((2, 4, 4, KV_HEADS * 16, HEAD_DIM), BF16),
             jax.ShapeDtypeStruct((TOKENS, KV_HEADS * HEAD_DIM), BF16),
             jax.ShapeDtypeStruct((RANK, TOKENS), BF16),
+            jax.ShapeDtypeStruct((TOKENS + 16, RANK), BF16),
+            jax.ShapeDtypeStruct((RANK, D), BF16),
         ],
         scratch_shapes=[
             pltpu.VMEM((TOKENS, ROWS), BF16),
@@ -204,14 +316,59 @@
             pltpu.VMEM((ROWS, (PROMPTS + 1) * HEAD_DIM), BF16),
             pltpu.VMEM((RANK, TOKENS), F32),
         ],
-        compiler_params=pltpu.CompilerParams(
-            vmem_limit_bytes=40 << 20, dimension_semantics=("arbitrary",)
-        ),
+        compiler_params=PARAMS,
         cost_estimate=pl.CostEstimate(
             flops=2_000_000_000, bytes_accessed=5 << 20, transcendentals=1 << 20
         ),
         name="attend_forward",
-    )(queries, cotangent, keys, own_keys, chosen, bias, rows, up)
+    )(queries, cotangent, keys, keys, own_keys, chosen, bias, rows, prompt_rows, up)
+
+
+def adapter_terms(low, back, got, first, up, rows, prompt_rows):
+    return pl.pallas_call(
+        adapter_kernel,
+        in_specs=[pl.BlockSpec(memory_space=pltpu.VMEM)] * 7,
+        out_specs=[pl.BlockSpec(memory_space=pltpu.VMEM)] * 3,
+        out_shape=[
+            jax.ShapeDtypeStruct((16, KV_HEADS * HEAD_DIM), BF16),
+            jax.ShapeDtypeStruct((RANK, 16), BF16),
+            jax.ShapeDtypeStruct((4, 128 + KV_HEADS * 16, HEAD_DIM), BF16),
+        ],
+        compiler_params=pltpu.CompilerParams(vmem_limit_bytes=16 << 20),
+        name="adapter_terms",
+    )(low, back, got, first, up, rows, prompt_rows)
+
+
+def project(rows, prompt_rows, weight, first, up, adapter):
+    width = KV_HEADS * HEAD_DIM
+    return pl.pallas_call(
+        project_kernel,
+        grid=(KV_HEADS,),
+        in_specs=[
+            whole((TOKENS, D)),
+            whole((16, D)),
+            pl.BlockSpec((1, 4, 2, 4, 128, HEAD_DIM), lambda k: (k, 0, 0, 0, 0, 0)),
+            whole((TOKENS + 16, RANK)),
+            heads_of(RANK, HEAD_DIM),
+            whole((4, 192, HEAD_DIM)),
+        ],
+        out_specs=[
+            heads_of(TOKENS, HEAD_DIM),
+            whole((4, 256, HEAD_DIM)),
+            heads_of(D, HEAD_DIM),
+        ],
+        out_shape=[
+            jax.ShapeDtypeStruct((TOKENS, width), BF16),
+            jax.ShapeDtypeStruct((4, 256, HEAD_DIM), BF16),
+            jax.ShapeDtypeStruct((D, width), BF16),
+        ],
+        scratch_shapes=[pltpu.VMEM((TOKENS + 16, D), BF16)],
+        compiler_params=PARAMS,
+        cost_estimate=pl.CostEstimate(
+            flops=600_000_000, bytes_accessed=10 << 20, transcendentals=0
+        ),
+        name="project",
+    )(rows, prompt_rows, weight, first, up, adapter)
 
 
 def attend_backward(queries, cotangent, keys, values, own_keys, own_values, chosen, bias):
@@ -222,7 +379,7 @@
             heads_of(TOKENS, WIDE),
             heads_of(TOKENS, WIDE),
             PROMPT_SPEC,
-            PROMPT_SPEC,
+            whole((2, 1104, HEAD_DIM)),
             heads_of(TOKENS, HEAD_DIM),
             heads_of(TOKENS, HEAD_DIM),
             whole((PAIR, HEAD_DIM)),
@@ -251,17 +408,14 @@
     )(queries, cotangent, keys, values, own_keys, own_values, chosen, bias)
 
 
-def reduce_parts(parts):
-    shape = parts.shape[3:]
-    got = swap(parts, "c").astype(F32)
-    part = (got[0] + got[1]).astype(BF16)
-    part = jnp.sum(swap(part, "y").astype(F32), axis=0).astype(BF16)
-    part = jnp.sum(swap(part, "zh").astype(F32), axis=0)
-    return part.reshape(shape)
-
-
-def gather_parts(part):
-    return gather(gather(gather(part, "zh"), "y"), "c")
+def sum_first(parts):
+    return jnp.sum(parts.astype(F32), axis=0)
+
+
+def reduce_to_zh(parts):
+    part = sum_first(swap(parts, "c")).astype(BF16)
+    part = sum_first(swap(part, "y")).astype(BF16)
+    return swap(part, "zh")
 
 
 def heads_first(rows):
@@ -270,6 +424,13 @@
 
 def heads_last(parts):
     return parts.reshape(KV_HEADS, 16, HEAD_DIM).transpose(1, 0, 2).reshape(16, KV_HEADS * HEAD_DIM)
+
+
+def sum_ring(part, axis):
+    total = part
+    for step in range(1, 4):
+        total = total + lax.ppermute(part, axis, [(i, (i + step) % 4) for i in range(4)])
+    return total
 
 
 def on_device(
@@ -293,61 +454,44 @@
     own_seen = (segments[:, None] == segments[None, :]) & (position[:, None] <= position[None, :])
     bias = jnp.tile(jnp.where(own_seen, 0.0, -1e30).astype(F32), (1, 2))
 
-    down_t = value_adapter_down.T
-    key_part = jnp.concatenate([heads_first(prompt_keys), down_t], axis=0)
-    key_all = gather_parts(key_part)
     own_columns = lax.dynamic_slice_in_dim(
         frozen_value_weight, lax.axis_index("x") * HEAD_DIM, HEAD_DIM, 1
     )
-    weight = gather(gather(gather(gather(own_columns, "zh"), "x"), "y"), "c")
-    weight = weight.transpose(1, 3, 0, 4, 2, 5).reshape(D, KV_HEADS * HEAD_DIM)
-    prompt_columns = swap(prompt_rows.reshape(16, 32, 128).transpose(1, 0, 2), SAMPLE)
-
-    send, low, back_t = attend_forward(
-        queries, cotangent, key_all, response_keys, chosen, bias, response_rows, value_adapter_up
-    )
-    got = reduce_parts(send)
-    prompt_low = heads_last(got[: KV_HEADS * 16].astype(BF16))
-    first_sum = got[KV_HEADS * 16 :]
-
-    down_full = key_all[:, :, :, KV_HEADS * 16 :].transpose(3, 1, 2, 0, 4).reshape(RANK, D)
-    local_rows = jnp.concatenate([response_rows, prompt_rows], axis=0)
-    first_proj = nt(local_rows, down_full).astype(BF16)
-    value_low = jnp.concatenate([low, prompt_low], axis=0)
-    prompt_back = nt(prompt_low, value_adapter_up).astype(BF16)
-    back_low = jnp.concatenate([back_t.T, prompt_back], axis=0)
-
-    second_part = tn(first_proj, value_low)
-    packed = jnp.concatenate(
-        [
-            second_part.reshape(RANK, 32, 16).transpose(1, 0, 2),
-            jnp.broadcast_to(prompt_back.astype(F32)[None], (32, 16, RANK)),
-            jnp.zeros((32, 16, 96), F32),
-        ],
-        axis=2,
-    )
-    packed = swap(packed, SAMPLE)
-    second_sum = jnp.sum(packed[:, :, :16], axis=0)
-    first_sum = first_sum + tn(
-        packed[:, :, 16:32].reshape(512, RANK).astype(BF16), prompt_columns.reshape(512, 128)
-    )
-    both = jnp.concatenate([first_sum, second_sum, jnp.zeros((RANK, 112), F32)], axis=1)
-    both = jnp.sum(gather(both, GROUP), axis=0)
+    start = gather(
+        jnp.concatenate([own_columns, heads_first(prompt_keys), value_adapter_down.T], axis=0), "zh"
+    )
+    weight = lax.all_gather(start[:, :128], ("x", "y", "c"))
+    weight = weight.reshape(4, 4, 2, 4, 128, HEAD_DIM)
+    key_all = gather(gather(start[:, 128:], "y"), "c")
+
+    send, low, back, first_proj, down = attend_forward(
+        queries, cotangent, key_all, response_keys, chosen, bias, response_rows, prompt_rows,
+        value_adapter_up,
+    )
+    prompt_low, prompt_back, adapter = adapter_terms(
+        low, back, reduce_to_zh(send), first_proj, value_adapter_up, response_rows, prompt_rows
+    )
+    values, part, weight = project(
+        response_rows, prompt_rows, weight, first_proj, value_adapter_up, adapter
+    )
+    part = in_vmem(after_zh_kernel, (4, 352, HEAD_DIM), "after_zh")(swap(part, "zh"))
+    part = in_vmem(after_y_kernel, (2, 1104, HEAD_DIM), "after_y")(swap(part, "y"))
+    part = swap(part, "c")
+    key_send, own_key_grad = attend_backward(
+        queries, cotangent, key_all, part, response_keys, values, chosen, bias
+    )
+    prompt_key_grad = heads_last(sum_first(reduce_to_zh(key_send)).astype(BF16))
+
     factor = ADAPTER_SCALE * float(73728) ** (-0.5)
-    first_grad = both[:, :128].T * factor
-    second_grad = gather(both[:, 128:] * factor, SAMPLE)[:, :, :16]
-    second_grad = second_grad.transpose(1, 0, 2).reshape(RANK, KV_HEADS * HEAD_DIM)
-
-    values = (nn(local_rows, weight) + ADAPTER_SCALE * nn(first_proj, value_adapter_up)).astype(BF16)
-    value_all = gather_parts(heads_first(values[TOKENS:]))
-    key_send, own_key_grad = attend_backward(
-        queries, cotangent, key_all, value_all, response_keys, values[:TOKENS], chosen, bias
-    )
-    prompt_key_grad = heads_last(reduce_parts(key_send).astype(BF16))
-    grads = (nt(value_low, weight) + ADAPTER_SCALE * nn(back_low, down_full)).astype(BF16)
+    both = sum_ring(sum_ring(sum_first(part[:, 1024:]), "x"), "zl") * factor
+    first_grad = both[:16].T
+    second_grad = heads_last(both[16:])
+
+    response_grad = nt(low, weight) + ADAPTER_SCALE * tn(back, down)
+    prompt_grad = nt(prompt_low, weight) + ADAPTER_SCALE * tn(prompt_back, down)
     return (
-        grads[:TOKENS],
-        grads[TOKENS:],
+        response_grad.astype(BF16),
+        prompt_grad.astype(BF16),
         own_key_grad,
         prompt_key_grad,
         first_grad,

time: 323 us -> 228 us (0.71)
  waiting for transfers between devices: 135 us -> 37.7 us
  blocking collectives: 63.6 us -> 83.2 us
  starting transfers between devices: 64 us -> 44.6 us
  local copies, waits for them, and re-layouts: 29.6 us -> 13.4 us
  between operations: 1.09 us -> 14.4 us
  Pallas kernels: 11.6 us -> 16.5 us
    all_to_all x14 -> x5, waiting for transfers between devices: 135 us -> 34.6 us  [swap(): return lax.all_to_all(array, axis, 0, 0, tiled=True)]
    all_to_all x14 -> x5, starting transfers between devices: 64 us -> 25.4 us  [swap(): return lax.all_to_all(array, axis, 0, 0, tiled=True)]
    all_to_all x6 -> x7, blocking collectives: 63.6 us -> 83.2 us  [swap(): return lax.all_to_all(array, axis, 0, 0, tiled=True)]
    ppermute x0 -> x6, starting transfers between devices: none -> 19.1 us  [sum_ring(): lax.ppermute(part, axis, [(i, (i + step) % 4) for i in range(4)])]
    broadcast_in_dim x12 -> x3, local copies, waits for them, and re-layouts: 11.1 us -> 0.88 us  [gather(): return swap(jnp.broadcast_to(array[None], (n,) + array.shape), axis)]
    pallas_call x0 -> x4, Pallas kernels: none -> 4.78 us  [the longest x1 3.36 us: project(): pl.pallas_call(project_kernel, grid=(KV_HEADS,), in_specs=[whole((TOKENS,...]
    transpose x8 -> x1, local copies, waits for them, and re-layouts: 5.09 us -> 0.6 us  [on_device(): first_grad = both[:16].T]
    dot_general x2, matrix products: 0.39 us -> 3.89 us  [tn(): lax.dot_general(left, right, (((0,), (0,)), ((), ())), preferred_element_...]
  transfers between devices with their start and end apart: 14 -> 12, of which waited for: 14 -> 7; matrix products, arithmetic and copies ran while one was open for 8% -> 7% of each run, Pallas kernels for 2% -> 5%
where the time goes in v2:
time: 228 us; the launch traced here: 225 us
  blocking collectives  83.2 us (36%)
  starting transfers between devices  44.6 us (20%)
  waiting for transfers between devices  37.7 us (17%)
  Pallas kernels  16.5 us (7%)
  between operations  14.4 us (6%)
  local copies, waits for them, and re-layouts  13.4 us (6%)
  matrix products  10.3 us (5%)
  other arithmetic  4.7 us (2%)
    all_to_all x7, blocking collectives, swap(): return lax.all_to_all(array, axis, 0, 0, tiled=True)  83.2 us
    all_to_all x5, waiting for transfers between devices, swap(): return lax.all_to_all(array, axis, 0, 0, tiled=True)  34.6 us
    all_to_all x5, starting transfers between devices, swap(): return lax.all_to_all(array, axis, 0, 0, tiled=True)  25.4 us
    ppermute x6, starting transfers between devices, sum_ring(): lax.ppermute(part, axis, [(i, (i + step) % 4) for i in range(4)])  19.1 us
    unnamed x26, local copies, waits for them, and re-layouts  9.68 us
    pallas_call x1, Pallas kernels, attend_backward(): pl.pallas_call(backward_kernel, grid=(KV_HEADS,), in_specs=[heads_of(TOKE...  6.4 us
    dot_general x2, matrix products, nt(): lax.dot_general(left, right, (((1,), (1,)), ((), ())), preferred_element_...  6.37 us
    pallas_call x1, Pallas kernels, attend_forward(): pl.pallas_call(forward_kernel, grid=(KV_HEADS,), in_specs=[heads_of(TOKEN...  5.31 us
  transfers between devices with their start and end apart: 12, of which 7 were waited for; matrix products, arithmetic and copies ran while one was open for 7% of the time, Pallas kernels for 5%

profile of v2, /device:TPU:1, one launch (start us, length us, event | category | flops | bytes accessed | tf_op | source)
XLA Modules:
  0.0 224.8 jit_solution(11044824506292552940)
XLA Ops:
  8.8 28.7 %all_to_all.60 = bf16[4,208,128]{2,1,0:T(8,128)(2,1)S(1)} all-to-all(bf16[4,208,128]{2,1,0:T(8,128)(2,1)S(1)} %broadcast_in_dim.18), channel_id=1, replica_groups=mesh['x'=4,'zl'=4,'y'=4,'zh'=4,'c'=2] {'zh'}, dimensions={0} | all-to-all | bytes 425984 | tf_op jit(solution)/shard_map/all_to_all | solution.py:29
  39.8 4.2 %all-to-all-start.1 = ((bf16[4,4,80,128]{3,2,1,0:T(8,128)(2,1)}), bf16[4,4,80,128]{3,2,1,0:T(8,128)(2,1)S(1)}, u32[]{:S(2)}, u32[]{:S(2)}) async-start(bf16[4,4,80,128]{3,2,1,0:T(8,128)(2,1)} %broadcast_in_dim.19), calls=%async_computation.1 | async-start | bytes 655360 | tf_op jit(solution)/shard_map/all_to_all | solution.py:29
  44.8 5.0 %all-to-all-done.1 = bf16[4,4,80,128]{3,2,1,0:T(8,128)(2,1)S(1)} async-done(((bf16[4,4,80,128]{3,2,1,0:T(8,128)(2,1)}), bf16[4,4,80,128]{3,2,1,0:T(8,128)(2,1)S(1)}, u32[]{:S(2)}, u32[]{:S(2)}) %all-to-all-start.1) | async-done | bytes 327712 | tf_op jit(solution)/shard_map/all_to_all | solution.py:29
  50.0 10.5 %all_to_all.61.key_ref.down_ref = bf16[2,4,4,80,128]{4,3,2,1,0:T(8,128)(2,1)S(1)} all-to-all(bf16[2,4,4,80,128]{4,3,2,1,0:T(8,128)(2,1)S(1)} %broadcast_in_dim.20), channel_id=1, replica_groups=mesh['x'=4,'zl'=4,'y'=4,'zh'=4,'c'=2] {'c'}, dimensions={0} | all-to-all | bytes 1310720 | tf_op jit(solution)/shard_map/all_to_all | solution.py:29
  63.1 5.3 %attend_forward.1 = (bf16[2,4,4,64,128]{4,3,2,1,0:T(8,128)(2,1)S(1)}, bf16[128,512]{1,0:T(8,128)(2,1)S(1)}, bf16[16,128]{1,0:T(8,128)(2,1)S(1)}, bf16[144,16]{1,0:T(8,128)(2,1)S(1)}, bf16[16,4096]{1,0:T(8,128)(2,1)S(1)}) custom-call(bf16[128,4096]{1,0:T(8,128)(2,1)S(1)} %copy-done.7, bf16[128,4096]{1,0:T(8,128)(2,1)S(1)} %copy-done.9, ...), custom_call_target="tpu_custom_call" | custom-call | flops 2000000000 | bytes 5242880 | tf_op jit(solution)/shard_map/attend_forward/pallas_call | solution.py:284
  68.4 4.1 %all_to_all.62 = bf16[2,4,4,64,128]{4,3,2,1,0:T(8,128)(2,1)S(1)} all-to-all(bf16[2,4,4,64,128]{4,3,2,1,0:T(8,128)(2,1)S(1)} %get-tuple-element.22), channel_id=1, replica_groups=mesh['x'=4,'zl'=4,'y'=4,'zh'=4,'c'=2] {'c'}, dimensions={0} | all-to-all | bytes 1048576 | tf_op jit(solution)/shard_map/all_to_all | solution.py:29
  73.4 9.8 %all_to_all.63 = bf16[4,4,64,128]{3,2,1,0:T(8,128)(2,1)S(1)} all-to-all(bf16[4,4,64,128]{3,2,1,0:T(8,128)(2,1)} %reduce_sum.79), channel_id=1, replica_groups=mesh['x'=4,'zl'=4,'y'=4,'zh'=4,'c'=2] {'y'}, dimensions={0} | all-to-all | bytes 524288 | tf_op jit(solution)/shard_map/all_to_all | solution.py:29
  83.2 15.8 %all_to_all.64.got_ref = bf16[4,64,128]{2,1,0:T(8,128)(2,1)S(1)} all-to-all(bf16[4,64,128]{2,1,0:T(8,128)(2,1)S(1)} %reduce_sum.80), channel_id=1, replica_groups=mesh['x'=4,'zl'=4,'y'=4,'zh'=4,'c'=2] {'zh'}, dimensions={0} | all-to-all | bytes 131072 | tf_op jit(solution)/shard_map/all_to_all | solution.py:29
  99.6 2.2 copy-done.4
  101.8 3.4 %project.1 = (bf16[128,512]{1,0:T(8,128)(2,1)S(1)}, bf16[4,256,128]{2,1,0:T(8,128)(2,1)}, bf16[4096,512]{1,0:T(8,128)(2,1)S(1)}) custom-call(bf16[128,4096]{1,0:T(8,128)(2,1)S(1)} %copy-done.3, bf16[16,4096]{1,0:T(8,128)(2,1)S(1)} %copy-done.5, bf16[4,4,2,4,128,128]{5,4,3,2,1,0:T(8,128)(2,1)S(1)} %bitcast.41, ...), custom_call_target="tpu_custom_call" | custom-call | flops 600000000 | bytes 10485760 | tf_op jit(solution)/shard_map/project/pallas_call | solution.py:344
  105.2 1.9 copy-done.1
  107.1 11.1 %all-to-all-start.6 = ((bf16[4,256,128]{2,1,0:T(8,128)(2,1)}), bf16[4,256,128]{2,1,0:T(8,128)(2,1)S(1)}, u32[]{:S(2)}, u32[]{:S(2)}) async-start(bf16[4,256,128]{2,1,0:T(8,128)(2,1)} %get-tuple-element.28), calls=%async_computation.6 | async-start | bytes 524288 | tf_op jit(solution)/shard_map/all_to_all | solution.py:29
  118.2 3.5 %fusion.7 = f32[16,4096]{1,0:T(8,128)S(1)} fusion(bf16[16,512]{1,0:T(8,128)(2,1)S(1)} %get-tuple-element.26, bf16[4096,512]{1,0:T(8,128)(2,1)} %copy-done.1), kind=kOutput, calls=%fused_computation.23 | convolution fusion | flops 67108864 | bytes 4472832 | tf_op jit(solution)/shard_map/dot_general | solution.py:38
  121.8 2.8 %fusion.6 = f32[128,4096]{1,0:T(8,128)} fusion(bf16[128,512]{1,0:T(8,128)(2,1)S(1)} %get-tuple-element.19.low_ref, bf16[4096,512]{1,0:T(8,128)(2,1)S(1)} %copy-done.2), kind=kOutput, calls=%fused_computation.22 | convolution fusion | flops 536870912 | bytes 6422528 | tf_op jit(solution)/shard_map/dot_general | solution.py:38
  124.6 9.7 %all-to-all-done.6.got_ref = bf16[4,256,128]{2,1,0:T(8,128)(2,1)S(1)} async-done(((bf16[4,256,128]{2,1,0:T(8,128)(2,1)}), bf16[4,256,128]{2,1,0:T(8,128)(2,1)S(1)}, u32[]{:S(2)}, u32[]{:S(2)}) %all-to-all-start.6) | async-done | bytes 262176 | tf_op jit(solution)/shard_map/all_to_all | solution.py:29
  135.1 3.5 %all-to-all-start.7 = ((bf16[4,352,128]{2,1,0:T(8,128)(2,1)}), bf16[4,352,128]{2,1,0:T(8,128)(2,1)S(1)}, u32[]{:S(2)}, u32[]{:S(2)}) async-start(bf16[4,352,128]{2,1,0:T(8,128)(2,1)} %after_zh.1), calls=%async_computation.7 | async-start | bytes 720896 | tf_op jit(solution)/shard_map/all_to_all | solution.py:29
  138.6 3.0 %fusion.1 = bf16[128,4096]{1,0:T(8,128)(2,1)} fusion(f32[128,4096]{1,0:T(8,128)} %fusion.6, bf16[16,128]{1,0:T(8,128)(2,1)S(1)} %get-tuple-element.21.back_ref, bf16[16,4096]{1,0:T(8,128)(2,1)S(1)} %get-tuple-element.25), kind=kOutput, calls=%fused_computation.2 | convolution fusion | flops 18350080 | bytes 3280896 | tf_op jit(solution)/shard_map/dot_general | solution.py:42
  141.6 3.0 %all-to-all-done.7.got_ref = bf16[4,352,128]{2,1,0:T(8,128)(2,1)S(1)} async-done(((bf16[4,352,128]{2,1,0:T(8,128)(2,1)}), bf16[4,352,128]{2,1,0:T(8,128)(2,1)S(1)}, u32[]{:S(2)}, u32[]{:S(2)}) %all-to-all-start.7) | async-done | bytes 360480 | tf_op jit(solution)/shard_map/all_to_all | solution.py:29
  144.7 7.6 %all_to_all.65.value_ref = bf16[2,1104,128]{2,1,0:T(8,128)(2,1)S(1)} all-to-all(bf16[2,1104,128]{2,1,0:T(8,128)(2,1)S(1)} %after_y.1), channel_id=1, replica_groups=mesh['x'=4,'zl'=4,'y'=4,'zh'=4,'c'=2] {'c'}, dimensions={0} | all-to-all | bytes 1130496 | tf_op jit(solution)/shard_map/all_to_all | solution.py:29
  152.2 3.8 %collective-permute-start.2 = (f32[80,128]{1,0:T(8,128)S(1)}, f32[80,128]{1,0:T(8,128)S(1)}, u32[]{:S(2)}, u32[]{:S(2)}) collective-permute-start(f32[80,128]{1,0:T(8,128)S(1)} %convert_reduce_fusion), channel_id=1, source_target_pairs={{0,384},{128,0},{256,128},{384,256},{1,385},{129,1},{257,129},{385... | collective-permute-start | bytes 122888 | tf_op jit(solution)/shard_map/ppermute | solution.py:432
  156.0 2.5 %collective-permute-start.1 = (f32[80,128]{1,0:T(8,128)S(1)}, f32[80,128]{1,0:T(8,128)S(1)}, u32[]{:S(2)}, u32[]{:S(2)}) collective-permute-start(f32[80,128]{1,0:T(8,128)S(1)} %convert_reduce_fusion), channel_id=1, source_target_pairs={{0,256},{128,384},{256,0},{384,128},{1,257},{129,385},{257,1},{385... | collective-permute-start | bytes 122888 | tf_op jit(solution)/shard_map/ppermute | solution.py:432
  158.5 2.0 collective-permute-start
  162.3 2.2 collective-permute-done
  164.5 3.4 %collective-permute-start.5 = (f32[80,128]{1,0:T(8,128)S(1)}, f32[80,128]{1,0:T(8,128)S(1)}, u32[]{:S(2)}, u32[]{:S(2)}) collective-permute-start(f32[80,128]{1,0:T(8,128)S(1)} %add_add_fusion), channel_id=1, source_target_pairs={{0,96},{32,0},{64,32},{96,64},{1,97},{33,1},{65,33},{97,65},{2,98}... | collective-permute-start | bytes 122888 | tf_op jit(solution)/shard_map/ppermute | solution.py:432
  167.9 5.3 %collective-permute-start.4 = (f32[80,128]{1,0:T(8,128)S(1)}, f32[80,128]{1,0:T(8,128)S(1)}, u32[]{:S(2)}, u32[]{:S(2)}) collective-permute-start(f32[80,128]{1,0:T(8,128)S(1)} %add_add_fusion), channel_id=1, source_target_pairs={{0,64},{32,96},{64,0},{96,32},{1,65},{33,97},{65,1},{97,33},{2,66}... | collective-permute-start | bytes 122888 | tf_op jit(solution)/shard_map/ppermute | solution.py:432
  173.2 2.2 collective-permute-start.3
  177.8 6.4 %attend_backward.1 = (bf16[2,4,4,64,128]{4,3,2,1,0:T(8,128)(2,1)S(1)}, bf16[128,512]{1,0:T(8,128)(2,1)}) custom-call(bf16[128,4096]{1,0:T(8,128)(2,1)S(1)} %copy-done.8, bf16[128,4096]{1,0:T(8,128)(2,1)S(1)} %copy-done.10, bf16[2,4,4,80,128]{4,3,2,1,0:T(8,128)(2,1)S(1)} %all_to_all.61.key_ref.down_ref, bf16[2,1104,128]{2,1,0:T(8,128)(2,1)S(1)} %all_to_all.65.value_ref, ...), custom_call_target="tpu_custom_call" | custom-call | flops 3000000000 | bytes 5242880 | tf_op jit(solution)/shard_map/attend_backward/pallas_call | solution.py:375
  184.2 6.7 %all_to_all.66 = bf16[2,4,4,64,128]{4,3,2,1,0:T(8,128)(2,1)S(1)} all-to-all(bf16[2,4,4,64,128]{4,3,2,1,0:T(8,128)(2,1)S(1)} %get-tuple-element.31), channel_id=1, replica_groups=mesh['x'=4,'zl'=4,'y'=4,'zh'=4,'c'=2] {'c'}, dimensions={0} | all-to-all | bytes 1048576 | tf_op jit(solution)/shard_map/all_to_all | solution.py:29
  191.8 3.4 %all-to-all-start.10 = ((bf16[4,4,64,128]{3,2,1,0:T(8,128)(2,1)}), bf16[4,4,64,128]{3,2,1,0:T(8,128)(2,1)S(1)}, u32[]{:S(2)}, u32[]{:S(2)}) async-start(bf16[4,4,64,128]{3,2,1,0:T(8,128)(2,1)} %reduce_sum.81), calls=%async_computation.10 | async-start | bytes 524288 | tf_op jit(solution)/shard_map/all_to_all | solution.py:29
  195.9 5.4 %all-to-all-done.10 = bf16[4,4,64,128]{3,2,1,0:T(8,128)(2,1)S(1)} async-done(((bf16[4,4,64,128]{3,2,1,0:T(8,128)(2,1)}), bf16[4,4,64,128]{3,2,1,0:T(8,128)(2,1)S(1)}, u32[]{:S(2)}, u32[]{:S(2)}) %all-to-all-start.10) | async-done | bytes 262176 | tf_op jit(solution)/shard_map/all_to_all | solution.py:29
  202.0 3.3 %all-to-all-start.11 = ((bf16[4,64,128]{2,1,0:T(8,128)(2,1)}), bf16[4,64,128]{2,1,0:T(8,128)(2,1)S(1)}, u32[]{:S(2)}, u32[]{:S(2)}) async-start(bf16[4,64,128]{2,1,0:T(8,128)(2,1)} %reduce_sum.82), calls=%async_computation.11 | async-start | bytes 131072 | tf_op jit(solution)/shard_map/all_to_all | solution.py:29
  205.9 11.4 %all-to-all-done.11 = bf16[4,64,128]{2,1,0:T(8,128)(2,1)S(1)} async-done(((bf16[4,64,128]{2,1,0:T(8,128)(2,1)}), bf16[4,64,128]{2,1,0:T(8,128)(2,1)S(1)}, u32[]{:S(2)}, u32[]{:S(2)}) %all-to-all-start.11) | async-done | bytes 65568 | tf_op jit(solution)/shard_map/all_to_all | solution.py:29
  (61 shorter events, 17.3 us)
Async XLA Ops:
  7.2 0.9 copy-start
  7.2 53.4 %copy-start.6 = (bf16[16,512]{1,0:T(8,128)(2,1)S(1)}, bf16[16,512]{1,0:T(8,128)(2,1)}, u32[]{:S(2)}) copy-start(bf16[16,512]{1,0:T(8,128)(2,1)} %up_ref.5) | copy-start | bytes 49156
  7.2 53.4 %copy-start.5 = (bf16[16,4096]{1,0:T(8,128)(2,1)S(1)}, bf16[16,4096]{1,0:T(8,128)(2,1)}, u32[]{:S(2)}) copy-start(bf16[16,4096]{1,0:T(8,128)(2,1)} %prompt_ref.5) | copy-start | bytes 393220
  7.2 53.4 %copy-start.3 = (bf16[128,4096]{1,0:T(8,128)(2,1)S(1)}, bf16[128,4096]{1,0:T(8,128)(2,1)}, u32[]{:S(2)}) copy-start(bf16[128,4096]{1,0:T(8,128)(2,1)} %x_ref.5) | copy-start | bytes 3145732
  7.2 53.4 %copy-start.11 = (bf16[128,512]{1,0:T(8,128)(2,1)S(1)}, bf16[128,512]{1,0:T(8,128)(2,1)}, u32[]{:S(2)}) copy-start(bf16[128,512]{1,0:T(8,128)(2,1)} %own_key_ref.3) | copy-start | bytes 393220
  7.2 92.4 %all-gather.3.cloned.1.call-start = ((), (), s32[]{:S(2)}) async-start(), calls=%async_computation.12 | async-start | bytes 4325376 | tf_op jit(solution)/shard_map/all_gather | solution.py:463
  39.8 10.1 %all-to-all-start.1 = ((bf16[4,4,80,128]{3,2,1,0:T(8,128)(2,1)}), bf16[4,4,80,128]{3,2,1,0:T(8,128)(2,1)S(1)}, u32[]{:S(2)}, u32[]{:S(2)}) async-start(bf16[4,4,80,128]{3,2,1,0:T(8,128)(2,1)} %broadcast_in_dim.19), calls=%async_computation.1 | async-start | bytes 655360 | tf_op jit(solution)/shard_map/all_to_all | solution.py:29
  60.6 1.2 copy-start.7
  61.9 1.2 copy-start.9
  99.6 2.2 copy-start.4
  105.2 1.9 copy-start.1
  107.1 27.2 %all-to-all-start.6 = ((bf16[4,256,128]{2,1,0:T(8,128)(2,1)}), bf16[4,256,128]{2,1,0:T(8,128)(2,1)S(1)}, u32[]{:S(2)}, u32[]{:S(2)}) async-start(bf16[4,256,128]{2,1,0:T(8,128)(2,1)} %get-tuple-element.28), calls=%async_computation.6 | async-start | bytes 524288 | tf_op jit(solution)/shard_map/all_to_all | solution.py:29
  118.2 3.5 %copy-start.2 = (bf16[4096,512]{1,0:T(8,128)(2,1)S(1)}, bf16[4096,512]{1,0:T(8,128)(2,1)}, u32[]{:S(2)}) copy-start(bf16[4096,512]{1,0:T(8,128)(2,1)} %copy-done.1) | copy-start | bytes 12582916
  135.1 9.5 %all-to-all-start.7 = ((bf16[4,352,128]{2,1,0:T(8,128)(2,1)}), bf16[4,352,128]{2,1,0:T(8,128)(2,1)S(1)}, u32[]{:S(2)}, u32[]{:S(2)}) async-start(bf16[4,352,128]{2,1,0:T(8,128)(2,1)} %after_zh.1), calls=%async_computation.7 | async-start | bytes 720896 | tf_op jit(solution)/shard_map/all_to_all | solution.py:29
  152.2 9.1 %collective-permute-start.2 = (f32[80,128]{1,0:T(8,128)S(1)}, f32[80,128]{1,0:T(8,128)S(1)}, u32[]{:S(2)}, u32[]{:S(2)}) collective-permute-start(f32[80,128]{1,0:T(8,128)S(1)} %convert_reduce_fusion), channel_id=1, source_target_pairs={{0,384},{128,0},{256,128},{384,256},{1,385},{129,1},{257,129},{385... | collective-permute-start | bytes 122888 | tf_op jit(solution)/shard_map/ppermute | solution.py:432
  156.0 6.3 %collective-permute-start.1 = (f32[80,128]{1,0:T(8,128)S(1)}, f32[80,128]{1,0:T(8,128)S(1)}, u32[]{:S(2)}, u32[]{:S(2)}) collective-permute-start(f32[80,128]{1,0:T(8,128)S(1)} %convert_reduce_fusion), channel_id=1, source_target_pairs={{0,256},{128,384},{256,0},{384,128},{1,257},{129,385},{257,1},{385... | collective-permute-start | bytes 122888 | tf_op jit(solution)/shard_map/ppermute | solution.py:432
  158.5 6.0 %collective-permute-start = (f32[80,128]{1,0:T(8,128)S(1)}, f32[80,128]{1,0:T(8,128)S(1)}, u32[]{:S(2)}, u32[]{:S(2)}) collective-permute-start(f32[80,128]{1,0:T(8,128)S(1)} %convert_reduce_fusion), channel_id=1, source_target_pairs={{0,128},{128,256},{256,384},{384,0},{1,129},{129,257},{257,385},{3... | collective-permute-start | bytes 122888 | tf_op jit(solution)/shard_map/ppermute | solution.py:432
  164.5 30.7 %collective-permute-start.5 = (f32[80,128]{1,0:T(8,128)S(1)}, f32[80,128]{1,0:T(8,128)S(1)}, u32[]{:S(2)}, u32[]{:S(2)}) collective-permute-start(f32[80,128]{1,0:T(8,128)S(1)} %add_add_fusion), channel_id=1, source_target_pairs={{0,96},{32,0},{64,32},{96,64},{1,97},{33,1},{65,33},{97,65},{2,98}... | collective-permute-start | bytes 122888 | tf_op jit(solution)/shard_map/ppermute | solution.py:432
  167.9 27.3 %collective-permute-start.4 = (f32[80,128]{1,0:T(8,128)S(1)}, f32[80,128]{1,0:T(8,128)S(1)}, u32[]{:S(2)}, u32[]{:S(2)}) collective-permute-start(f32[80,128]{1,0:T(8,128)S(1)} %add_add_fusion), channel_id=1, source_target_pairs={{0,64},{32,96},{64,0},{96,32},{1,65},{33,97},{65,1},{97,33},{2,66}... | collective-permute-start | bytes 122888 | tf_op jit(solution)/shard_map/ppermute | solution.py:432
  173.2 22.0 %collective-permute-start.3 = (f32[80,128]{1,0:T(8,128)S(1)}, f32[80,128]{1,0:T(8,128)S(1)}, u32[]{:S(2)}, u32[]{:S(2)}) collective-permute-start(f32[80,128]{1,0:T(8,128)S(1)} %add_add_fusion), channel_id=1, source_target_pairs={{0,32},{32,64},{64,96},{96,0},{1,33},{33,65},{65,97},{97,1},{2,34}... | collective-permute-start | bytes 122888 | tf_op jit(solution)/shard_map/ppermute | solution.py:432
  175.4 1.2 copy-start.8
  176.6 1.2 copy-start.10
  191.8 9.5 %all-to-all-start.10 = ((bf16[4,4,64,128]{3,2,1,0:T(8,128)(2,1)}), bf16[4,4,64,128]{3,2,1,0:T(8,128)(2,1)S(1)}, u32[]{:S(2)}, u32[]{:S(2)}) async-start(bf16[4,4,64,128]{3,2,1,0:T(8,128)(2,1)} %reduce_sum.81), calls=%async_computation.10 | async-start | bytes 524288 | tf_op jit(solution)/shard_map/all_to_all | solution.py:29
  202.0 15.3 %all-to-all-start.11 = ((bf16[4,64,128]{2,1,0:T(8,128)(2,1)}), bf16[4,64,128]{2,1,0:T(8,128)(2,1)S(1)}, u32[]{:S(2)}, u32[]{:S(2)}) async-start(bf16[4,64,128]{2,1,0:T(8,128)(2,1)} %reduce_sum.82), calls=%async_computation.11 | async-start | bytes 131072 | tf_op jit(solution)/shard_map/all_to_all | solution.py:29
Sparse Core Ops, SparseCore 0:
  38.3 60.4 all-gather.2

commit v3 on v2

v3 whole, which is shorter than its diff:
```python
import jax
import jax.numpy as jnp
import numpy as np
from jax import lax
from jax.experimental import pallas as pl
from jax.experimental.pallas import tpu as pltpu
from jax.sharding import Mesh, PartitionSpec as P

HEADS = 32
KV_HEADS = 4
HEAD_DIM = 128
GROUP_SIZE = HEADS // KV_HEADS
PROMPT_LEN = 128
PROMPTS = 4
RANK = 16
TOKENS = 128
D = 4096
SCALE = HEAD_DIM**-0.5
ADAPTER_SCALE = 2.0
FACTOR = ADAPTER_SCALE * float(73728) ** (-0.5)
AXES = ("x", "zl", "y", "zh", "c")
SAMPLE = ("y", "zh", "c")
GROUP = ("x", "zl")
OWNERS = ("y", "c")
PAIR = 2 * TOKENS
F32 = jnp.float32
BF16 = jnp.bfloat16


def swap(array, axis):
    return lax.all_to_all(array, axis, 0, 0, tiled=True)


def gather(array, axis):
    n = lax.axis_size(axis)
    return swap(jnp.broadcast_to(array[None], (n,) + array.shape), axis)


def nt(left, right):
    return lax.dot_general(left, right, (((1,), (1,)), ((), ())), preferred_element_type=F32)


def tn(left, right):
    return lax.dot_general(left, right, (((0,), (0,)), ((), ())), preferred_element_type=F32)


def nn(left, right):
    return jnp.dot(left, right, preferred_element_type=F32)


def expand(rows, chosen):
    zero = jnp.zeros_like(rows)
    return jnp.concatenate([jnp.where(chosen == p, rows, zero) for p in range(PROMPTS)], axis=1)


def pair_rows(ref, pair):
    first = 2 * pair * HEAD_DIM
    return jnp.concatenate(
        [ref[:, first : first + HEAD_DIM], ref[:, first + HEAD_DIM : first + 2 * HEAD_DIM]], axis=0
    )


def prompt_block(ref):
    return jnp.concatenate(
        [
            jnp.concatenate([ref[p, c, zh] for zh in range(4) for c in range(2)], axis=0)
            for p in range(PROMPTS)
        ],
        axis=1,
    )


def value_block(ref, k):
    def part(c, p, zh):
        return ref[p * 2 + c, pl.ds(pl.multiple_of(zh * 64 + k * 16, 16), 16), :]

    return jnp.concatenate(
        [
            jnp.concatenate([part(c, p, zh) for zh in range(4) for c in range(2)], axis=0)
            for p in range(PROMPTS)
        ],
        axis=1,
    )


def spread(ref, k, block):
    for p in range(PROMPTS):
        for zh in range(4):
            for c in range(2):
                s = (zh * 2 + c) * 16
                row = pl.multiple_of(zh * 64 + k * 16, 16)
                ref[p * 2 + c, pl.ds(row, 16), :] = block[
                    s : s + 16, p * HEAD_DIM : (p + 1) * HEAD_DIM
                ].astype(ref.dtype)


def softmax_pair(key_cat, own_key, expanded, rows, bias):
    seen = nt(key_cat, expanded) * SCALE
    own = nt(own_key, rows) * SCALE + bias
    top = jnp.maximum(jnp.max(seen, axis=0, keepdims=True), jnp.max(own, axis=0, keepdims=True))
    seen, own = jnp.exp(seen - top), jnp.exp(own - top)
    total = jnp.sum(seen, axis=0, keepdims=True) + jnp.sum(own, axis=0, keepdims=True)
    return seen / total, own / total


BLOCKS = [
    (((y * 4 + zh) * 2 + c) * 128, y, zh, c) for y in range(4) for zh in range(4) for c in range(2)
]


def forward_kernel(
    q_ref, cot_ref, key_ref, down_ref, own_key_ref, chosen_ref, bias_ref, x_ref, up_ref,
    send_ref, low_ref, back_ref, first_ref, down_out_ref, softmax_ref,
    probs, own_probs, cots, back,
):
    k = pl.program_id(0)
    key_cat = prompt_block(key_ref)
    own_key = own_key_ref[...]
    chosen = chosen_ref[...]
    bias = bias_ref[...]
    for pair in range(GROUP_SIZE // 2):
        rows = pair_rows(q_ref, pair)
        seen, own = softmax_pair(key_cat, own_key, expand(rows, chosen), rows, bias)
        at = pl.ds(pair * PAIR, PAIR)
        softmax_ref[0, :TOKENS, at] = seen
        softmax_ref[0, TOKENS:, at] = own
        probs[:, at] = seen.astype(BF16)
        own_probs[:, at] = own.astype(BF16)
        cot = pair_rows(cot_ref, pair)
        cots[at, : PROMPTS * HEAD_DIM] = expand(cot, chosen)
        cots[at, PROMPTS * HEAD_DIM :] = cot
    spread(send_ref, k, nn(probs[...], cots[:, : PROMPTS * HEAD_DIM]))
    low = nn(own_probs[...], cots[:, PROMPTS * HEAD_DIM :]).astype(BF16)
    low_ref[...] = low

    @pl.when(k == 0)
    def _():
        back[...] = jnp.zeros_like(back)
        for at, y, zh, c in BLOCKS:
            down_out_ref[:, at : at + 128] = down_ref[y, c, zh]
        first_ref[...] = nt(x_ref[...], down_out_ref[...]).astype(BF16)

    back[...] += nt(up_ref[...], low)

    @pl.when(k == KV_HEADS - 1)
    def _():
        back_ref[...] = back[...].astype(BF16)


def place_before(place, step):
    return lax.rem(place + (4 - step), 4)


def adapter_kernel(
    place_ref, low_ref, back_ref, got_ref, first_ref, up_ref, down_ref, x_ref,
    prompt_ref, prompt1_ref, prompt2_ref, prompt3_ref,
    part_ref, send_ref,
    total,
):
    total[...] = total_of(got_ref[...]).astype(BF16)
    for zh in range(4):
        part_ref[zh] = total[zh * 64 : (zh + 1) * 64, :]
    up = up_ref[...]
    first = first_ref[...]
    prompts = jnp.concatenate(
        [prompt_ref[...], prompt1_ref[...], prompt2_ref[...], prompt3_ref[...]], axis=0
    )
    prompt_first = nt(prompts, down_ref[...]).astype(BF16)
    prompt_back = jnp.zeros((RANK, 64), F32)
    for k in range(KV_HEADS):
        at = slice(k * HEAD_DIM, (k + 1) * HEAD_DIM)
        starts = [place_before(place_ref[2], step) * 64 + k * 16 for step in range(4)]
        low = jnp.concatenate(
            [total[pl.ds(pl.multiple_of(row, 16), 16), :] for row in starts], axis=0
        )
        prompt_back = prompt_back + nt(up[:, at], low)
        second = tn(first, low_ref[:, at]) + tn(prompt_first, low)
        send_ref[512 + k * 16 : 512 + (k + 1) * 16, :] = second.astype(BF16)
    grad = nn(back_ref[...], x_ref[...]) + nn(prompt_back.astype(BF16), prompts)
    grad = grad.astype(BF16)
    for at, y, zh, c in BLOCKS:
        row = ((y * 2 + c) * 4 + zh) * 16
        send_ref[row : row + 16, :] = grad[:, at : at + 128]


def project_kernel(
    place_ref, x_ref, prompt_ref, prompt1_ref, prompt2_ref, prompt3_ref,
    weight_ref, other_ref, down_ref, up_ref,
    values_ref, send_ref, weight_out_ref,
    rows, first,
):
    k = pl.program_id(0)

    @pl.when(k == 0)
    def _():
        rows[:TOKENS, :] = x_ref[...]
        for step, ref in enumerate((prompt_ref, prompt1_ref, prompt2_ref, prompt3_ref)):
            rows[TOKENS + step * 16 : TOKENS + (step + 1) * 16, :] = ref[...]
        first[...] = nt(rows[...], down_ref[...]).astype(BF16)

    for y in range(4):
        for zh in range(4):
            for ref, c in ((weight_ref, place_ref[3]), (other_ref, 1 - place_ref[3])):
                row = pl.multiple_of(((y * 4 + zh) * 2 + c) * 128, 128)
                weight_out_ref[pl.ds(row, 128), :] = ref[0, y, zh]
    values = nn(rows[...], weight_out_ref[...]) + ADAPTER_SCALE * nn(first[...], up_ref[...])
    values = values.astype(BF16)
    values_ref[...] = values[:TOKENS]
    for step in range(4):
        row = place_before(place_ref[2], step) * 64 + k * 16
        part = values[TOKENS + step * 16 : TOKENS + (step + 1) * 16]
        for owner in range(8):
            send_ref[owner, pl.ds(pl.multiple_of(row, 16), 16), :] = part


def total_of(parts):
    parts = parts.astype(F32)
    total = parts[0]
    for i in range(1, parts.shape[0]):
        total = total + parts[i]
    return total


def keys_y_kernel(got_ref, value_ref, send_ref):
    second = total_of(got_ref[:, 320:, :]).astype(BF16)
    for zh in range(4):
        send_ref[zh, :64, :] = total_of(got_ref[:, zh * 64 : (zh + 1) * 64, :]).astype(BF16)
        send_ref[zh, 64:128, :] = value_ref[zh]
        at = 256 + zh * 16
        send_ref[zh, 128:144, :] = total_of(got_ref[:, at : at + 16, :]).astype(BF16)
        send_ref[zh, 144:, :] = second


def keys_zh_kernel(got_ref, key_ref, low_ref, send_ref):
    total = total_of(got_ref[...])
    for k in range(KV_HEADS):
        at = slice(k * HEAD_DIM, (k + 1) * HEAD_DIM)
        key_ref[:, at] = total[k * 16 : (k + 1) * 16].astype(BF16)
        low_ref[:, at] = total[64 + k * 16 : 64 + (k + 1) * 16].astype(BF16)
    terms = total[128:].astype(BF16)
    for g in range(16):
        send_ref[g] = terms


def group_kernel(got_ref, first_ref, second_ref):
    total = total_of(got_ref[...]) * FACTOR
    first_ref[...] = total[:16]
    for k in range(KV_HEADS):
        second_ref[:, k * HEAD_DIM : (k + 1) * HEAD_DIM] = total[16 + k * 16 : 16 + (k + 1) * 16]


def prompt_kernel(low_ref, up_ref, down_ref, weight_ref, grad_ref, back):
    @pl.when(pl.program_id(0) == 0)
    def _():
        back[...] = nt(low_ref[...], up_ref[...]).astype(BF16)

    grad = nt(low_ref[...], weight_ref[...]) + ADAPTER_SCALE * nn(back[...], down_ref[...])
    grad_ref[...] = grad.astype(BF16)


def in_vmem(kernel, n, shapes, name):
    return pl.pallas_call(
        kernel,
        in_specs=[pl.BlockSpec(memory_space=pltpu.VMEM)] * n,
        out_specs=jax.tree.map(lambda _: pl.BlockSpec(memory_space=pltpu.VMEM), shapes),
        out_shape=shapes,
        compiler_params=pltpu.CompilerParams(vmem_limit_bytes=16 << 20),
        name=name,
    )


def sent(*shape):
    return jax.ShapeDtypeStruct(shape, BF16)


def backward_kernel(
    q_ref, cot_ref, softmax_ref, value_ref, own_value_ref, chosen_ref, adapter_ref,
    send_ref, own_ref,
    grads, own_grads, queries,
):
    k = pl.program_id(0)

    @pl.when(k == 0)
    def _():
        for owner in range(8):
            send_ref[owner, 256:320, :] = adapter_ref[owner * 64 : (owner + 1) * 64, :]
            send_ref[owner, 320:, :] = adapter_ref[512:, :]

    value_cat = value_block(value_ref, k)
    own_value = own_value_ref[...]
    chosen = chosen_ref[...]
    for pair in range(GROUP_SIZE // 2):
        rows = pair_rows(q_ref, pair)
        at = pl.ds(pair * PAIR, PAIR)
        queries[at, : PROMPTS * HEAD_DIM] = expand(rows, chosen)
        queries[at, PROMPTS * HEAD_DIM :] = rows
        seen = softmax_ref[0, :TOKENS, at]
        own = softmax_ref[0, TOKENS:, at]
        cot = pair_rows(cot_ref, pair)
        seen_grad = nt(value_cat, expand(cot, chosen))
        own_grad = nt(own_value, cot)
        delta = jnp.sum(seen.astype(BF16).astype(F32) * seen_grad, axis=0, keepdims=True) + jnp.sum(
            own.astype(BF16).astype(F32) * own_grad, axis=0, keepdims=True
        )
        grads[:, at] = (seen * (seen_grad - delta)).astype(BF16)
        own_grads[:, at] = (own * (own_grad - delta)).astype(BF16)
    spread(send_ref, k, nn(grads[...], queries[:, : PROMPTS * HEAD_DIM]) * SCALE)
    own_ref[...] = (nn(own_grads[...], queries[:, PROMPTS * HEAD_DIM :]) * SCALE).astype(BF16)


def whole(shape):
    return pl.BlockSpec(shape, lambda k: (0,) * len(shape))


def heads_of(rows, width):
    return pl.BlockSpec((rows, width), lambda k: (0, k))


PROMPT_SPEC = pl.BlockSpec((4, 2, 4, 16, HEAD_DIM), lambda k: (0, 0, 0, k, 0))
WIDE = GROUP_SIZE * HEAD_DIM
ROWS = GROUP_SIZE * TOKENS


DOWN_SPEC = pl.BlockSpec((4, 2, 4, 16, HEAD_DIM), lambda k: (0, 0, 0, KV_HEADS, 0))
PARAMS = pltpu.CompilerParams(vmem_limit_bytes=56 << 20, dimension_semantics=("arbitrary",))


def attend_forward(queries, cotangent, keys, own_keys, chosen, bias, rows, up):
    return pl.pallas_call(
        forward_kernel,
        grid=(KV_HEADS,),
        in_specs=[
            heads_of(TOKENS, WIDE),
            heads_of(TOKENS, WIDE),
            PROMPT_SPEC,
            DOWN_SPEC,
            heads_of(TOKENS, HEAD_DIM),
            whole((PAIR, HEAD_DIM)),
            whole((TOKENS, PAIR)),
            whole((TOKENS, D)),
            heads_of(RANK, HEAD_DIM),
        ],
        out_specs=[
            whole((8, 256, HEAD_DIM)),
            heads_of(TOKENS, HEAD_DIM),
            whole((RANK, TOKENS)),
            whole((TOKENS, RANK)),
            whole((RANK, D)),
            pl.BlockSpec((1, 2 * TOKENS, ROWS), lambda k: (k, 0, 0)),
        ],
        out_shape=[
            sent(8, 256, HEAD_DIM),
            sent(TOKENS, KV_HEADS * HEAD_DIM),
            sent(RANK, TOKENS),
            sent(TOKENS, RANK),
            sent(RANK, D),
            jax.ShapeDtypeStruct((KV_HEADS, 2 * TOKENS, ROWS), F32),
        ],
        scratch_shapes=[
            pltpu.VMEM((TOKENS, ROWS), BF16),
            pltpu.VMEM((TOKENS, ROWS), BF16),
            pltpu.VMEM((ROWS, (PROMPTS + 1) * HEAD_DIM), BF16),
            pltpu.VMEM((RANK, TOKENS), F32),
        ],
        compiler_params=PARAMS,
        cost_estimate=pl.CostEstimate(
            flops=2_000_000_000, bytes_accessed=5 << 20, transcendentals=1 << 20
        ),
        name="attend_forward",
    )(queries, cotangent, keys, keys, own_keys, chosen, bias, rows, up)


def adapter_terms(place, low, back, got, first, up, down, rows, prompts):
    vmem = pl.BlockSpec(memory_space=pltpu.VMEM)
    return pl.pallas_call(
        adapter_kernel,
        in_specs=[pl.BlockSpec(memory_space=pltpu.SMEM)] + [vmem] * 11,
        out_specs=[vmem] * 2,
        out_shape=[sent(4, 64, HEAD_DIM), sent(576, HEAD_DIM)],
        scratch_shapes=[pltpu.VMEM((256, HEAD_DIM), BF16)],
        compiler_params=pltpu.CompilerParams(vmem_limit_bytes=24 << 20),
        name="adapter_terms",
    )(place, low, back, got, first, up, down, rows, *prompts)


def project(place, rows, prompts, weight, other, down, up):
    width = KV_HEADS * HEAD_DIM

    def const(*shape):
        return pl.BlockSpec(shape, lambda k, place: (0,) * len(shape))

    def head(rows):
        return pl.BlockSpec((rows, HEAD_DIM), lambda k, place: (0, k))

    block = pl.BlockSpec((1, 4, 4, 128, HEAD_DIM), lambda k, place: (k, 0, 0, 0, 0))
    return pl.pallas_call(
        project_kernel,
        grid_spec=pltpu.PrefetchScalarGridSpec(
            num_scalar_prefetch=1,
            grid=(KV_HEADS,),
            in_specs=[
                const(TOKENS, D),
                const(16, D),
                const(16, D),
                const(16, D),
                const(16, D),
                block,
                block,
                const(RANK, D),
                head(RANK),
            ],
            out_specs=[head(TOKENS), const(8, 256, HEAD_DIM), head(D)],
            scratch_shapes=[
                pltpu.VMEM((TOKENS + 64, D), BF16),
                pltpu.VMEM((TOKENS + 64, RANK), BF16),
            ],
        ),
        out_shape=[sent(TOKENS, width), sent(8, 256, HEAD_DIM), sent(D, width)],
        compiler_params=PARAMS,
        cost_estimate=pl.CostEstimate(
            flops=600_000_000, bytes_accessed=10 << 20, transcendentals=0
        ),
        name="project",
    )(place, rows, *prompts, weight, other, down, up)


def prompt_gradient(low, up, down, weight):
    width = KV_HEADS * HEAD_DIM
    return pl.pallas_call(
        prompt_kernel,
        grid=(4,),
        in_specs=[
            whole((16, width)),
            whole((RANK, width)),
            heads_of(RANK, 1024),
            pl.BlockSpec((1024, width), lambda k: (k, 0)),
        ],
        out_specs=heads_of(16, 1024),
        out_shape=sent(16, D),
        scratch_shapes=[pltpu.VMEM((16, RANK), BF16)],
        compiler_params=PARAMS,
        name="prompt_gradient",
    )(low, up, down, weight)


def attend_backward(queries, cotangent, softmax, values, own_values, chosen, adapter):
    return pl.pallas_call(
        backward_kernel,
        grid=(KV_HEADS,),
        in_specs=[
            heads_of(TOKENS, WIDE),
            heads_of(TOKENS, WIDE),
            pl.BlockSpec((1, 2 * TOKENS, ROWS), lambda k: (k, 0, 0)),
            whole((8, 256, HEAD_DIM)),
            heads_of(TOKENS, HEAD_DIM),
            whole((PAIR, HEAD_DIM)),
            whole((576, HEAD_DIM)),
        ],
        out_specs=[whole((8, 384, HEAD_DIM)), heads_of(TOKENS, HEAD_DIM)],
        out_shape=[sent(8, 384, HEAD_DIM), sent(TOKENS, KV_HEADS * HEAD_DIM)],
        scratch_shapes=[
            pltpu.VMEM((TOKENS, ROWS), BF16),
            pltpu.VMEM((TOKENS, ROWS), BF16),
            pltpu.VMEM((ROWS, (PROMPTS + 1) * HEAD_DIM), BF16),
        ],
        compiler_params=PARAMS,
        cost_estimate=pl.CostEstimate(
            flops=3_000_000_000, bytes_accessed=9 << 20, transcendentals=0
        ),
        name="attend_backward",
    )(queries, cotangent, softmax, values, own_values, chosen, adapter)


def heads_first(rows):
    return rows.reshape(16, KV_HEADS, HEAD_DIM).transpose(1, 0, 2).reshape(KV_HEADS * 16, HEAD_DIM)


def from_others(part, axis):
    return [
        lax.ppermute(part, axis, [(i, (i + step) % 4) for i in range(4)]) for step in range(1, 4)
    ]


def after(array, *others):
    return lax.optimization_barrier((array, *others))[0]


def on_device(
    response_rows,
    prompt_rows,
    queries,
    response_keys,
    prompt_keys,
    cotangent,
    segment_index,
    prompt_choice,
    frozen_value_weight,
    value_adapter_down,
    value_adapter_up,
):
    segments = segment_index.reshape(TOKENS)
    onehot = (segments[:, None] == jnp.arange(8, dtype=jnp.int32)[None, :]).astype(jnp.int32)
    token_prompt = jnp.sum(onehot * prompt_choice.reshape(1, 8), axis=1)
    chosen = jnp.broadcast_to(jnp.tile(token_prompt, 2)[:, None], (PAIR, HEAD_DIM))
    position = jnp.arange(TOKENS, dtype=jnp.int32)
    own_seen = (segments[:, None] == segments[None, :]) & (position[:, None] <= position[None, :])
    bias = jnp.tile(jnp.where(own_seen, 0.0, -1e30).astype(F32), (1, 2))

    own_columns = lax.dynamic_slice_in_dim(
        frozen_value_weight, lax.axis_index("x") * HEAD_DIM, HEAD_DIM, 1
    )
    start = gather(
        jnp.concatenate([own_columns, heads_first(prompt_keys), value_adapter_down.T], axis=0), "zh"
    )
    place = jnp.stack([lax.axis_index(axis) for axis in ("x", "y", "zh", "c")]).astype(jnp.int32)
    key_all = gather(start[:, 128:], OWNERS).reshape(4, 2, 4, 80, HEAD_DIM)
    weight_part, prompt_part = lax.optimization_barrier((start[:, :128], prompt_rows, key_all))[:2]
    prompts = [prompt_rows, *from_others(prompt_part, "zh")]
    weight = gather(weight_part, ("x", "y")).reshape(4, 4, 4, 128, HEAD_DIM)

    send, low, back, first_proj, down, softmax = attend_forward(
        queries, cotangent, key_all, response_keys, chosen, bias, response_rows, value_adapter_up
    )
    other = lax.ppermute(after(weight, low, *prompts), "c", [(0, 1), (1, 0)])
    value_part, adapter = adapter_terms(
        place, low, back, swap(send, OWNERS), first_proj, value_adapter_up, down, response_rows,
        prompts,
    )
    values, part, weight = project(
        place, response_rows, prompts, weight, other, down, value_adapter_up
    )
    key_send, own_key_grad = attend_backward(
        queries, cotangent, softmax, swap(part, OWNERS), values, chosen, adapter
    )
    part = in_vmem(keys_y_kernel, 2, sent(4, 208, HEAD_DIM), "keys_y")(
        swap(key_send, OWNERS), value_part
    )
    response_grad = nt(low, weight) + ADAPTER_SCALE * tn(back, down)
    response_grad = response_grad.astype(BF16)
    part, response_grad = lax.optimization_barrier((swap(part, "zh"), response_grad))
    prompt_key_grad, prompt_low, part = in_vmem(
        keys_zh_kernel,
        1,
        [sent(16, KV_HEADS * HEAD_DIM), sent(16, KV_HEADS * HEAD_DIM), sent(16, 80, HEAD_DIM)],
        "keys_zh",
    )(part)
    first_grad, second_grad = in_vmem(
        group_kernel,
        1,
        [
            jax.ShapeDtypeStruct((RANK, 128), F32),
            jax.ShapeDtypeStruct((RANK, KV_HEADS * HEAD_DIM), F32),
        ],
        "over_group",
    )(swap(part, GROUP))
    return (
        response_grad,
        prompt_gradient(prompt_low, value_adapter_up, down, weight),
        own_key_grad,
        prompt_key_grad,
        first_grad.T,
        second_grad,
    )


def solution(mesh):
    fine = Mesh(np.asarray(mesh.devices).reshape(4, 4, 4, 4, 2), AXES)
    rows = P(AXES, None)
    in_specs = (rows,) * 8 + (P(SAMPLE, None), P(SAMPLE, None), P())
    out_specs = (rows,) * 4 + (P(SAMPLE, None), P())
    return jax.shard_map(
        on_device, mesh=fine, in_specs=in_specs, out_specs=out_specs, check_vma=False
    )
```

time: 228 us -> 192 us (0.84)
  blocking collectives: 83.2 us -> 45.2 us
  Pallas kernels: 16.5 us -> 31.5 us
  between operations: 14.4 us -> 0.92 us
  waiting for transfers between devices: 37.7 us -> 47.1 us
  matrix products: 10.3 us -> 5.1 us
  other arithmetic: 4.7 us -> 1.51 us
  starting transfers between devices: 44.6 us -> 47.7 us
    all_to_all x7 -> x2, blocking collectives: 83.2 us -> 45.2 us  [swap(): return lax.all_to_all(array, axis, 0, 0, tiled=True)]
    ppermute x6 -> x4, waiting for transfers between devices: 3.1 us -> 16 us  [the longest x3 16 us: from_others(): lax.ppermute(part, axis, [(i, (i + step) % 4) for i in range(4)])]
    pallas_call x3 -> x5, Pallas kernels: 4.23 us -> 14.7 us  [the longest x1 7.7 us: project(): pl.pallas_call(project_kernel, grid_spec=pltpu.PrefetchScalarGridSpec(num...]
    all_to_all x5 -> x6, starting transfers between devices: 25.4 us -> 31.2 us  [swap(): return lax.all_to_all(array, axis, 0, 0, tiled=True)]
    all_to_all x5 -> x6, waiting for transfers between devices: 34.6 us -> 31 us  [swap(): return lax.all_to_all(array, axis, 0, 0, tiled=True)]
    dot_general x2 -> x1, matrix products: 3.89 us -> 0.45 us  [tn(): lax.dot_general(left, right, (((0,), (0,)), ((), ())), preferred_element_...]
    pallas_call x1, Pallas kernels: 5.31 us -> 8.24 us  [attend_forward(): pl.pallas_call(forward_kernel, grid=(KV_HEADS,), in_specs=[heads_of(TOKEN...]
    ppermute x6 -> x4, starting transfers between devices: 19.1 us -> 16.5 us  [the longest x3 14.1 us: from_others(): lax.ppermute(part, axis, [(i, (i + step) % 4) for i in range(4)])]
  transfers between devices with their start and end apart: 12 -> 10, of which waited for: 7 -> 6; matrix products, arithmetic and copies ran while one was open for 7% -> 4% of each run, Pallas kernels for 5% -> 12%
where the time goes in v3:
time: 192 us; the launch traced here: 191 us
  starting transfers between devices  47.7 us (25%)
  waiting for transfers between devices  47.1 us (25%)
  blocking collectives  45.2 us (24%)
  Pallas kernels  31.5 us (16%)
  local copies, waits for them, and re-layouts  11.5 us (6%)
  matrix products  5.1 us (3%)
    all_to_all x2, blocking collectives, swap(): return lax.all_to_all(array, axis, 0, 0, tiled=True)  45.2 us
    all_to_all x6, starting transfers between devices, swap(): return lax.all_to_all(array, axis, 0, 0, tiled=True)  31.2 us
    all_to_all x6, waiting for transfers between devices, swap(): return lax.all_to_all(array, axis, 0, 0, tiled=True)  31 us
    ppermute x3, waiting for transfers between devices, from_others(): lax.ppermute(part, axis, [(i, (i + step) % 4) for i in range(4)])  16 us
    ppermute x3, starting transfers between devices, from_others(): lax.ppermute(part, axis, [(i, (i + step) % 4) for i in range(4)])  14.1 us
    pallas_call x1, Pallas kernels, attend_forward(): pl.pallas_call(forward_kernel, grid=(KV_HEADS,), in_specs=[heads_of(TOKEN...  8.24 us
    pallas_call x1, Pallas kernels, project(): pl.pallas_call(project_kernel, grid_spec=pltpu.PrefetchScalarGridSpec(num...  7.7 us
    unnamed x47, local copies, waits for them, and re-layouts  7.1 us
  transfers between devices with their start and end apart: 10, of which 6 were waited for; matrix products, arithmetic and copies ran while one was open for 4% of the time, Pallas kernels for 12%

profile of v3, /device:TPU:1, one launch (start us, length us, event | category | flops | bytes accessed | tf_op | source)
XLA Modules:
  0.0 190.5 jit_solution(13571610302219275527)
XLA Ops:
  2.3 28.7 %all_to_all.40 = bf16[4,208,128]{2,1,0:T(8,128)(2,1)S(1)} all-to-all(bf16[4,208,128]{2,1,0:T(8,128)(2,1)S(1)} %broadcast_in_dim.18), channel_id=1, replica_groups=mesh['x'=4,'zl'=4,'y'=4,'zh'=4,'c'=2] {'zh'}, dimensions={0} | all-to-all | bytes 425984 | tf_op jit(solution)/shard_map/all_to_all | solution.py:31
  31.0 0.9 broadcast_in_dim.19
  31.9 9.7 %all-to-all-start.1 = ((bf16[8,4,80,128]{3,2,1,0:T(8,128)(2,1)}), bf16[8,4,80,128]{3,2,1,0:T(8,128)(2,1)S(1)}, u32[]{:S(2)}, u32[]{:S(2)}) async-start(bf16[8,4,80,128]{3,2,1,0:T(8,128)(2,1)} %broadcast_in_dim.19), calls=%async_computation.1 | async-start | bytes 1310720 | tf_op jit(solution)/shard_map/all_to_all | solution.py:31
  41.6 10.9 %all-to-all-done.1 = bf16[8,4,80,128]{3,2,1,0:T(8,128)(2,1)S(1)} async-done(((bf16[8,4,80,128]{3,2,1,0:T(8,128)(2,1)}), bf16[8,4,80,128]{3,2,1,0:T(8,128)(2,1)S(1)}, u32[]{:S(2)}, u32[]{:S(2)}) %all-to-all-start.1) | async-done | bytes 655392 | tf_op jit(solution)/shard_map/all_to_all | solution.py:31
  52.5 1.9 broadcast_in_dim.42
  54.4 4.9 %all-to-all-start.2 = ((bf16[16,4,128,128]{3,2,1,0:T(8,128)(2,1)}), bf16[16,4,128,128]{3,2,1,0:T(8,128)(2,1)}, u32[]{:S(2)}, u32[]{:S(2)}) async-start(bf16[16,4,128,128]{3,2,1,0:T(8,128)(2,1)} %broadcast_in_dim.42), calls=%async_computation.2 | async-start | bytes 4194304 | tf_op jit(solution)/shard_map/all_to_all | solution.py:31
  60.2 4.9 %collective-permute-start = (bf16[16,4096]{1,0:T(8,128)(2,1)S(1)}, bf16[16,4096]{1,0:T(8,128)(2,1)S(1)}, u32[]{:S(2)}, u32[]{:S(2)}) collective-permute-start(bf16[16,4096]{1,0:T(8,128)(2,1)S(1)} %copy-done.4), channel_id=1, source_target_pairs={{0,2},{2,4},{4,6},{6,0},{1,3},{3,5},{5,7},{7,1},{8,10},{10,12},{12... | collective-permute-start | bytes 393224 | tf_op jit(solution)/shard_map/ppermute | solution.py:480
  65.1 4.5 %collective-permute-start.1 = (bf16[16,4096]{1,0:T(8,128)(2,1)S(1)}, bf16[16,4096]{1,0:T(8,128)(2,1)S(1)}, u32[]{:S(2)}, u32[]{:S(2)}) collective-permute-start(bf16[16,4096]{1,0:T(8,128)(2,1)S(1)} %copy-done.4), channel_id=1, source_target_pairs={{0,4},{2,6},{4,0},{6,2},{1,5},{3,7},{5,1},{7,3},{8,12},{10,14},{12... | collective-permute-start | bytes 393224 | tf_op jit(solution)/shard_map/ppermute | solution.py:480
  69.6 4.7 %collective-permute-start.2 = (bf16[16,4096]{1,0:T(8,128)(2,1)S(1)}, bf16[16,4096]{1,0:T(8,128)(2,1)S(1)}, u32[]{:S(2)}, u32[]{:S(2)}) collective-permute-start(bf16[16,4096]{1,0:T(8,128)(2,1)S(1)} %copy-done.4), channel_id=1, source_target_pairs={{0,6},{2,0},{4,2},{6,4},{1,7},{3,1},{5,3},{7,5},{8,14},{10,8},{12,... | collective-permute-start | bytes 393224 | tf_op jit(solution)/shard_map/ppermute | solution.py:480
  75.1 8.2 %attend_forward.1 = (bf16[8,256,128]{2,1,0:T(8,128)(2,1)}, bf16[128,512]{1,0:T(8,128)(2,1)}, bf16[16,128]{1,0:T(8,128)(2,1)}, bf16[128,16]{1,0:T(8,128)(2,1)}, b...) custom-call(bf16[128,4096]{1,0:T(8,128)(2,1)} %q_ref.3, bf16[128,4096]{1,0:T(8,128)(2,1)} %cot_ref.3, ...), custom_call_target="tpu_custom_call" | custom-call | flops 2000000000 | bytes 5242880 | tf_op jit(solution)/shard_map/attend_forward/pallas_call | solution.py:329
  83.3 1.0 collective-permute-done.1.prompt2_ref
  84.4 15.0 %collective-permute-done.2.prompt3_ref = bf16[16,4096]{1,0:T(8,128)(2,1)S(1)} collective-permute-done((bf16[16,4096]{1,0:T(8,128)(2,1)S(1)}, bf16[16,4096]{1,0:T(8,128)(2,1)S(1)}, u32[]{:S(2)}, u32[]{:S(2)}) %collective-permute-start.2) | collective-permute-done | bytes 131104 | tf_op jit(solution)/shard_map/ppermute | solution.py:480
  99.4 2.4 %collective-permute-start.3 = (bf16[4,4,4,128,128]{4,3,2,1,0:T(8,128)(2,1)}, bf16[4,4,4,128,128]{4,3,2,1,0:T(8,128)(2,1)S(1)}, u32[]{:S(2)}, u32[]{:S(2)}) collective-permute-start(bf16[4,4,4,128,128]{4,3,2,1,0:T(8,128)(2,1)} %bitcast.11.weight_ref), channel_id=1, source_target_pairs={{0,1},{1,0},{2,3},{3,2},{4,5},{5,4},{6,7},{7,6},{8,9},{9,8},{10,11... | collective-permute-start | bytes 6291464 | tf_op jit(solution)/shard_map/ppermute | solution.py:524
  101.8 4.5 %all-to-all-start.4 = ((bf16[8,256,128]{2,1,0:T(8,128)(2,1)}), bf16[8,256,128]{2,1,0:T(8,128)(2,1)S(1)}, u32[]{:S(2)}, u32[]{:S(2)}) async-start(bf16[8,256,128]{2,1,0:T(8,128)(2,1)} %get-tuple-element.38), calls=%async_computation.4 | async-start | bytes 1048576 | tf_op jit(solution)/shard_map/all_to_all | solution.py:31
  107.0 1.4 copy-done.18
  108.4 7.7 %project.1 = (bf16[128,512]{1,0:T(8,128)(2,1)}, bf16[8,256,128]{2,1,0:T(8,128)(2,1)}, bf16[4096,512]{1,0:T(8,128)(2,1)}) custom-call(s32[4]{0:T(128)} %pad_add_fusion.place_ref, bf16[128,4096]{1,0:T(8,128)(2,1)} %x_ref.5, bf16[16,4096]{1,0:T(8,128)(2,1)} %prompt_ref.3, bf16[16,4096]{1,0:T(8,128)(2,1)} %copy-done.6, bf16[16,4096]{1,0:T(8,128)(2,1)} %copy-done.8, ...), custom_call_target="tpu_custom_call" | custom-call | flops 600000000 | bytes 10485760 | tf_op jit(solution)/shard_map/project/pallas_call | solution.py:396
  116.2 4.8 %all-to-all-start.3 = ((bf16[8,256,128]{2,1,0:T(8,128)(2,1)}), bf16[8,256,128]{2,1,0:T(8,128)(2,1)S(1)}, u32[]{:S(2)}, u32[]{:S(2)}) async-start(bf16[8,256,128]{2,1,0:T(8,128)(2,1)} %get-tuple-element.35), calls=%async_computation.3 | async-start | bytes 1048576 | tf_op jit(solution)/shard_map/all_to_all | solution.py:31
  121.0 0.9 copy-done.7
  121.9 0.9 copy-done.9
  122.8 0.9 copy-done.11
  123.7 1.6 adapter_terms.1
  126.0 4.4 %all-to-all-done.3.value_ref = bf16[8,256,128]{2,1,0:T(8,128)(2,1)S(1)} async-done(((bf16[8,256,128]{2,1,0:T(8,128)(2,1)}), bf16[8,256,128]{2,1,0:T(8,128)(2,1)S(1)}, u32[]{:S(2)}, u32[]{:S(2)}) %all-to-all-start.3) | async-done | bytes 524320 | tf_op jit(solution)/shard_map/all_to_all | solution.py:31
  130.4 0.8 copy-done.20
  131.3 7.0 %attend_backward.1 = (bf16[8,384,128]{2,1,0:T(8,128)(2,1)}, bf16[128,512]{1,0:T(8,128)(2,1)}) custom-call(bf16[128,4096]{1,0:T(8,128)(2,1)} %q_ref.3, bf16[128,4096]{1,0:T(8,128)(2,1)} %cot_ref.3, f32[4,256,1024]{2,1,0:T(8,128)} %get-tuple-element.29.softmax_ref, bf16[8,256,128]{2,1,0:T(8,128)(2,1)} %copy-done.20, ...), custom_call_target="tpu_custom_call" | custom-call | flops 3000000000 | bytes 9437184 | tf_op jit(solution)/shard_map/attend_backward/pallas_call | solution.py:447
  138.3 16.5 %all_to_all.41.got_ref = bf16[8,384,128]{2,1,0:T(8,128)(2,1)S(1)} all-to-all(bf16[8,384,128]{2,1,0:T(8,128)(2,1)} %get-tuple-element.41), channel_id=1, replica_groups=mesh['x'=4,'zl'=4,'y'=4,'zh'=4,'c'=2] {'y','c'}, dimensions={0} | all-to-all | bytes 1572864 | tf_op jit(solution)/shard_map/all_to_all | solution.py:31
  154.8 0.8 keys_y.1
  155.6 3.4 %all-to-all-start.6 = ((bf16[4,208,128]{2,1,0:T(8,128)(2,1)}), bf16[4,208,128]{2,1,0:T(8,128)(2,1)S(1)}, u32[]{:S(2)}, u32[]{:S(2)}) async-start(bf16[4,208,128]{2,1,0:T(8,128)(2,1)} %keys_y.1), calls=%async_computation.6 | async-start | bytes 425984 | tf_op jit(solution)/shard_map/all_to_all | solution.py:31
  159.4 4.7 %fusion = bf16[128,4096]{1,0:T(8,128)(2,1)} fusion(f32[128,4096]{1,0:T(8,128)S(1)} %convolution_multiply_fusion, bf16[128,512]{1,0:T(8,128)(2,1)S(1)} %copy-done.3, bf16[4096,512]{1,0:T(8,128)(2,1)} %get-tuple-element.43.weight_ref), kind=kOutput, calls=%fused_computation.2 | convolution fusion | flops 537919488 | bytes 7471104 | tf_op jit(solution)/shard_map/dot_general | solution.py:40
  164.1 9.5 %all-to-all-done.6.got_ref = bf16[4,208,128]{2,1,0:T(8,128)(2,1)S(1)} async-done(((bf16[4,208,128]{2,1,0:T(8,128)(2,1)}), bf16[4,208,128]{2,1,0:T(8,128)(2,1)S(1)}, u32[]{:S(2)}, u32[]{:S(2)}) %all-to-all-start.6) | async-done | bytes 213024 | tf_op jit(solution)/shard_map/all_to_all | solution.py:31
  175.0 3.9 %all-to-all-start.7 = ((bf16[16,80,128]{2,1,0:T(8,128)(2,1)}), bf16[16,80,128]{2,1,0:T(8,128)(2,1)S(1)}, u32[]{:S(2)}, u32[]{:S(2)}) async-start(bf16[16,80,128]{2,1,0:T(8,128)(2,1)} %get-tuple-element.49), calls=%async_computation.7 | async-start | bytes 655360 | tf_op jit(solution)/shard_map/all_to_all | solution.py:31
  178.9 4.8 %prompt_gradient.1 = bf16[16,4096]{1,0:T(8,128)(2,1)} custom-call(bf16[16,512]{1,0:T(8,128)(2,1)} %copy-done.14, bf16[16,512]{1,0:T(8,128)(2,1)} %up_ref.7, bf16[16,4096]{1,0:T(8,128)(2,1)} %get-tuple-element.34.down_ref, bf16[4096,512]{1,0:T(8,128)(2,1)} %get-tuple-element.43.weight_ref), custom_call_target="tpu_custom_call" | custom-call | tf_op jit(solution)/shard_map/prompt_gradient/pallas_call | solution.py:429
  183.7 6.2 %all-to-all-done.7.got_ref = bf16[16,80,128]{2,1,0:T(8,128)(2,1)S(1)} async-done(((bf16[16,80,128]{2,1,0:T(8,128)(2,1)}), bf16[16,80,128]{2,1,0:T(8,128)(2,1)S(1)}, u32[]{:S(2)}, u32[]{:S(2)}) %all-to-all-start.7) | async-done | bytes 327712 | tf_op jit(solution)/shard_map/all_to_all | solution.py:31
  (61 shorter events, 7.2 us)
Async XLA Ops:
  0.6 0.9 copy-start
  31.9 20.6 %all-to-all-start.1 = ((bf16[8,4,80,128]{3,2,1,0:T(8,128)(2,1)}), bf16[8,4,80,128]{3,2,1,0:T(8,128)(2,1)S(1)}, u32[]{:S(2)}, u32[]{:S(2)}) async-start(bf16[8,4,80,128]{3,2,1,0:T(8,128)(2,1)} %broadcast_in_dim.19), calls=%async_computation.1 | async-start | bytes 1310720 | tf_op jit(solution)/shard_map/all_to_all | solution.py:31
  52.5 1.9 copy-start.19
  54.3 4.9 %copy-start.21 = (s32[1,128]{1,0:T(1,128)S(1)}, s32[1,128]{1,0:T(1,128)}, u32[]{:S(2)}) copy-start(s32[1,128]{1,0:T(1,128)} %param.17) | copy-start | bytes 1540
  54.3 5.8 %copy-start.22 = (s32[1,8]{1,0:T(1,128)S(1)}, s32[1,8]{1,0:T(1,128)}, u32[]{:S(2)}) copy-start(s32[1,8]{1,0:T(1,128)} %param.18) | copy-start | bytes 100
  54.3 5.9 %copy-start.4 = (bf16[16,4096]{1,0:T(8,128)(2,1)S(1)}, bf16[16,4096]{1,0:T(8,128)(2,1)}, u32[]{:S(2)}) copy-start(bf16[16,4096]{1,0:T(8,128)(2,1)} %prompt_ref.3) | copy-start | bytes 393220
  54.4 45.0 %all-to-all-start.2 = ((bf16[16,4,128,128]{3,2,1,0:T(8,128)(2,1)}), bf16[16,4,128,128]{3,2,1,0:T(8,128)(2,1)}, u32[]{:S(2)}, u32[]{:S(2)}) async-start(bf16[16,4,128,128]{3,2,1,0:T(8,128)(2,1)} %broadcast_in_dim.42), calls=%async_computation.2 | async-start | bytes 4194304 | tf_op jit(solution)/shard_map/all_to_all | solution.py:31
  60.2 23.1 %collective-permute-start = (bf16[16,4096]{1,0:T(8,128)(2,1)S(1)}, bf16[16,4096]{1,0:T(8,128)(2,1)S(1)}, u32[]{:S(2)}, u32[]{:S(2)}) collective-permute-start(bf16[16,4096]{1,0:T(8,128)(2,1)S(1)} %copy-done.4), channel_id=1, source_target_pairs={{0,2},{2,4},{4,6},{6,0},{1,3},{3,5},{5,7},{7,1},{8,10},{10,12},{12... | collective-permute-start | bytes 393224 | tf_op jit(solution)/shard_map/ppermute | solution.py:480
  65.1 19.3 %collective-permute-start.1 = (bf16[16,4096]{1,0:T(8,128)(2,1)S(1)}, bf16[16,4096]{1,0:T(8,128)(2,1)S(1)}, u32[]{:S(2)}, u32[]{:S(2)}) collective-permute-start(bf16[16,4096]{1,0:T(8,128)(2,1)S(1)} %copy-done.4), channel_id=1, source_target_pairs={{0,4},{2,6},{4,0},{6,2},{1,5},{3,7},{5,1},{7,3},{8,12},{10,14},{12... | collective-permute-start | bytes 393224 | tf_op jit(solution)/shard_map/ppermute | solution.py:480
  69.6 29.8 %collective-permute-start.2 = (bf16[16,4096]{1,0:T(8,128)(2,1)S(1)}, bf16[16,4096]{1,0:T(8,128)(2,1)S(1)}, u32[]{:S(2)}, u32[]{:S(2)}) collective-permute-start(bf16[16,4096]{1,0:T(8,128)(2,1)S(1)} %copy-done.4), channel_id=1, source_target_pairs={{0,6},{2,0},{4,2},{6,4},{1,7},{3,1},{5,3},{7,5},{8,14},{10,8},{12,... | collective-permute-start | bytes 393224 | tf_op jit(solution)/shard_map/ppermute | solution.py:480
  83.3 25.0 %copy-start.6 = (bf16[16,4096]{1,0:T(8,128)(2,1)}, bf16[16,4096]{1,0:T(8,128)(2,1)S(1)}, u32[]{:S(2)}) copy-start(bf16[16,4096]{1,0:T(8,128)(2,1)S(1)} %collective-permute-done.prompt1_ref) | copy-start | bytes 393220
  84.4 24.0 %copy-start.8 = (bf16[16,4096]{1,0:T(8,128)(2,1)}, bf16[16,4096]{1,0:T(8,128)(2,1)S(1)}, u32[]{:S(2)}) copy-start(bf16[16,4096]{1,0:T(8,128)(2,1)S(1)} %collective-permute-done.1.prompt2_ref) | copy-start | bytes 393220
  99.4 9.0 %copy-start.10 = (bf16[16,4096]{1,0:T(8,128)(2,1)}, bf16[16,4096]{1,0:T(8,128)(2,1)S(1)}, u32[]{:S(2)}) copy-start(bf16[16,4096]{1,0:T(8,128)(2,1)S(1)} %collective-permute-done.2.prompt3_ref) | copy-start | bytes 393220
  99.4 7.6 %collective-permute-start.3 = (bf16[4,4,4,128,128]{4,3,2,1,0:T(8,128)(2,1)}, bf16[4,4,4,128,128]{4,3,2,1,0:T(8,128)(2,1)S(1)}, u32[]{:S(2)}, u32[]{:S(2)}) collective-permute-start(bf16[4,4,4,128,128]{4,3,2,1,0:T(8,128)(2,1)} %bitcast.11.weight_ref), channel_id=1, source_target_pairs={{0,1},{1,0},{2,3},{3,2},{4,5},{5,4},{6,7},{7,6},{8,9},{9,8},{10,11... | collective-permute-start | bytes 6291464 | tf_op jit(solution)/shard_map/ppermute | solution.py:524
  101.8 14.3 %all-to-all-start.4 = ((bf16[8,256,128]{2,1,0:T(8,128)(2,1)}), bf16[8,256,128]{2,1,0:T(8,128)(2,1)S(1)}, u32[]{:S(2)}, u32[]{:S(2)}) async-start(bf16[8,256,128]{2,1,0:T(8,128)(2,1)} %get-tuple-element.38), calls=%async_computation.4 | async-start | bytes 1048576 | tf_op jit(solution)/shard_map/all_to_all | solution.py:31
  106.9 1.4 copy-start.18
  108.3 12.6 %copy-start.1 = (bf16[128,4096]{1,0:T(8,128)(2,1)S(1)}, bf16[128,4096]{1,0:T(8,128)(2,1)}, u32[]{:S(2)}) copy-start(bf16[128,4096]{1,0:T(8,128)(2,1)} %x_ref.5) | copy-start | bytes 3145732
  108.4 12.6 %copy-start.2 = (bf16[16,4096]{1,0:T(8,128)(2,1)S(1)}, bf16[16,4096]{1,0:T(8,128)(2,1)}, u32[]{:S(2)}) copy-start(bf16[16,4096]{1,0:T(8,128)(2,1)} %get-tuple-element.34.down_ref) | copy-start | bytes 393220
  108.4 12.6 %copy-start.3 = (bf16[128,512]{1,0:T(8,128)(2,1)S(1)}, bf16[128,512]{1,0:T(8,128)(2,1)}, u32[]{:S(2)}) copy-start(bf16[128,512]{1,0:T(8,128)(2,1)} %get-tuple-element.32.low_ref) | copy-start | bytes 393220
  108.4 12.6 %copy-start.5 = (bf16[16,4096]{1,0:T(8,128)(2,1)S(1)}, bf16[16,4096]{1,0:T(8,128)(2,1)}, u32[]{:S(2)}) copy-start(bf16[16,4096]{1,0:T(8,128)(2,1)} %prompt_ref.3) | copy-start | bytes 393220
  108.4 12.6 %copy-start.12 = (bf16[16,512]{1,0:T(8,128)(2,1)S(1)}, bf16[16,512]{1,0:T(8,128)(2,1)}, u32[]{:S(2)}) copy-start(bf16[16,512]{1,0:T(8,128)(2,1)} %up_ref.7) | copy-start | bytes 49156
  108.4 12.6 %copy-start.13 = (bf16[128,16]{1,0:T(8,128)(2,1)S(1)}, bf16[128,16]{1,0:T(8,128)(2,1)}, u32[]{:S(2)}) copy-start(bf16[128,16]{1,0:T(8,128)(2,1)} %get-tuple-element.39.first_ref) | copy-start | bytes 12292
  108.4 12.6 %copy-start.15 = (bf16[16,128]{1,0:T(8,128)(2,1)S(1)}, bf16[16,128]{1,0:T(8,128)(2,1)}, u32[]{:S(2)}) copy-start(bf16[16,128]{1,0:T(8,128)(2,1)} %get-tuple-element.37.back_ref) | copy-start | bytes 12292
  108.4 12.6 %copy-start.16 = (s32[4]{0:T(128)S(1)}, s32[4]{0:T(128)}, u32[]{:S(2)}) copy-start(s32[4]{0:T(128)} %pad_add_fusion.place_ref) | copy-start | bytes 52
  116.2 14.3 %all-to-all-start.3 = ((bf16[8,256,128]{2,1,0:T(8,128)(2,1)}), bf16[8,256,128]{2,1,0:T(8,128)(2,1)S(1)}, u32[]{:S(2)}, u32[]{:S(2)}) async-start(bf16[8,256,128]{2,1,0:T(8,128)(2,1)} %get-tuple-element.35), calls=%async_computation.3 | async-start | bytes 1048576 | tf_op jit(solution)/shard_map/all_to_all | solution.py:31
  121.0 0.9 copy-start.7
  121.9 0.9 copy-start.9
  122.8 0.9 copy-start.11
  125.3 0.7 copy-start.17
  130.4 0.8 copy-start.20
  155.6 18.0 %all-to-all-start.6 = ((bf16[4,208,128]{2,1,0:T(8,128)(2,1)}), bf16[4,208,128]{2,1,0:T(8,128)(2,1)S(1)}, u32[]{:S(2)}, u32[]{:S(2)}) async-start(bf16[4,208,128]{2,1,0:T(8,128)(2,1)} %keys_y.1), calls=%async_computation.6 | async-start | bytes 425984 | tf_op jit(solution)/shard_map/all_to_all | solution.py:31
  175.0 14.9 %all-to-all-start.7 = ((bf16[16,80,128]{2,1,0:T(8,128)(2,1)}), bf16[16,80,128]{2,1,0:T(8,128)(2,1)S(1)}, u32[]{:S(2)}, u32[]{:S(2)}) async-start(bf16[16,80,128]{2,1,0:T(8,128)(2,1)} %get-tuple-element.49), calls=%async_computation.7 | async-start | bytes 655360 | tf_op jit(solution)/shard_map/all_to_all | solution.py:31
  (1 other events, 0.6 us)

commit v4 on v3

--- a/solution.py
+++ b/solution.py
@@ -109,9 +109,9 @@
 
 
 def forward_kernel(
-    q_ref, cot_ref, key_ref, down_ref, own_key_ref, chosen_ref, bias_ref, x_ref, up_ref,
-    send_ref, low_ref, back_ref, first_ref, down_out_ref, softmax_ref,
-    probs, own_probs, cots, back,
+    q_ref, cot_ref, key_ref, own_key_ref, chosen_ref, bias_ref, x_ref, up_ref, down_ref,
+    send_ref, low_ref, back_ref, grad_ref, second_ref, softmax_ref,
+    probs, own_probs, cots, back, first,
 ):
     k = pl.program_id(0)
     key_cat = prompt_block(key_ref)
@@ -136,15 +136,15 @@
     @pl.when(k == 0)
     def _():
         back[...] = jnp.zeros_like(back)
-        for at, y, zh, c in BLOCKS:
-            down_out_ref[:, at : at + 128] = down_ref[y, c, zh]
-        first_ref[...] = nt(x_ref[...], down_out_ref[...]).astype(BF16)
+        first[...] = nt(x_ref[...], down_ref[...]).astype(BF16)
 
     back[...] += nt(up_ref[...], low)
+    second_ref[...] = tn(first[...], low)
 
     @pl.when(k == KV_HEADS - 1)
     def _():
         back_ref[...] = back[...].astype(BF16)
+        grad_ref[...] = nn(back_ref[...], x_ref[...])
 
 
 def place_before(place, step):
@@ -152,7 +152,7 @@
 
 
 def adapter_kernel(
-    place_ref, low_ref, back_ref, got_ref, first_ref, up_ref, down_ref, x_ref,
+    place_ref, keys_ref, got_ref, grad_ref, second_ref, up_ref, down_ref,
     prompt_ref, prompt1_ref, prompt2_ref, prompt3_ref,
     part_ref, send_ref,
     total,
@@ -161,7 +161,6 @@
     for zh in range(4):
         part_ref[zh] = total[zh * 64 : (zh + 1) * 64, :]
     up = up_ref[...]
-    first = first_ref[...]
     prompts = jnp.concatenate(
         [prompt_ref[...], prompt1_ref[...], prompt2_ref[...], prompt3_ref[...]], axis=0
     )
@@ -174,19 +173,20 @@
             [total[pl.ds(pl.multiple_of(row, 16), 16), :] for row in starts], axis=0
         )
         prompt_back = prompt_back + nt(up[:, at], low)
-        second = tn(first, low_ref[:, at]) + tn(prompt_first, low)
-        send_ref[512 + k * 16 : 512 + (k + 1) * 16, :] = second.astype(BF16)
-    grad = nn(back_ref[...], x_ref[...]) + nn(prompt_back.astype(BF16), prompts)
-    grad = grad.astype(BF16)
+        second = (second_ref[:, at] + tn(prompt_first, low)).astype(BF16)
+        for owner in range(8):
+            send_ref[owner, 320 + k * 16 : 320 + (k + 1) * 16, :] = second
+    grad = (grad_ref[...] + nn(prompt_back.astype(BF16), prompts)).astype(BF16)
     for at, y, zh, c in BLOCKS:
-        row = ((y * 2 + c) * 4 + zh) * 16
-        send_ref[row : row + 16, :] = grad[:, at : at + 128]
+        row = 256 + zh * 16
+        send_ref[y * 2 + c, row : row + 16, :] = grad[:, at : at + 128]
+    send_ref[:, :256, :] = keys_ref[...]
 
 
 def project_kernel(
     place_ref, x_ref, prompt_ref, prompt1_ref, prompt2_ref, prompt3_ref,
-    weight_ref, other_ref, down_ref, up_ref,
-    values_ref, send_ref, weight_out_ref,
+    weight_ref, other_ref, up_ref,
+    values_ref, send_ref, weight_out_ref, down_ref,
     rows, first,
 ):
     k = pl.program_id(0)
@@ -196,13 +196,18 @@
         rows[:TOKENS, :] = x_ref[...]
         for step, ref in enumerate((prompt_ref, prompt1_ref, prompt2_ref, prompt3_ref)):
             rows[TOKENS + step * 16 : TOKENS + (step + 1) * 16, :] = ref[...]
+        for y in range(4):
+            for zh in range(4):
+                for ref, c in ((weight_ref, place_ref[3]), (other_ref, 1 - place_ref[3])):
+                    at = pl.multiple_of(((y * 4 + zh) * 2 + c) * 128, 128)
+                    down_ref[:, pl.ds(at, 128)] = ref[0, y, zh, 128:, :]
         first[...] = nt(rows[...], down_ref[...]).astype(BF16)
 
     for y in range(4):
         for zh in range(4):
             for ref, c in ((weight_ref, place_ref[3]), (other_ref, 1 - place_ref[3])):
                 row = pl.multiple_of(((y * 4 + zh) * 2 + c) * 128, 128)
-                weight_out_ref[pl.ds(row, 128), :] = ref[0, y, zh]
+                weight_out_ref[pl.ds(row, 128), :] = ref[0, y, zh, :128, :]
     values = nn(rows[...], weight_out_ref[...]) + ADAPTER_SCALE * nn(first[...], up_ref[...])
     values = values.astype(BF16)
     values_ref[...] = values[:TOKENS]
@@ -274,18 +279,11 @@
 
 
 def backward_kernel(
-    q_ref, cot_ref, softmax_ref, value_ref, own_value_ref, chosen_ref, adapter_ref,
+    q_ref, cot_ref, softmax_ref, value_ref, own_value_ref, chosen_ref,
     send_ref, own_ref,
     grads, own_grads, queries,
 ):
     k = pl.program_id(0)
-
-    @pl.when(k == 0)
-    def _():
-        for owner in range(8):
-            send_ref[owner, 256:320, :] = adapter_ref[owner * 64 : (owner + 1) * 64, :]
-            send_ref[owner, 320:, :] = adapter_ref[512:, :]
-
     value_cat = value_block(value_ref, k)
     own_value = own_value_ref[...]
     chosen = chosen_ref[...]
@@ -321,11 +319,10 @@
 ROWS = GROUP_SIZE * TOKENS
 
 
-DOWN_SPEC = pl.BlockSpec((4, 2, 4, 16, HEAD_DIM), lambda k: (0, 0, 0, KV_HEADS, 0))
 PARAMS = pltpu.CompilerParams(vmem_limit_bytes=56 << 20, dimension_semantics=("arbitrary",))
 
 
-def attend_forward(queries, cotangent, keys, own_keys, chosen, bias, rows, up):
+def attend_forward(queries, cotangent, keys, own_keys, chosen, bias, rows, up, down):
     return pl.pallas_call(
         forward_kernel,
         grid=(KV_HEADS,),
@@ -333,27 +330,27 @@
             heads_of(TOKENS, WIDE),
             heads_of(TOKENS, WIDE),
             PROMPT_SPEC,
-            DOWN_SPEC,
             heads_of(TOKENS, HEAD_DIM),
             whole((PAIR, HEAD_DIM)),
             whole((TOKENS, PAIR)),
             whole((TOKENS, D)),
             heads_of(RANK, HEAD_DIM),
+            whole((RANK, D)),
         ],
         out_specs=[
             whole((8, 256, HEAD_DIM)),
             heads_of(TOKENS, HEAD_DIM),
             whole((RANK, TOKENS)),
-            whole((TOKENS, RANK)),
             whole((RANK, D)),
+            heads_of(RANK, HEAD_DIM),
             pl.BlockSpec((1, 2 * TOKENS, ROWS), lambda k: (k, 0, 0)),
         ],
         out_shape=[
             sent(8, 256, HEAD_DIM),
             sent(TOKENS, KV_HEADS * HEAD_DIM),
             sent(RANK, TOKENS),
-            sent(TOKENS, RANK),
-            sent(RANK, D),
+            jax.ShapeDtypeStruct((RANK, D), F32),
+            jax.ShapeDtypeStruct((RANK, KV_HEADS * HEAD_DIM), F32),
             jax.ShapeDtypeStruct((KV_HEADS, 2 * TOKENS, ROWS), F32),
         ],
         scratch_shapes=[
@@ -361,29 +358,30 @@
             pltpu.VMEM((TOKENS, ROWS), BF16),
             pltpu.VMEM((ROWS, (PROMPTS + 1) * HEAD_DIM), BF16),
             pltpu.VMEM((RANK, TOKENS), F32),
+            pltpu.VMEM((TOKENS, RANK), BF16),
         ],
         compiler_params=PARAMS,
         cost_estimate=pl.CostEstimate(
             flops=2_000_000_000, bytes_accessed=5 << 20, transcendentals=1 << 20
         ),
         name="attend_forward",
-    )(queries, cotangent, keys, keys, own_keys, chosen, bias, rows, up)
-
-
-def adapter_terms(place, low, back, got, first, up, down, rows, prompts):
+    )(queries, cotangent, keys, own_keys, chosen, bias, rows, up, down)
+
+
+def adapter_terms(place, keys, got, grad, second, up, down, prompts):
     vmem = pl.BlockSpec(memory_space=pltpu.VMEM)
     return pl.pallas_call(
         adapter_kernel,
-        in_specs=[pl.BlockSpec(memory_space=pltpu.SMEM)] + [vmem] * 11,
+        in_specs=[pl.BlockSpec(memory_space=pltpu.SMEM)] + [vmem] * 10,
         out_specs=[vmem] * 2,
-        out_shape=[sent(4, 64, HEAD_DIM), sent(576, HEAD_DIM)],
+        out_shape=[sent(4, 64, HEAD_DIM), sent(8, 384, HEAD_DIM)],
         scratch_shapes=[pltpu.VMEM((256, HEAD_DIM), BF16)],
         compiler_params=pltpu.CompilerParams(vmem_limit_bytes=24 << 20),
         name="adapter_terms",
-    )(place, low, back, got, first, up, down, rows, *prompts)
-
-
-def project(place, rows, prompts, weight, other, down, up):
+    )(place, keys, got, grad, second, up, down, *prompts)
+
+
+def project(place, rows, prompts, weight, other, up):
     width = KV_HEADS * HEAD_DIM
 
     def const(*shape):
@@ -392,7 +390,7 @@
     def head(rows):
         return pl.BlockSpec((rows, HEAD_DIM), lambda k, place: (0, k))
 
-    block = pl.BlockSpec((1, 4, 4, 128, HEAD_DIM), lambda k, place: (k, 0, 0, 0, 0))
+    block = pl.BlockSpec((1, 4, 4, 144, HEAD_DIM), lambda k, place: (k, 0, 0, 0, 0))
     return pl.pallas_call(
         project_kernel,
         grid_spec=pltpu.PrefetchScalarGridSpec(
@@ -406,22 +404,21 @@
                 const(16, D),
                 block,
                 block,
-                const(RANK, D),
                 head(RANK),
             ],
-            out_specs=[head(TOKENS), const(8, 256, HEAD_DIM), head(D)],
+            out_specs=[head(TOKENS), const(8, 256, HEAD_DIM), head(D), const(RANK, D)],
             scratch_shapes=[
                 pltpu.VMEM((TOKENS + 64, D), BF16),
                 pltpu.VMEM((TOKENS + 64, RANK), BF16),
             ],
         ),
-        out_shape=[sent(TOKENS, width), sent(8, 256, HEAD_DIM), sent(D, width)],
+        out_shape=[sent(TOKENS, width), sent(8, 256, HEAD_DIM), sent(D, width), sent(RANK, D)],
         compiler_params=PARAMS,
         cost_estimate=pl.CostEstimate(
             flops=600_000_000, bytes_accessed=10 << 20, transcendentals=0
         ),
         name="project",
-    )(place, rows, *prompts, weight, other, down, up)
+    )(place, rows, *prompts, weight, other, up)
 
 
 def prompt_gradient(low, up, down, weight):
@@ -443,7 +440,7 @@
     )(low, up, down, weight)
 
 
-def attend_backward(queries, cotangent, softmax, values, own_values, chosen, adapter):
+def attend_backward(queries, cotangent, softmax, values, own_values, chosen):
     return pl.pallas_call(
         backward_kernel,
         grid=(KV_HEADS,),
@@ -454,10 +451,9 @@
             whole((8, 256, HEAD_DIM)),
             heads_of(TOKENS, HEAD_DIM),
             whole((PAIR, HEAD_DIM)),
-            whole((576, HEAD_DIM)),
-        ],
-        out_specs=[whole((8, 384, HEAD_DIM)), heads_of(TOKENS, HEAD_DIM)],
-        out_shape=[sent(8, 384, HEAD_DIM), sent(TOKENS, KV_HEADS * HEAD_DIM)],
+        ],
+        out_specs=[whole((8, 256, HEAD_DIM)), heads_of(TOKENS, HEAD_DIM)],
+        out_shape=[sent(8, 256, HEAD_DIM), sent(TOKENS, KV_HEADS * HEAD_DIM)],
         scratch_shapes=[
             pltpu.VMEM((TOKENS, ROWS), BF16),
             pltpu.VMEM((TOKENS, ROWS), BF16),
@@ -468,17 +464,15 @@
             flops=3_000_000_000, bytes_accessed=9 << 20, transcendentals=0
         ),
         name="attend_backward",
-    )(queries, cotangent, softmax, values, own_values, chosen, adapter)
+    )(queries, cotangent, softmax, values, own_values, chosen)
 
 
 def heads_first(rows):
     return rows.reshape(16, KV_HEADS, HEAD_DIM).transpose(1, 0, 2).reshape(KV_HEADS * 16, HEAD_DIM)
 
 
-def from_others(part, axis):
-    return [
-        lax.ppermute(part, axis, [(i, (i + step) % 4) for i in range(4)]) for step in range(1, 4)
-    ]
+def move(part, axis, step):
+    return lax.ppermute(part, axis, [(i, (i + step) % 4) for i in range(4)])
 
 
 def after(array, *others):
@@ -510,27 +504,30 @@
         frozen_value_weight, lax.axis_index("x") * HEAD_DIM, HEAD_DIM, 1
     )
     start = gather(
-        jnp.concatenate([own_columns, heads_first(prompt_keys), value_adapter_down.T], axis=0), "zh"
+        jnp.concatenate([own_columns, value_adapter_down.T, heads_first(prompt_keys)], axis=0), "zh"
     )
     place = jnp.stack([lax.axis_index(axis) for axis in ("x", "y", "zh", "c")]).astype(jnp.int32)
-    key_all = gather(start[:, 128:], OWNERS).reshape(4, 2, 4, 80, HEAD_DIM)
-    weight_part, prompt_part = lax.optimization_barrier((start[:, :128], prompt_rows, key_all))[:2]
-    prompts = [prompt_rows, *from_others(prompt_part, "zh")]
-    weight = gather(weight_part, ("x", "y")).reshape(4, 4, 4, 128, HEAD_DIM)
-
-    send, low, back, first_proj, down, softmax = attend_forward(
-        queries, cotangent, key_all, response_keys, chosen, bias, response_rows, value_adapter_up
-    )
-    other = lax.ppermute(after(weight, low, *prompts), "c", [(0, 1), (1, 0)])
-    value_part, adapter = adapter_terms(
-        place, low, back, swap(send, OWNERS), first_proj, value_adapter_up, down, response_rows,
-        prompts,
-    )
-    values, part, weight = project(
-        place, response_rows, prompts, weight, other, down, value_adapter_up
-    )
+    weight = gather(start[:, :144], ("x", "y")).reshape(4, 4, 4, 144, HEAD_DIM)
+    before, behind = lax.optimization_barrier((prompt_rows, prompt_rows, start))[:2]
+    before, behind = move(before, "zh", 1), move(behind, "zh", 3)
+    prompts = [prompt_rows, before, move(before, "zh", 1), behind]
+    other = lax.ppermute(after(weight, *prompts), "c", [(0, 1), (1, 0)])
+    key_all = gather(after(start[:, 144:], weight), OWNERS).reshape(4, 2, 4, 64, HEAD_DIM)
+
+    values, part, weight, down = project(
+        place, response_rows, prompts, weight, other, value_adapter_up
+    )
+    value_all = swap(after(part, key_all), OWNERS)
+    send, low, back, token_grad, token_second, softmax = attend_forward(
+        queries, cotangent, key_all, response_keys, chosen, bias, response_rows, value_adapter_up,
+        down,
+    )
+    got = swap(after(send, value_all), OWNERS)
     key_send, own_key_grad = attend_backward(
-        queries, cotangent, softmax, swap(part, OWNERS), values, chosen, adapter
+        queries, cotangent, softmax, value_all, values, chosen
+    )
+    value_part, key_send = adapter_terms(
+        place, key_send, got, token_grad, token_second, value_adapter_up, down, prompts
     )
     part = in_vmem(keys_y_kernel, 2, sent(4, 208, HEAD_DIM), "keys_y")(
         swap(key_send, OWNERS), value_part

time: 192 us -> 181 us (0.943)
  waiting for transfers between devices: 47.1 us -> 25.7 us
  starting transfers between devices: 47.7 us -> 61.6 us
  local copies, waits for them, and re-layouts: 11.5 us -> 6.95 us
    all_to_all x6, waiting for transfers between devices: 31 us -> 16.4 us  [swap(): return lax.all_to_all(array, axis, 0, 0, tiled=True)]
    ppermute x4, starting transfers between devices: 16.5 us -> 29.7 us  [the longest x3 16.1 us: move(): return lax.ppermute(part, axis, [(i, (i + step) % 4) for i in range(4)])]
    ppermute x4, waiting for transfers between devices: 16 us -> 9.3 us  [the longest x3 9.3 us: move(): return lax.ppermute(part, axis, [(i, (i + step) % 4) for i in range(4)])]
    unnamed x47 -> x45, local copies, waits for them, and re-layouts: 7.1 us -> 2.54 us
  transfers between devices with their start and end apart: 10 -> 10, of which waited for: 6 -> 7; matrix products, arithmetic and copies ran while one was open for 4% -> 5% of each run, Pallas kernels for 12% -> 16%
where the time goes in v4:
time: 181 us; the launch traced here: 178 us
  starting transfers between devices  61.6 us (34%)
  blocking collectives  44.3 us (24%)
  Pallas kernels  31.7 us (18%)
  waiting for transfers between devices  25.7 us (14%)
  local copies, waits for them, and re-layouts  6.95 us (4%)
  matrix products  5.1 us (3%)
    all_to_all x2, blocking collectives, swap(): return lax.all_to_all(array, axis, 0, 0, tiled=True)  44.3 us
    all_to_all x6, starting transfers between devices, swap(): return lax.all_to_all(array, axis, 0, 0, tiled=True)  31.8 us
    all_to_all x6, waiting for transfers between devices, swap(): return lax.all_to_all(array, axis, 0, 0, tiled=True)  16.4 us
    ppermute x3, starting transfers between devices, move(): return lax.ppermute(part, axis, [(i, (i + step) % 4) for i in range(4)])  16.1 us
    ppermute x1, starting transfers between devices, on_device(): other = lax.ppermute(after(weight, *prompts), 'c', [(0, 1), (1, 0)])  13.7 us
    ppermute x3, waiting for transfers between devices, move(): return lax.ppermute(part, axis, [(i, (i + step) % 4) for i in range(4)])  9.3 us
    pallas_call x1, Pallas kernels, attend_forward(): pl.pallas_call(forward_kernel, grid=(KV_HEADS,), in_specs=[heads_of(TOKEN...  8.67 us
    pallas_call x1, Pallas kernels, project(): pl.pallas_call(project_kernel, grid_spec=pltpu.PrefetchScalarGridSpec(num...  7.68 us
  transfers between devices with their start and end apart: 10, of which 7 were waited for; matrix products, arithmetic and copies ran while one was open for 5% of the time, Pallas kernels for 16%

profile of v4, /device:TPU:1, one launch (start us, length us, event | category | flops | bytes accessed | tf_op | source)
XLA Modules:
  0.0 177.7 jit_solution(4580265590896127412)
XLA Ops:
  0.7 0.8 copy_bitcast_fusion.1
  1.6 0.7 pad_maximum_fusion
  2.3 28.7 %all_to_all.40 = bf16[4,208,128]{2,1,0:T(8,128)(2,1)S(1)} all-to-all(bf16[4,208,128]{2,1,0:T(8,128)(2,1)S(1)} %broadcast_in_dim.18), channel_id=1, replica_groups=mesh['x'=4,'zl'=4,'y'=4,'zh'=4,'c'=2] {'zh'}, dimensions={0} | all-to-all | bytes 425984 | tf_op jit(solution)/shard_map/all_to_all | solution.py:31
  31.0 1.9 %broadcast_in_dim.19 = bf16[16,4,144,128]{3,2,1,0:T(8,128)(2,1)} broadcast(bf16[4,144,128]{2,1,0:T(8,128)(2,1)S(1)} %slice.9), dimensions={1,2,3} | broadcast | bytes 2506752 | tf_op jit(solution)/shard_map/broadcast_in_dim | solution.py:36
  32.9 6.9 %all-to-all-start.1 = ((bf16[16,4,144,128]{3,2,1,0:T(8,128)(2,1)}), bf16[16,4,144,128]{3,2,1,0:T(8,128)(2,1)}, u32[]{:S(2)}, u32[]{:S(2)}) async-start(bf16[16,4,144,128]{3,2,1,0:T(8,128)(2,1)} %broadcast_in_dim.19), calls=%async_computation.1 | async-start | bytes 4718592 | tf_op jit(solution)/shard_map/all_to_all | solution.py:31
  39.8 5.5 %collective-permute-start = (bf16[16,4096]{1,0:T(8,128)(2,1)S(1)}, bf16[16,4096]{1,0:T(8,128)(2,1)S(1)}, u32[]{:S(2)}, u32[]{:S(2)}) collective-permute-start(bf16[16,4096]{1,0:T(8,128)(2,1)S(1)} %copy-done.3), channel_id=1, source_target_pairs={{0,2},{2,4},{4,6},{6,0},{1,3},{3,5},{5,7},{7,1},{8,10},{10,12},{12... | collective-permute-start | bytes 393224 | tf_op jit(solution)/shard_map/ppermute | solution.py:475
  45.3 3.7 %collective-permute-start.2 = (bf16[16,4096]{1,0:T(8,128)(2,1)S(1)}, bf16[16,4096]{1,0:T(8,128)(2,1)S(1)}, u32[]{:S(2)}, u32[]{:S(2)}) collective-permute-start(bf16[16,4096]{1,0:T(8,128)(2,1)S(1)} %copy-done.3), channel_id=1, source_target_pairs={{0,6},{2,0},{4,2},{6,4},{1,7},{3,1},{5,3},{7,5},{8,14},{10,8},{12,... | collective-permute-start | bytes 393224 | tf_op jit(solution)/shard_map/ppermute | solution.py:475
  49.5 6.9 %collective-permute-start.1 = (bf16[16,4096]{1,0:T(8,128)(2,1)S(1)}, bf16[16,4096]{1,0:T(8,128)(2,1)S(1)}, u32[]{:S(2)}, u32[]{:S(2)}) collective-permute-start(bf16[16,4096]{1,0:T(8,128)(2,1)S(1)} %collective-permute-done.prompt1_ref), channel_id=1, source_target_pairs={{0,2},{2,4},{4,6},{6,0},{1,3},{3,5},{5,7},{7,1},{8,10},{10,12},{12... | collective-permute-start | bytes 393224 | tf_op jit(solution)/shard_map/ppermute | solution.py:475
  56.4 8.8 %collective-permute-done.1.prompt2_ref = bf16[16,4096]{1,0:T(8,128)(2,1)S(1)} collective-permute-done((bf16[16,4096]{1,0:T(8,128)(2,1)S(1)}, bf16[16,4096]{1,0:T(8,128)(2,1)S(1)}, u32[]{:S(2)}, u32[]{:S(2)}) %collective-permute-start.1) | collective-permute-done | bytes 131104 | tf_op jit(solution)/shard_map/ppermute | solution.py:475
  65.6 13.7 %collective-permute-start.3 = (bf16[4,4,4,144,128]{4,3,2,1,0:T(8,128)(2,1)}, bf16[4,4,4,144,128]{4,3,2,1,0:T(8,128)(2,1)}, u32[]{:S(2)}, u32[]{:S(2)}) collective-permute-start(bf16[4,4,4,144,128]{4,3,2,1,0:T(8,128)(2,1)} %bitcast.7.weight_ref), channel_id=1, source_target_pairs={{0,1},{1,0},{2,3},{3,2},{4,5},{5,4},{6,7},{7,6},{8,9},{9,8},{10,11... | collective-permute-start | bytes 7077896 | tf_op jit(solution)/shard_map/ppermute | solution.py:514
  79.3 0.9 broadcast_in_dim.20
  80.2 4.0 %all-to-all-start.2 = ((bf16[8,4,64,128]{3,2,1,0:T(8,128)(2,1)}), bf16[8,4,64,128]{3,2,1,0:T(8,128)(2,1)S(1)}, u32[]{:S(2)}, u32[]{:S(2)}) async-start(bf16[8,4,64,128]{3,2,1,0:T(8,128)(2,1)} %broadcast_in_dim.20), calls=%async_computation.2 | async-start | bytes 1048576 | tf_op jit(solution)/shard_map/all_to_all | solution.py:31
  85.0 7.7 %project.1 = (bf16[128,512]{1,0:T(8,128)(2,1)}, bf16[8,256,128]{2,1,0:T(8,128)(2,1)}, bf16[4096,512]{1,0:T(8,128)(2,1)}, bf16[16,4096]{1,0:T(8,128)(2,1)}) custom-call(s32[4]{0:T(128)} %pad_add_fusion.place_ref, bf16[128,4096]{1,0:T(8,128)(2,1)} %x_ref.3, bf16[16,4096]{1,0:T(8,128)(2,1)} %prompt_ref.3, bf16[16,4096]{1,0:T(8,128)(2,1)} %copy-done.5, ...), custom_call_target="tpu_custom_call" | custom-call | flops 600000000 | bytes 10485760 | tf_op jit(solution)/shard_map/project/pallas_call | solution.py:394
  92.7 1.1 all-to-all-done.2
  93.7 4.3 %all-to-all-start.3 = ((bf16[8,256,128]{2,1,0:T(8,128)(2,1)}), bf16[8,256,128]{2,1,0:T(8,128)(2,1)S(1)}, u32[]{:S(2)}, u32[]{:S(2)}) async-start(bf16[8,256,128]{2,1,0:T(8,128)(2,1)} %get-tuple-element.40), calls=%async_computation.3 | async-start | bytes 1048576 | tf_op jit(solution)/shard_map/all_to_all | solution.py:31
  98.8 0.8 broadcast_in_dim.40.chosen_ref
  99.6 8.7 %attend_forward.1 = (bf16[8,256,128]{2,1,0:T(8,128)(2,1)}, bf16[128,512]{1,0:T(8,128)(2,1)}, bf16[16,128]{1,0:T(8,128)(2,1)}, f32[16,4096]{1,0:T(8,128)}, f32[16,512]{1,0:T(8,128)}, /*index=5*/f32[4,256,1024]{2,1,0:T(8,128)}) custom-call(bf16[128,4096]{1,0:T(8,128)(2,1)} %q_ref.3, bf16[128,4096]{1,0:T(8,128)(2,1)} %cot_ref.3, ...), custom_call_target="tpu_custom_call" | custom-call | flops 2000000000 | bytes 5242880 | tf_op jit(solution)/shard_map/attend_forward/pallas_call | solution.py:326
  108.3 4.8 %all-to-all-start.4 = ((bf16[8,256,128]{2,1,0:T(8,128)(2,1)}), bf16[8,256,128]{2,1,0:T(8,128)(2,1)S(1)}, u32[]{:S(2)}, u32[]{:S(2)}) async-start(bf16[8,256,128]{2,1,0:T(8,128)(2,1)} %get-tuple-element.44), calls=%async_computation.4 | async-start | bytes 1048576 | tf_op jit(solution)/shard_map/all_to_all | solution.py:31
  113.2 7.0 %attend_backward.1 = (bf16[8,256,128]{2,1,0:T(8,128)(2,1)}, bf16[128,512]{1,0:T(8,128)(2,1)}) custom-call(bf16[128,4096]{1,0:T(8,128)(2,1)} %q_ref.3, bf16[128,4096]{1,0:T(8,128)(2,1)} %cot_ref.3, f32[4,256,1024]{2,1,0:T(8,128)} %get-tuple-element.38.softmax_ref, bf16[8,256,128]{2,1,0:T(8,128)(2,1)} %copy-done.17, ...), custom_call_target="tpu_custom_call" | custom-call | flops 3000000000 | bytes 9437184 | tf_op jit(solution)/shard_map/attend_backward/pallas_call | solution.py:444
  120.2 2.4 %all-to-all-done.4.got_ref = bf16[8,256,128]{2,1,0:T(8,128)(2,1)S(1)} async-done(((bf16[8,256,128]{2,1,0:T(8,128)(2,1)}), bf16[8,256,128]{2,1,0:T(8,128)(2,1)S(1)}, u32[]{:S(2)}, u32[]{:S(2)}) %all-to-all-start.4) | async-done | bytes 524320 | tf_op jit(solution)/shard_map/all_to_all | solution.py:31
  122.7 1.0 copy-done.2
  123.7 1.4 adapter_terms.1
  125.1 15.6 %all_to_all.41.got_ref = bf16[8,384,128]{2,1,0:T(8,128)(2,1)S(1)} all-to-all(bf16[8,384,128]{2,1,0:T(8,128)(2,1)S(1)} %get-tuple-element.47), channel_id=1, replica_groups=mesh['x'=4,'zl'=4,'y'=4,'zh'=4,'c'=2] {'y','c'}, dimensions={0} | all-to-all | bytes 1572864 | tf_op jit(solution)/shard_map/all_to_all | solution.py:31
  140.7 0.8 keys_y.1
  141.6 5.7 %all-to-all-start.6 = ((bf16[4,208,128]{2,1,0:T(8,128)(2,1)}), bf16[4,208,128]{2,1,0:T(8,128)(2,1)S(1)}, u32[]{:S(2)}, u32[]{:S(2)}) async-start(bf16[4,208,128]{2,1,0:T(8,128)(2,1)} %keys_y.1), calls=%async_computation.6 | async-start | bytes 425984 | tf_op jit(solution)/shard_map/all_to_all | solution.py:31
  147.7 4.6 %fusion = bf16[128,4096]{1,0:T(8,128)(2,1)} fusion(f32[128,4096]{1,0:T(8,128)S(1)} %convolution_multiply_fusion, bf16[128,512]{1,0:T(8,128)(2,1)S(1)} %copy-done.18, bf16[4096,512]{1,0:T(8,128)(2,1)} %get-tuple-element.50.weight_ref), kind=kOutput, calls=%fused_computation.2 | convolution fusion | flops 537919488 | bytes 7471104 | tf_op jit(solution)/shard_map/dot_general | solution.py:40
  152.4 8.1 %all-to-all-done.6.got_ref = bf16[4,208,128]{2,1,0:T(8,128)(2,1)S(1)} async-done(((bf16[4,208,128]{2,1,0:T(8,128)(2,1)}), bf16[4,208,128]{2,1,0:T(8,128)(2,1)S(1)}, u32[]{:S(2)}, u32[]{:S(2)}) %all-to-all-start.6) | async-done | bytes 213024 | tf_op jit(solution)/shard_map/all_to_all | solution.py:31
  160.5 0.8 keys_zh.1
  161.9 6.0 %all-to-all-start.7 = ((bf16[16,80,128]{2,1,0:T(8,128)(2,1)}), bf16[16,80,128]{2,1,0:T(8,128)(2,1)S(1)}, u32[]{:S(2)}, u32[]{:S(2)}) async-start(bf16[16,80,128]{2,1,0:T(8,128)(2,1)} %get-tuple-element.57), calls=%async_computation.7 | async-start | bytes 655360 | tf_op jit(solution)/shard_map/all_to_all | solution.py:31
  167.9 4.8 %prompt_gradient.1 = bf16[16,4096]{1,0:T(8,128)(2,1)} custom-call(bf16[16,512]{1,0:T(8,128)(2,1)} %copy-done.14, bf16[16,512]{1,0:T(8,128)(2,1)} %up_ref.7, bf16[16,4096]{1,0:T(8,128)(2,1)} %get-tuple-element.37.down_ref, bf16[4096,512]{1,0:T(8,128)(2,1)} %get-tuple-element.50.weight_ref), custom_call_target="tpu_custom_call" | custom-call | tf_op jit(solution)/shard_map/prompt_gradient/pallas_call | solution.py:426
  172.7 4.4 %all-to-all-done.7.got_ref = bf16[16,80,128]{2,1,0:T(8,128)(2,1)S(1)} async-done(((bf16[16,80,128]{2,1,0:T(8,128)(2,1)}), bf16[16,80,128]{2,1,0:T(8,128)(2,1)S(1)}, u32[]{:S(2)}, u32[]{:S(2)}) %all-to-all-start.7) | async-done | bytes 327712 | tf_op jit(solution)/shard_map/all_to_all | solution.py:31
  177.1 0.7 over_group.1
  (59 shorter events, 3.7 us)
Async XLA Ops:
  0.6 0.9 copy-start
  32.9 6.9 %copy-start.3 = (bf16[16,4096]{1,0:T(8,128)(2,1)S(1)}, bf16[16,4096]{1,0:T(8,128)(2,1)}, u32[]{:S(2)}) copy-start(bf16[16,4096]{1,0:T(8,128)(2,1)} %prompt_ref.3) | copy-start | bytes 393220
  32.9 52.0 %copy-start.20 = (s32[1,128]{1,0:T(1,128)S(1)}, s32[1,128]{1,0:T(1,128)}, u32[]{:S(2)}) copy-start(s32[1,128]{1,0:T(1,128)} %param.17) | copy-start | bytes 1540
  32.9 32.8 %all-to-all-start.1 = ((bf16[16,4,144,128]{3,2,1,0:T(8,128)(2,1)}), bf16[16,4,144,128]{3,2,1,0:T(8,128)(2,1)}, u32[]{:S(2)}, u32[]{:S(2)}) async-start(bf16[16,4,144,128]{3,2,1,0:T(8,128)(2,1)} %broadcast_in_dim.19), calls=%async_computation.1 | async-start | bytes 4718592 | tf_op jit(solution)/shard_map/all_to_all | solution.py:31
  39.8 9.7 %collective-permute-start = (bf16[16,4096]{1,0:T(8,128)(2,1)S(1)}, bf16[16,4096]{1,0:T(8,128)(2,1)S(1)}, u32[]{:S(2)}, u32[]{:S(2)}) collective-permute-start(bf16[16,4096]{1,0:T(8,128)(2,1)S(1)} %copy-done.3), channel_id=1, source_target_pairs={{0,2},{2,4},{4,6},{6,0},{1,3},{3,5},{5,7},{7,1},{8,10},{10,12},{12... | collective-permute-start | bytes 393224 | tf_op jit(solution)/shard_map/ppermute | solution.py:475
  45.3 11.1 %collective-permute-start.2 = (bf16[16,4096]{1,0:T(8,128)(2,1)S(1)}, bf16[16,4096]{1,0:T(8,128)(2,1)S(1)}, u32[]{:S(2)}, u32[]{:S(2)}) collective-permute-start(bf16[16,4096]{1,0:T(8,128)(2,1)S(1)} %copy-done.3), channel_id=1, source_target_pairs={{0,6},{2,0},{4,2},{6,4},{1,7},{3,1},{5,3},{7,5},{8,14},{10,8},{12,... | collective-permute-start | bytes 393224 | tf_op jit(solution)/shard_map/ppermute | solution.py:475
  49.5 35.5 %copy-start.5 = (bf16[16,4096]{1,0:T(8,128)(2,1)}, bf16[16,4096]{1,0:T(8,128)(2,1)S(1)}, u32[]{:S(2)}) copy-start(bf16[16,4096]{1,0:T(8,128)(2,1)S(1)} %collective-permute-done.prompt1_ref) | copy-start | bytes 393220
  49.5 15.7 %collective-permute-start.1 = (bf16[16,4096]{1,0:T(8,128)(2,1)S(1)}, bf16[16,4096]{1,0:T(8,128)(2,1)S(1)}, u32[]{:S(2)}, u32[]{:S(2)}) collective-permute-start(bf16[16,4096]{1,0:T(8,128)(2,1)S(1)} %collective-permute-done.prompt1_ref), channel_id=1, source_target_pairs={{0,2},{2,4},{4,6},{6,0},{1,3},{3,5},{5,7},{7,1},{8,10},{10,12},{12... | collective-permute-start | bytes 393224 | tf_op jit(solution)/shard_map/ppermute | solution.py:475
  56.4 28.6 %copy-start.7 = (bf16[16,4096]{1,0:T(8,128)(2,1)}, bf16[16,4096]{1,0:T(8,128)(2,1)S(1)}, u32[]{:S(2)}) copy-start(bf16[16,4096]{1,0:T(8,128)(2,1)S(1)} %collective-permute-done.2.prompt3_ref) | copy-start | bytes 393220
  65.2 19.8 %copy-start.9 = (bf16[16,4096]{1,0:T(8,128)(2,1)}, bf16[16,4096]{1,0:T(8,128)(2,1)S(1)}, u32[]{:S(2)}) copy-start(bf16[16,4096]{1,0:T(8,128)(2,1)S(1)} %collective-permute-done.1.prompt2_ref) | copy-start | bytes 393220
  65.6 19.3 %collective-permute-start.3 = (bf16[4,4,4,144,128]{4,3,2,1,0:T(8,128)(2,1)}, bf16[4,4,4,144,128]{4,3,2,1,0:T(8,128)(2,1)}, u32[]{:S(2)}, u32[]{:S(2)}) collective-permute-start(bf16[4,4,4,144,128]{4,3,2,1,0:T(8,128)(2,1)} %bitcast.7.weight_ref), channel_id=1, source_target_pairs={{0,1},{1,0},{2,3},{3,2},{4,5},{5,4},{6,7},{7,6},{8,9},{9,8},{10,11... | collective-permute-start | bytes 7077896 | tf_op jit(solution)/shard_map/ppermute | solution.py:514
  80.2 13.5 %all-to-all-start.2 = ((bf16[8,4,64,128]{3,2,1,0:T(8,128)(2,1)}), bf16[8,4,64,128]{3,2,1,0:T(8,128)(2,1)S(1)}, u32[]{:S(2)}, u32[]{:S(2)}) async-start(bf16[8,4,64,128]{3,2,1,0:T(8,128)(2,1)} %broadcast_in_dim.20), calls=%async_computation.2 | async-start | bytes 1048576 | tf_op jit(solution)/shard_map/all_to_all | solution.py:31
  84.9 13.1 %copy-start.21 = (s32[1,8]{1,0:T(1,128)S(1)}, s32[1,8]{1,0:T(1,128)}, u32[]{:S(2)}) copy-start(s32[1,8]{1,0:T(1,128)} %param.18) | copy-start | bytes 100
  93.7 5.8 %copy-start.16 = (bf16[8,4,64,128]{3,2,1,0:T(8,128)(2,1)}, bf16[8,4,64,128]{3,2,1,0:T(8,128)(2,1)S(1)}, u32[]{:S(2)}) copy-start(bf16[8,4,64,128]{3,2,1,0:T(8,128)(2,1)S(1)} %all-to-all-done.2) | copy-start | bytes 1572868
  93.7 14.5 %all-to-all-start.3 = ((bf16[8,256,128]{2,1,0:T(8,128)(2,1)}), bf16[8,256,128]{2,1,0:T(8,128)(2,1)S(1)}, u32[]{:S(2)}, u32[]{:S(2)}) async-start(bf16[8,256,128]{2,1,0:T(8,128)(2,1)} %get-tuple-element.40), calls=%async_computation.3 | async-start | bytes 1048576 | tf_op jit(solution)/shard_map/all_to_all | solution.py:31
  108.3 4.8 %copy-start.17 = (bf16[8,256,128]{2,1,0:T(8,128)(2,1)}, bf16[8,256,128]{2,1,0:T(8,128)(2,1)S(1)}, u32[]{:S(2)}) copy-start(bf16[8,256,128]{2,1,0:T(8,128)(2,1)S(1)} %all-to-all-done.3.value_ref) | copy-start | bytes 1572868
  108.3 14.3 %all-to-all-start.4 = ((bf16[8,256,128]{2,1,0:T(8,128)(2,1)}), bf16[8,256,128]{2,1,0:T(8,128)(2,1)S(1)}, u32[]{:S(2)}, u32[]{:S(2)}) async-start(bf16[8,256,128]{2,1,0:T(8,128)(2,1)} %get-tuple-element.44), calls=%async_computation.4 | async-start | bytes 1048576 | tf_op jit(solution)/shard_map/all_to_all | solution.py:31
  113.1 9.5 %copy-start.1 = (bf16[16,4096]{1,0:T(8,128)(2,1)S(1)}, bf16[16,4096]{1,0:T(8,128)(2,1)}, u32[]{:S(2)}) copy-start(bf16[16,4096]{1,0:T(8,128)(2,1)} %get-tuple-element.37.down_ref) | copy-start | bytes 393220
  113.1 9.5 %copy-start.4 = (bf16[16,4096]{1,0:T(8,128)(2,1)S(1)}, bf16[16,4096]{1,0:T(8,128)(2,1)}, u32[]{:S(2)}) copy-start(bf16[16,4096]{1,0:T(8,128)(2,1)} %prompt_ref.3) | copy-start | bytes 393220
  113.1 9.5 %copy-start.6 = (bf16[16,4096]{1,0:T(8,128)(2,1)S(1)}, bf16[16,4096]{1,0:T(8,128)(2,1)}, u32[]{:S(2)}) copy-start(bf16[16,4096]{1,0:T(8,128)(2,1)} %copy-done.5) | copy-start | bytes 393220
  113.1 9.5 %copy-start.8 = (bf16[16,4096]{1,0:T(8,128)(2,1)S(1)}, bf16[16,4096]{1,0:T(8,128)(2,1)}, u32[]{:S(2)}) copy-start(bf16[16,4096]{1,0:T(8,128)(2,1)} %copy-done.7) | copy-start | bytes 393220
  113.1 9.5 %copy-start.10 = (bf16[16,4096]{1,0:T(8,128)(2,1)S(1)}, bf16[16,4096]{1,0:T(8,128)(2,1)}, u32[]{:S(2)}) copy-start(bf16[16,4096]{1,0:T(8,128)(2,1)} %copy-done.9) | copy-start | bytes 393220
  113.1 9.5 %copy-start.11 = (f32[16,4096]{1,0:T(8,128)S(1)}, f32[16,4096]{1,0:T(8,128)}, u32[]{:S(2)}) copy-start(f32[16,4096]{1,0:T(8,128)} %get-tuple-element.45.grad_ref) | copy-start | bytes 786436
  113.2 9.5 %copy-start.12 = (bf16[16,512]{1,0:T(8,128)(2,1)S(1)}, bf16[16,512]{1,0:T(8,128)(2,1)}, u32[]{:S(2)}) copy-start(bf16[16,512]{1,0:T(8,128)(2,1)} %up_ref.7) | copy-start | bytes 49156
  113.2 9.5 %copy-start.13 = (f32[16,512]{1,0:T(8,128)S(1)}, f32[16,512]{1,0:T(8,128)}, u32[]{:S(2)}) copy-start(f32[16,512]{1,0:T(8,128)} %get-tuple-element.46.second_ref) | copy-start | bytes 98308
  113.2 9.5 %copy-start.15 = (s32[4]{0:T(128)S(1)}, s32[4]{0:T(128)}, u32[]{:S(2)}) copy-start(s32[4]{0:T(128)} %pad_add_fusion.place_ref) | copy-start | bytes 52
  122.7 1.0 copy-start.2
  123.7 23.6 %copy-start.19 = (bf16[16,128]{1,0:T(8,128)(2,1)S(1)}, bf16[16,128]{1,0:T(8,128)(2,1)}, u32[]{:S(2)}) copy-start(bf16[16,128]{1,0:T(8,128)(2,1)} %get-tuple-element.51) | copy-start | bytes 12292
  125.1 22.6 %copy-start.18 = (bf16[128,512]{1,0:T(8,128)(2,1)S(1)}, bf16[128,512]{1,0:T(8,128)(2,1)}, u32[]{:S(2)}) copy-start(bf16[128,512]{1,0:T(8,128)(2,1)} %get-tuple-element.49) | copy-start | bytes 393220
  141.6 18.9 %all-to-all-start.6 = ((bf16[4,208,128]{2,1,0:T(8,128)(2,1)}), bf16[4,208,128]{2,1,0:T(8,128)(2,1)S(1)}, u32[]{:S(2)}, u32[]{:S(2)}) async-start(bf16[4,208,128]{2,1,0:T(8,128)(2,1)} %keys_y.1), calls=%async_computation.6 | async-start | bytes 425984 | tf_op jit(solution)/shard_map/all_to_all | solution.py:31
  161.3 0.6 copy-start.14
  161.9 15.2 %all-to-all-start.7 = ((bf16[16,80,128]{2,1,0:T(8,128)(2,1)}), bf16[16,80,128]{2,1,0:T(8,128)(2,1)S(1)}, u32[]{:S(2)}, u32[]{:S(2)}) async-start(bf16[16,80,128]{2,1,0:T(8,128)(2,1)} %get-tuple-element.57), calls=%async_computation.7 | async-start | bytes 655360 | tf_op jit(solution)/shard_map/all_to_all | solution.py:31

commit v5 on v4

v5 whole, which is shorter than its diff:
```python
import jax
import jax.numpy as jnp
import numpy as np
from jax import lax
from jax.experimental import pallas as pl
from jax.experimental.pallas import tpu as pltpu
from jax.sharding import Mesh, PartitionSpec as P

HEADS = 32
KV_HEADS = 4
HEAD_DIM = 128
GROUP_SIZE = HEADS // KV_HEADS
PROMPT_LEN = 128
PROMPTS = 4
RANK = 16
TOKENS = 128
D = 4096
HALF = D // 2
SCALE = HEAD_DIM**-0.5
ADAPTER_SCALE = 2.0
FACTOR = ADAPTER_SCALE * float(73728) ** (-0.5)
AXES = ("x", "zl", "y", "zh", "c")
SAMPLE = ("y", "zh", "c")
GROUP = ("x", "zl")
OWNERS = ("y", "c")
PAIR = 2 * TOKENS
F32 = jnp.float32
BF16 = jnp.bfloat16


def swap(array, axis):
    return lax.all_to_all(array, axis, 0, 0, tiled=True)


def gather(array, axis):
    n = lax.axis_size(axis)
    return swap(jnp.broadcast_to(array[None], (n,) + array.shape), axis)


def nt(left, right):
    return lax.dot_general(left, right, (((1,), (1,)), ((), ())), preferred_element_type=F32)


def tn(left, right):
    return lax.dot_general(left, right, (((0,), (0,)), ((), ())), preferred_element_type=F32)


def nn(left, right):
    return jnp.dot(left, right, preferred_element_type=F32)


def expand(rows, mask, axis=1):
    return jnp.concatenate([rows * mask[p] for p in range(PROMPTS)], axis=axis)


def masks_of(segment_ref, choice_ref, mask_ref, mask_t_ref):
    segment = segment_ref[...]
    prompt = jnp.zeros_like(segment)
    for i in range(choice_ref.shape[1]):
        prompt = jnp.where(segment == i, choice_ref[0, i], prompt)
    chosen = jnp.broadcast_to(jnp.concatenate([prompt, prompt], axis=1), (HEAD_DIM, PAIR))
    for p in range(PROMPTS):
        mask = jnp.where(chosen == p, 1.0, 0.0).astype(F32)
        mask_t_ref[p] = mask.astype(BF16)
        mask_ref[p] = mask.T.astype(BF16)


def own_bias(segment_ref):
    segment = jnp.broadcast_to(segment_ref[...], (TOKENS, TOKENS))
    row = lax.broadcasted_iota(jnp.int32, (TOKENS, TOKENS), 0)
    column = lax.broadcasted_iota(jnp.int32, (TOKENS, TOKENS), 1)
    bias = jnp.where((segment.T == segment) & (row <= column), 0.0, -1e30).astype(F32)
    return jnp.concatenate([bias, bias], axis=1)


def pair_rows(ref, pair):
    first = 2 * pair * HEAD_DIM
    return jnp.concatenate(
        [ref[:, first : first + HEAD_DIM], ref[:, first + HEAD_DIM : first + 2 * HEAD_DIM]], axis=0
    )


def prompt_block(ref):
    return jnp.concatenate(
        [jnp.concatenate([ref[2 * p], ref[2 * p + 1]], axis=0) for p in range(PROMPTS)], axis=1
    )


def spread(ref, block):
    for p in range(PROMPTS):
        for c in range(2):
            ref[2 * p + c, :64, :] = block[
                c * 64 : (c + 1) * 64, p * HEAD_DIM : (p + 1) * HEAD_DIM
            ].astype(ref.dtype)


def softmax_pair(key_cat, own_key, expanded, columns, bias):
    seen = nn(key_cat, expanded) * SCALE
    own = nn(own_key, columns) * SCALE + bias
    top = jnp.maximum(jnp.max(seen, axis=0, keepdims=True), jnp.max(own, axis=0, keepdims=True))
    seen, own = jnp.exp(seen - top), jnp.exp(own - top)
    total = jnp.sum(seen, axis=0, keepdims=True) + jnp.sum(own, axis=0, keepdims=True)
    share = 1.0 / total
    return seen * share, own * share


BLOCKS = [
    (((y * 4 + zh) * 2 + c) * 128, y, zh, c) for y in range(4) for zh in range(4) for c in range(2)
]


def forward_kernel(
    choice_ref, q_ref, cot_ref, key_ref, own_key_ref, segment_ref, x_ref, up_ref, down_ref,
    send_ref, low_ref, grad_ref, second_ref, softmax_ref,
    cots, back, first, mask, mask_t, bias,
):
    k = pl.program_id(0)
    key_cat = prompt_block(key_ref)
    own_key = own_key_ref[...]

    @pl.when(k == 0)
    def _():
        masks_of(segment_ref, choice_ref, mask, mask_t)
        bias[...] = own_bias(segment_ref)

    for pair in range(GROUP_SIZE // 2):
        columns = pair_rows(q_ref, pair).T
        seen, own = softmax_pair(key_cat, own_key, expand(columns, mask_t, 0), columns, bias[...])
        at = pl.ds(pair * PAIR, PAIR)
        softmax_ref[0, :TOKENS, at] = seen.astype(BF16)
        softmax_ref[0, TOKENS:, at] = own.astype(BF16)
        cot = pair_rows(cot_ref, pair)
        cots[at, : PROMPTS * HEAD_DIM] = expand(cot, mask)
        cots[at, PROMPTS * HEAD_DIM :] = cot
    spread(send_ref, nn(softmax_ref[0, :TOKENS, :], cots[:, : PROMPTS * HEAD_DIM]))
    low = nn(softmax_ref[0, TOKENS:, :], cots[:, PROMPTS * HEAD_DIM :]).astype(BF16)
    low_ref[...] = low

    @pl.when(k == 0)
    def _():
        back[...] = jnp.zeros_like(back)
        first[...] = nt(x_ref[...], down_ref[...]).astype(BF16)

    back[...] += nt(up_ref[...], low)
    second_ref[...] = tn(first[...], low)

    @pl.when(k == KV_HEADS - 1)
    def _():
        grad_ref[...] = nn(back[...].astype(BF16), x_ref[...])


def place_before(place, step):
    return lax.rem(place + (4 - step), 4)


def adapter_kernel(
    keys_ref, got_ref, grad_ref, second_ref, up_ref, down_ref,
    prompt_ref, prompt1_ref, far_ref, far_rest_ref, prompt3_ref,
    part_ref, send_ref,
):
    low = total_of(got_ref[...]).astype(BF16)
    part_ref[...] = low
    far = jnp.concatenate([far_ref[...], far_rest_ref[:, : D - HALF]], axis=1)
    prompts = jnp.concatenate(
        [prompt_ref[:, :D], prompt1_ref[:, :D], far, prompt3_ref[:, :D]], axis=0
    )
    prompt_first = nt(prompts, down_ref[...]).astype(BF16)
    prompt_back = nt(up_ref[...], low).astype(BF16)
    second = (second_ref[...] + tn(prompt_first, low)).astype(BF16)
    grad = (grad_ref[...] + nn(prompt_back, prompts)).astype(BF16)
    send_ref[:, :64, :] = keys_ref[...]
    for at, y, zh, c in BLOCKS:
        send_ref[y * 2 + c, 64:80, zh * 128 : (zh + 1) * 128] = grad[:, at : at + 128]
    for owner in range(8):
        send_ref[owner, 80:, :] = second


def project_kernel(
    x_ref, prompt_ref, prompt1_ref, far_ref, far_rest_ref, prompt3_ref, up_ref,
    factor_ref, other_factor_ref, *refs,
):
    parts, (values_ref, send_ref, down_ref, rows, first, weight) = refs[:8], refs[8:]
    k = pl.program_id(0)
    core = lax.axis_index("c")
    places = [(i % 4, core if i < 4 else 1 - core, ref) for i, ref in enumerate(parts)]

    @pl.when(k == 0)
    def _():
        rows[:TOKENS, :] = x_ref[...]
        for step, ref in ((0, prompt_ref), (1, prompt1_ref), (3, prompt3_ref)):
            rows[TOKENS + step * 16 : TOKENS + (step + 1) * 16, :] = ref[...]
        rows[TOKENS + 32 : TOKENS + 48, :HALF] = far_ref[...]
        rows[TOKENS + 32 : TOKENS + 48, HALF:] = far_rest_ref[...]
        for ref, c in ((factor_ref, core), (other_factor_ref, 1 - core)):
            for y in range(4):
                for zh in range(4):
                    at = pl.multiple_of(((y * 4 + zh) * 2 + c) * 128, 128)
                    down_ref[:, pl.ds(at, 128)] = ref[zh, y]
        first[...] = nt(rows[...], down_ref[...]).astype(BF16)

    for y, c, ref in places:
        for zh in range(4):
            row = pl.multiple_of(((y * 4 + zh) * 2 + c) * 128, 128)
            weight[pl.ds(row, 128), :] = ref[0, 0, zh * 128 : (zh + 1) * 128, :]
    values = nn(rows[...], weight[...]) + ADAPTER_SCALE * nn(first[...], up_ref[...])
    values = values.astype(BF16)
    values_ref[...] = values[:TOKENS]
    for owner in range(8):
        send_ref[owner] = values[TOKENS:]


def total_of(parts):
    parts = parts.astype(F32)
    total = parts[0]
    for i in range(1, parts.shape[0]):
        total = total + parts[i]
    return total


def keys_y_kernel(got_ref, value_ref, send_ref):
    total = total_of(got_ref[...]).astype(BF16)
    value = value_ref[...]
    for zh in range(4):
        owner = place_before(lax.axis_index("zh"), zh)
        for k in range(KV_HEADS):
            at = slice(k * HEAD_DIM, (k + 1) * HEAD_DIM)
            rows = slice(zh * 16, (zh + 1) * 16)
            send_ref[owner, k * 16 : (k + 1) * 16, :] = total[rows, at]
            send_ref[owner, 64 + k * 16 : 64 + (k + 1) * 16, :] = value[rows, at]
            send_ref[zh, 144 + k * 16 : 144 + (k + 1) * 16, :] = total[80:, at]
        send_ref[zh, 128:144, :] = total[64:80, zh * 128 : (zh + 1) * 128]


def keys_zh_kernel(got_ref, key_ref, low_ref, send_ref):
    total = total_of(got_ref[...])
    for k in range(KV_HEADS):
        at = slice(k * HEAD_DIM, (k + 1) * HEAD_DIM)
        key_ref[:, at] = total[k * 16 : (k + 1) * 16].astype(BF16)
        low_ref[:, at] = total[64 + k * 16 : 64 + (k + 1) * 16].astype(BF16)
    terms = total[128:].astype(BF16)
    for g in range(16):
        send_ref[g] = terms


def weight_copies_kernel(start_ref, send_ref, part, sems):
    for zh in range(4):
        part[zh * 128 : (zh + 1) * 128, :] = start_ref[zh, :128, :]
    part[512:, :] = start_ref[lax.axis_index("x"), 128:, :]
    copies = [
        pltpu.make_async_copy(part, send_ref.at[i], sems.at[i]) for i in range(send_ref.shape[0])
    ]
    for copy in copies:
        copy.start()
    for copy in copies:
        copy.wait()


def key_copies_kernel(key_ref, key1_ref, key2_ref, key3_ref, send_ref):
    for step, ref in enumerate((key_ref, key1_ref, key2_ref, key3_ref)):
        for owner in range(8):
            send_ref[owner, step * 16 : (step + 1) * 16, :] = ref[...]


def group_kernel(got_ref, first_ref, second_ref):
    total = total_of(got_ref[...]) * FACTOR
    first_ref[...] = total[:16]
    for k in range(KV_HEADS):
        second_ref[:, k * HEAD_DIM : (k + 1) * HEAD_DIM] = total[16 + k * 16 : 16 + (k + 1) * 16]


def gradient_kernel(low_ref, up_ref, down_ref, *refs):
    parts, (grad_ref, back, weight) = refs[:8], refs[8:]

    @pl.when(pl.program_id(0) == 0)
    def _():
        back[...] = nt(low_ref[...], up_ref[...]).astype(BF16)

    core = lax.axis_index("c")
    for i, ref in enumerate(parts):
        c = core if i < 4 else 1 - core
        at = slice(i % 4 * HEAD_DIM, (i % 4 + 1) * HEAD_DIM)
        for zh in range(4):
            row = pl.multiple_of((zh * 2 + c) * 128, 128)
            weight[pl.ds(row, 128), at] = ref[0, 0, zh * 128 : (zh + 1) * 128, :]
    grad = nt(weight[...], low_ref[...]).T + ADAPTER_SCALE * nn(back[...], down_ref[...])
    grad_ref[...] = grad.astype(BF16)


def in_vmem(kernel, n, shapes, name):
    return pl.pallas_call(
        kernel,
        in_specs=[pl.BlockSpec(memory_space=pltpu.VMEM)] * n,
        out_specs=jax.tree.map(lambda _: pl.BlockSpec(memory_space=pltpu.VMEM), shapes),
        out_shape=shapes,
        compiler_params=pltpu.CompilerParams(vmem_limit_bytes=24 << 20),
        name=name,
    )


def sent(*shape):
    return jax.ShapeDtypeStruct(shape, BF16)


def backward_kernel(
    choice_ref, q_ref, cot_ref, softmax_ref, value_ref, own_value_ref, segment_ref,
    send_ref, own_ref,
    grads, own_grads, queries, mask, mask_t,
):
    @pl.when(pl.program_id(0) == 0)
    def _():
        masks_of(segment_ref, choice_ref, mask, mask_t)

    value_cat = prompt_block(value_ref)
    own_value = own_value_ref[...]
    for pair in range(GROUP_SIZE // 2):
        rows = pair_rows(q_ref, pair)
        at = pl.ds(pair * PAIR, PAIR)
        queries[at, : PROMPTS * HEAD_DIM] = expand(rows, mask)
        queries[at, PROMPTS * HEAD_DIM :] = rows
        seen = softmax_ref[0, :TOKENS, at].astype(F32)
        own = softmax_ref[0, TOKENS:, at].astype(F32)
        columns = pair_rows(cot_ref, pair).T
        seen_grad = nn(value_cat, expand(columns, mask_t, 0))
        own_grad = nn(own_value, columns)
        delta = jnp.sum(seen * seen_grad, axis=0, keepdims=True) + jnp.sum(
            own * own_grad, axis=0, keepdims=True
        )
        grads[:, at] = (seen * (seen_grad - delta)).astype(BF16)
        own_grads[:, at] = (own * (own_grad - delta)).astype(BF16)
    spread(send_ref, nn(grads[...], queries[:, : PROMPTS * HEAD_DIM]) * SCALE)
    own_ref[...] = (nn(own_grads[...], queries[:, PROMPTS * HEAD_DIM :]) * SCALE).astype(BF16)


def whole(shape):
    return pl.BlockSpec(shape, lambda k: (0,) * len(shape))


def heads_of(rows, width):
    return pl.BlockSpec((rows, width), lambda k: (0, k))


PROMPT_SPEC = pl.BlockSpec((8, 64, HEAD_DIM), lambda k: (0, 0, k))
WIDE = GROUP_SIZE * HEAD_DIM
ROWS = GROUP_SIZE * TOKENS


MASKS = [
    pltpu.VMEM((PROMPTS, PAIR, HEAD_DIM), BF16),
    pltpu.VMEM((PROMPTS, HEAD_DIM, PAIR), BF16),
]
PARAMS = pltpu.CompilerParams(vmem_limit_bytes=56 << 20, dimension_semantics=("arbitrary",))


def attend_forward(choice, queries, cotangent, keys, own_keys, segments, rows, up, down):
    return pl.pallas_call(
        forward_kernel,
        grid=(KV_HEADS,),
        in_specs=[
            pl.BlockSpec(memory_space=pltpu.SMEM),
            heads_of(TOKENS, WIDE),
            heads_of(TOKENS, WIDE),
            PROMPT_SPEC,
            heads_of(TOKENS, HEAD_DIM),
            whole((1, TOKENS)),
            whole((TOKENS, D)),
            heads_of(RANK, HEAD_DIM),
            whole((RANK, D)),
        ],
        out_specs=[
            PROMPT_SPEC,
            heads_of(TOKENS, HEAD_DIM),
            whole((RANK, D)),
            heads_of(RANK, HEAD_DIM),
            pl.BlockSpec((1, 2 * TOKENS, ROWS), lambda k: (k, 0, 0)),
        ],
        out_shape=[
            sent(8, 64, KV_HEADS * HEAD_DIM),
            sent(TOKENS, KV_HEADS * HEAD_DIM),
            jax.ShapeDtypeStruct((RANK, D), F32),
            jax.ShapeDtypeStruct((RANK, KV_HEADS * HEAD_DIM), F32),
            sent(KV_HEADS, 2 * TOKENS, ROWS),
        ],
        scratch_shapes=[
            pltpu.VMEM((ROWS, (PROMPTS + 1) * HEAD_DIM), BF16),
            pltpu.VMEM((RANK, TOKENS), F32),
            pltpu.VMEM((TOKENS, RANK), BF16),
            *MASKS,
            pltpu.VMEM((TOKENS, PAIR), F32),
        ],
        compiler_params=PARAMS,
        cost_estimate=pl.CostEstimate(
            flops=2_000_000_000, bytes_accessed=5 << 20, transcendentals=1 << 20
        ),
        name="attend_forward",
    )(choice, queries, cotangent, keys, own_keys, segments, rows, up, down)


def adapter_terms(keys, got, grad, second, up, down, prompts):
    width = KV_HEADS * HEAD_DIM
    return in_vmem(
        adapter_kernel, 11, [sent(64, width), sent(8, 96, width)], "adapter_terms"
    )(keys, got, grad, second, up, down, *prompts)


def weight_copies(start):
    return pl.pallas_call(
        weight_copies_kernel,
        in_specs=[pl.BlockSpec(memory_space=pltpu.VMEM)],
        out_specs=pl.BlockSpec(memory_space=pl.ANY),
        out_shape=sent(16, 528, HEAD_DIM),
        scratch_shapes=[pltpu.VMEM((528, HEAD_DIM), BF16), pltpu.SemaphoreType.DMA((16,))],
        name="weight_copies",
    )(start)


def key_copies(parts):
    width = KV_HEADS * HEAD_DIM
    return pl.pallas_call(
        key_copies_kernel,
        grid=(1,),
        in_specs=[
            pl.BlockSpec((16, width), lambda i, at=p.shape[1] // width - 1: (0, at)) for p in parts
        ],
        out_specs=whole((8, 64, width)),
        out_shape=sent(8, 64, width),
        name="key_copies",
    )(*parts)


def project(rows, prompts, weight, other, up):
    width = KV_HEADS * HEAD_DIM

    def run(y):
        return pl.BlockSpec((1, 1, 512, HEAD_DIM), lambda k: (k, y, 0, 0))

    runs = [run(y) for y in range(4)]
    factor = pl.BlockSpec((4, 4, RANK, HEAD_DIM), lambda k: (0, 0, 512 // RANK, 0))
    return pl.pallas_call(
        project_kernel,
        grid=(KV_HEADS,),
        in_specs=[
            whole((TOKENS, D)),
            whole((16, D)),
            whole((16, D)),
            whole((16, HALF)),
            whole((16, D - HALF)),
            whole((16, D)),
            heads_of(RANK, HEAD_DIM),
            factor,
            factor,
            *runs,
            *runs,
        ],
        out_specs=[
            heads_of(TOKENS, HEAD_DIM),
            PROMPT_SPEC,
            whole((RANK, D)),
        ],
        out_shape=[
            sent(TOKENS, width),
            sent(8, 64, width),
            sent(RANK, D),
        ],
        scratch_shapes=[
            pltpu.VMEM((TOKENS + 64, D), BF16),
            pltpu.VMEM((TOKENS + 64, RANK), BF16),
            pltpu.VMEM((D, HEAD_DIM), BF16),
        ],
        compiler_params=PARAMS,
        cost_estimate=pl.CostEstimate(
            flops=600_000_000, bytes_accessed=10 << 20, transcendentals=0
        ),
        name="project",
    )(rows, *prompts, up, weight, other, *[weight] * 4, *[other] * 4)


def input_gradient(low, up, down, weight, other):
    rows, width = low.shape

    def head(k):
        return pl.BlockSpec((1, 1, 512, HEAD_DIM), lambda y: (k, y, 0, 0))

    heads = [head(k) for k in range(KV_HEADS)]
    return pl.pallas_call(
        gradient_kernel,
        grid=(4,),
        in_specs=[
            whole((rows, width)),
            whole((RANK, width)),
            heads_of(RANK, 1024),
            *heads,
            *heads,
        ],
        out_specs=heads_of(rows, 1024),
        out_shape=sent(rows, D),
        scratch_shapes=[pltpu.VMEM((rows, RANK), BF16), pltpu.VMEM((1024, width), BF16)],
        compiler_params=PARAMS,
        cost_estimate=pl.CostEstimate(
            flops=rows * D * width * 2, bytes_accessed=5 << 20, transcendentals=0
        ),
        name="input_gradient",
    )(low, up, down, *[weight] * 4, *[other] * 4)


def attend_backward(choice, queries, cotangent, softmax, values, own_values, segments):
    return pl.pallas_call(
        backward_kernel,
        grid=(KV_HEADS,),
        in_specs=[
            pl.BlockSpec(memory_space=pltpu.SMEM),
            heads_of(TOKENS, WIDE),
            heads_of(TOKENS, WIDE),
            pl.BlockSpec((1, 2 * TOKENS, ROWS), lambda k: (k, 0, 0)),
            PROMPT_SPEC,
            heads_of(TOKENS, HEAD_DIM),
            whole((1, TOKENS)),
        ],
        out_specs=[PROMPT_SPEC, heads_of(TOKENS, HEAD_DIM)],
        out_shape=[sent(8, 64, KV_HEADS * HEAD_DIM), sent(TOKENS, KV_HEADS * HEAD_DIM)],
        scratch_shapes=[
            pltpu.VMEM((TOKENS, ROWS), BF16),
            pltpu.VMEM((TOKENS, ROWS), BF16),
            pltpu.VMEM((ROWS, (PROMPTS + 1) * HEAD_DIM), BF16),
            *MASKS,
        ],
        compiler_params=PARAMS,
        cost_estimate=pl.CostEstimate(
            flops=3_000_000_000, bytes_accessed=9 << 20, transcendentals=0
        ),
        name="attend_backward",
    )(choice, queries, cotangent, softmax, values, own_values, segments)


def move(part, axis, step):
    return lax.ppermute(part, axis, [(i, (i + step) % 4) for i in range(4)])


def after(array, *others):
    return lax.optimization_barrier((array, *others))[0]


def on_device(
    response_rows,
    prompt_rows,
    queries,
    response_keys,
    prompt_keys,
    cotangent,
    segment_index,
    prompt_choice,
    frozen_value_weight,
    value_adapter_down,
    value_adapter_up,
):
    own_columns = lax.dynamic_slice_in_dim(
        frozen_value_weight, lax.axis_index("x") * HEAD_DIM, HEAD_DIM, 1
    )
    start = gather(jnp.concatenate([own_columns, value_adapter_down.T], axis=0), "zh")
    own_prompts = after(jnp.concatenate([prompt_rows, prompt_keys], axis=1), start)
    weight = swap(weight_copies(start), ("x", "y"))
    before, behind = move(own_prompts, "zh", 1), move(own_prompts, "zh", 3)
    far, far_rest = move(before[:, :HALF], "zh", 1), move(behind[:, HALF:], "zh", 3)
    prompts = [own_prompts, before, far, far_rest, behind]
    weight, *prompts = lax.optimization_barrier((weight, *prompts))
    other = lax.ppermute(weight, "c", [(0, 1), (1, 0)])
    key_all = swap(key_copies([own_prompts, before, far_rest, behind]), OWNERS)

    shape = (4, 4, 528, HEAD_DIM)
    weights = [weight.reshape(shape), other.reshape(shape)]
    values, part, down = project(response_rows, prompts, *weights, value_adapter_up)
    value_all = swap(after(part, key_all), OWNERS)
    send, low, token_grad, token_second, softmax = attend_forward(
        prompt_choice, queries, cotangent, key_all, response_keys, segment_index, response_rows,
        value_adapter_up, down,
    )
    got = swap(after(send, value_all), OWNERS)
    key_send, own_key_grad = attend_backward(
        prompt_choice, queries, cotangent, softmax, value_all, values, segment_index
    )
    value_part, key_send = adapter_terms(
        key_send, got, token_grad, token_second, value_adapter_up, down, prompts
    )
    part = in_vmem(keys_y_kernel, 2, sent(4, 208, HEAD_DIM), "keys_y")(
        swap(key_send, OWNERS), value_part
    )
    response_grad = input_gradient(low, value_adapter_up, down, *weights)
    part, response_grad = lax.optimization_barrier((swap(part, "zh"), response_grad))
    prompt_key_grad, prompt_low, part = in_vmem(
        keys_zh_kernel,
        1,
        [sent(16, KV_HEADS * HEAD_DIM), sent(16, KV_HEADS * HEAD_DIM), sent(16, 80, HEAD_DIM)],
        "keys_zh",
    )(part)
    first_grad, second_grad = in_vmem(
        group_kernel,
        1,
        [
            jax.ShapeDtypeStruct((RANK, 128), F32),
            jax.ShapeDtypeStruct((RANK, KV_HEADS * HEAD_DIM), F32),
        ],
        "over_group",
    )(swap(part, GROUP))
    return (
        response_grad,
        input_gradient(prompt_low, value_adapter_up, down, *weights),
        own_key_grad,
        prompt_key_grad,
        first_grad.T,
        second_grad,
    )


def solution(mesh):
    fine = Mesh(np.asarray(mesh.devices).reshape(4, 4, 4, 4, 2), AXES)
    rows = P(AXES, None)
    in_specs = (rows,) * 8 + (P(SAMPLE, None), P(SAMPLE, None), P())
    out_specs = (rows,) * 4 + (P(SAMPLE, None), P())
    return jax.shard_map(
        on_device, mesh=fine, in_specs=in_specs, out_specs=out_specs, check_vma=False
    )
```

time: 181 us -> 181 us (level)
  the two profiles are of different devices: /device:TPU:1 before, /device:TPU:8 now
where the time goes in v5:
time: 181 us; the launch traced here: 179 us
  starting transfers between devices  60.2 us (33%)
  blocking collectives  45.9 us (25%)
  Pallas kernels  39.3 us (22%)
  waiting for transfers between devices  29.8 us (16%)
  local copies, waits for them, and re-layouts  2.66 us (1%)
    all_to_all x2, blocking collectives, swap(): return lax.all_to_all(array, axis, 0, 0, tiled=True)  45.9 us
    all_to_all x6, starting transfers between devices, swap(): return lax.all_to_all(array, axis, 0, 0, tiled=True)  37.1 us
    ppermute x4, starting transfers between devices, move(): return lax.ppermute(part, axis, [(i, (i + step) % 4) for i in range(4)])  21.2 us
    all_to_all x6, waiting for transfers between devices, swap(): return lax.all_to_all(array, axis, 0, 0, tiled=True)  18.7 us
    ppermute x4, waiting for transfers between devices, move(): return lax.ppermute(part, axis, [(i, (i + step) % 4) for i in range(4)])  11.1 us
    pallas_call x2, Pallas kernels, input_gradient(): pl.pallas_call(gradient_kernel, grid=(4,), in_specs=[whole((rows, width))...  11.1 us
    pallas_call x1, Pallas kernels, attend_forward(): pl.pallas_call(forward_kernel, grid=(KV_HEADS,), in_specs=[pl.BlockSpec(m...  8.35 us
    pallas_call x1, Pallas kernels, project(): pl.pallas_call(project_kernel, grid=(KV_HEADS,), in_specs=[whole((TOKENS,...  6.72 us
  transfers between devices with their start and end apart: 11, of which 8 were waited for; matrix products, arithmetic and copies ran while one was open for 0% of the time, Pallas kernels for 19%

profile of v5, /device:TPU:8, one launch (start us, length us, event | category | flops | bytes accessed | tf_op | source)
XLA Modules:
  0.0 179.5 jit_solution(10383036665378518660)
XLA Ops:
  0.7 0.9 copy-done
  1.5 0.7 pad_maximum_fusion.1
  2.3 30.2 %all_to_all.40.start_ref = bf16[4,144,128]{2,1,0:T(8,128)(2,1)} all-to-all(bf16[4,144,128]{2,1,0:T(8,128)(2,1)S(1)} %broadcast_in_dim.2), channel_id=1, replica_groups=mesh['x'=4,'zl'=4,'y'=4,'zh'=4,'c'=2] {'zh'}, dimensions={0} | all-to-all | bytes 294912 | tf_op jit(solution)/shard_map/all_to_all | solution.py:32
  32.5 2.4 %weight_copies.1 = bf16[16,528,128]{2,1,0:T(8,128)(2,1)} custom-call(bf16[4,144,128]{2,1,0:T(8,128)(2,1)} %all_to_all.40.start_ref), custom_call_target="tpu_custom_call" | custom-call | tf_op jit(solution)/shard_map/weight_copies/pallas_call | solution.py:406
  34.9 7.5 %all-to-all-start.2 = ((bf16[16,528,128]{2,1,0:T(8,128)(2,1)}), bf16[16,528,128]{2,1,0:T(8,128)(2,1)S(1)}, u32[]{:S(2)}, u32[]{:S(2)}) async-start(bf16[16,528,128]{2,1,0:T(8,128)(2,1)} %weight_copies.1), calls=%async_computation.2 | async-start | bytes 4325376 | tf_op jit(solution)/shard_map/all_to_all | solution.py:32
  42.5 2.5 %collective-permute-start.1 = (bf16[16,4608]{1,0:T(8,128)(2,1)S(1)}, bf16[16,4608]{1,0:T(8,128)(2,1)S(1)}, u32[]{:S(2)}, u32[]{:S(2)}) collective-permute-start(bf16[16,4608]{1,0:T(8,128)(2,1)S(1)} %pad_maximum_fusion.key_ref.prompt_ref), channel_id=1, source_target_pairs={{0,6},{2,0},{4,2},{6,4},{1,7},{3,1},{5,3},{7,5},{8,14},{10,8},{12,... | collective-permute-start | bytes 442376 | tf_op jit(solution)/shard_map/ppermute | solution.py:535
  45.0 7.2 %collective-permute-start = (bf16[16,4608]{1,0:T(8,128)(2,1)S(1)}, bf16[16,4608]{1,0:T(8,128)(2,1)S(1)}, u32[]{:S(2)}, u32[]{:S(2)}) collective-permute-start(bf16[16,4608]{1,0:T(8,128)(2,1)S(1)} %pad_maximum_fusion.key_ref.prompt_ref), channel_id=1, source_target_pairs={{0,2},{2,4},{4,6},{6,0},{1,3},{3,5},{5,7},{7,1},{8,10},{10,12},{12... | collective-permute-start | bytes 442376 | tf_op jit(solution)/shard_map/ppermute | solution.py:535
  52.3 5.9 %collective-permute-done.1.key3_ref.prompt3_ref = bf16[16,4608]{1,0:T(8,128)(2,1)S(1)} collective-permute-done((bf16[16,4608]{1,0:T(8,128)(2,1)S(1)}, bf16[16,4608]{1,0:T(8,128)(2,1)S(1)}, u32[]{:S(2)}, u32[]{:S(2)}) %collective-permute-start.1) | collective-permute-done | bytes 147488 | tf_op jit(solution)/shard_map/ppermute | solution.py:535
  58.2 4.3 %collective-permute-start.2 = (bf16[16,2560]{1,0:T(8,128)(2,1)S(1)}, bf16[16,2560]{1,0:T(8,128)(2,1)S(1)}, u32[]{:S(2)}, u32[]{:S(2)}) collective-permute-start(bf16[16,2560]{1,0:T(8,128)(2,1)S(1)} %slice.8), channel_id=1, source_target_pairs={{0,6},{2,0},{4,2},{6,4},{1,7},{3,1},{5,3},{7,5},{8,14},{10,8},{12,... | collective-permute-start | bytes 245768 | tf_op jit(solution)/shard_map/ppermute | solution.py:535
  62.5 0.8 collective-permute-done.key1_ref.prompt1_ref
  63.3 7.1 %collective-permute-start.3 = (bf16[16,2048]{1,0:T(8,128)(2,1)S(1)}, bf16[16,2048]{1,0:T(8,128)(2,1)S(1)}, u32[]{:S(2)}, u32[]{:S(2)}) collective-permute-start(bf16[16,2048]{1,0:T(8,128)(2,1)S(1)} %slice.9), channel_id=1, source_target_pairs={{0,2},{2,4},{4,6},{6,0},{1,3},{3,5},{5,7},{7,1},{8,10},{10,12},{12... | collective-permute-start | bytes 196616 | tf_op jit(solution)/shard_map/ppermute | solution.py:535
  70.5 4.4 %collective-permute-done.3.far_ref = bf16[16,2048]{1,0:T(8,128)(2,1)S(1)} collective-permute-done((bf16[16,2048]{1,0:T(8,128)(2,1)S(1)}, bf16[16,2048]{1,0:T(8,128)(2,1)S(1)}, u32[]{:S(2)}, u32[]{:S(2)}) %collective-permute-start.3) | collective-permute-done | bytes 65568 | tf_op jit(solution)/shard_map/ppermute | solution.py:535
  74.8 1.9 %collective-permute-start.4 = (bf16[16,528,128]{2,1,0:T(8,128)(2,1)S(1)}, bf16[16,528,128]{2,1,0:T(8,128)(2,1)}, u32[]{:S(2)}, u32[]{:S(2)}) collective-permute-start(bf16[16,528,128]{2,1,0:T(8,128)(2,1)S(1)} %all-to-all-done.2), channel_id=1, source_target_pairs={{0,1},{1,0},{2,3},{3,2},{4,5},{5,4},{6,7},{7,6},{8,9},{9,8},{10,11... | collective-permute-start | bytes 6488072 | tf_op jit(solution)/shard_map/ppermute | solution.py:565
  76.8 1.6 key_copies.1
  78.4 4.9 %all-to-all-start.1 = ((bf16[8,64,512]{2,1,0:T(8,128)(2,1)}), bf16[8,64,512]{2,1,0:T(8,128)(2,1)S(1)}, u32[]{:S(2)}, u32[]{:S(2)}) async-start(bf16[8,64,512]{2,1,0:T(8,128)(2,1)} %key_copies.1), calls=%async_computation.1 | async-start | bytes 1048576 | tf_op jit(solution)/shard_map/all_to_all | solution.py:32
  83.3 6.7 %project.1 = (bf16[128,512]{1,0:T(8,128)(2,1)}, bf16[8,64,512]{2,1,0:T(8,128)(2,1)}, bf16[16,4096]{1,0:T(8,128)(2,1)}) custom-call(bf16[128,4096]{1,0:T(8,128)(2,1)} %x_ref.3, bf16[16,4608]{1,0:T(8,128)(2,1)} %copy-done.1, bf16[16,4608]{1,0:T(8,128)(2,1)} %copy-done.5, bf16[16,2048]{1,0:T(8,128)(2,1)} %copy-done.11, bf16[16,2560]{1,0:T(8,128)(2,1)} %copy-done.8, ...), custom_call_target="tpu_custom_call" | custom-call | flops 600000000 | bytes 10485760 | tf_op jit(solution)/shard_map/project/pallas_call | solution.py:438
  90.1 2.1 %all-to-all-done.1.key_ref = bf16[8,64,512]{2,1,0:T(8,128)(2,1)S(1)} async-done(((bf16[8,64,512]{2,1,0:T(8,128)(2,1)}), bf16[8,64,512]{2,1,0:T(8,128)(2,1)S(1)}, u32[]{:S(2)}, u32[]{:S(2)}) %all-to-all-start.1) | async-done | bytes 524320 | tf_op jit(solution)/shard_map/all_to_all | solution.py:32
  92.2 4.9 %all-to-all-start.3 = ((bf16[8,64,512]{2,1,0:T(8,128)(2,1)}), bf16[8,64,512]{2,1,0:T(8,128)(2,1)S(1)}, u32[]{:S(2)}, u32[]{:S(2)}) async-start(bf16[8,64,512]{2,1,0:T(8,128)(2,1)} %get-tuple-element.44), calls=%async_computation.3 | async-start | bytes 1048576 | tf_op jit(solution)/shard_map/all_to_all | solution.py:32
  97.1 8.3 %attend_forward.1 = (bf16[8,64,512]{2,1,0:T(8,128)(2,1)}, bf16[128,512]{1,0:T(8,128)(2,1)}, f32[16,4096]{1,0:T(8,128)}, f32[16,512]{1,0:T(8,128)}, bf16[4,256,1024]{2,1,0:T(8,128)(2,1)}) custom-call(s32[1,8]{1,0:T(1,128)} %choice_ref.3, bf16[128,4096]{1,0:T(8,128)(2,1)} %q_ref.3, bf16[128,4096]{1,0:T(8,128)(2,1)} %cot_ref.3, bf16[8,64,512]{2,1,0:T(8,128)(2,1)} %copy-done.18, ...), custom_call_target="tpu_custom_call" | custom-call | flops 2000000000 | bytes 5242880 | tf_op jit(solution)/shard_map/attend_forward/pallas_call | solution.py:355
  106.0 4.8 %all-to-all-start.4 = ((bf16[8,64,512]{2,1,0:T(8,128)(2,1)}), bf16[8,64,512]{2,1,0:T(8,128)(2,1)S(1)}, u32[]{:S(2)}, u32[]{:S(2)}) async-start(bf16[8,64,512]{2,1,0:T(8,128)(2,1)} %get-tuple-element.48), calls=%async_computation.4 | async-start | bytes 1048576 | tf_op jit(solution)/shard_map/all_to_all | solution.py:32
  110.9 6.2 %attend_backward.1 = (bf16[8,64,512]{2,1,0:T(8,128)(2,1)}, bf16[128,512]{1,0:T(8,128)(2,1)}) custom-call(s32[1,8]{1,0:T(1,128)} %choice_ref.3, bf16[128,4096]{1,0:T(8,128)(2,1)} %q_ref.3, bf16[128,4096]{1,0:T(8,128)(2,1)} %cot_ref.3, bf16[4,256,1024]{2,1,0:T(8,128)(2,1)} %get-tuple-element.42.softmax_ref, bf16[8,64,512]{2,1,0:T(8,128)(2,1)} %copy-done.19, ...), custom_call_target="tpu_custom_call" | custom-call | flops 3000000000 | bytes 9437184 | tf_op jit(solution)/shard_map/attend_backward/pallas_call | solution.py:506
  117.1 2.6 %all-to-all-done.4.got_ref = bf16[8,64,512]{2,1,0:T(8,128)(2,1)S(1)} async-done(((bf16[8,64,512]{2,1,0:T(8,128)(2,1)}), bf16[8,64,512]{2,1,0:T(8,128)(2,1)S(1)}, u32[]{:S(2)}, u32[]{:S(2)}) %all-to-all-start.4) | async-done | bytes 524320 | tf_op jit(solution)/shard_map/all_to_all | solution.py:32
  119.8 1.0 copy-done.10
  121.5 15.7 %all_to_all.41.got_ref = bf16[8,96,512]{2,1,0:T(8,128)(2,1)S(1)} all-to-all(bf16[8,96,512]{2,1,0:T(8,128)(2,1)S(1)} %get-tuple-element.51), channel_id=1, replica_groups=mesh['x'=4,'zl'=4,'y'=4,'zh'=4,'c'=2] {'y','c'}, dimensions={0} | all-to-all | bytes 1572864 | tf_op jit(solution)/shard_map/all_to_all | solution.py:32
  137.2 0.8 keys_y.1
  138.0 8.4 %all-to-all-start.6 = ((bf16[4,208,128]{2,1,0:T(8,128)(2,1)}), bf16[4,208,128]{2,1,0:T(8,128)(2,1)S(1)}, u32[]{:S(2)}, u32[]{:S(2)}) async-start(bf16[4,208,128]{2,1,0:T(8,128)(2,1)} %keys_y.1), calls=%async_computation.6 | async-start | bytes 425984 | tf_op jit(solution)/shard_map/all_to_all | solution.py:32
  146.4 5.8 %input_gradient.2 = bf16[128,4096]{1,0:T(8,128)(2,1)} custom-call(bf16[128,512]{1,0:T(8,128)(2,1)} %get-tuple-element.53.low_ref, bf16[16,512]{1,0:T(8,128)(2,1)} %up_ref.9, bf16[16,4096]{1,0:T(8,128)(2,1)} %get-tuple-element.41.down_ref, bf16[4,4,528,128]{3,2,1,0:T(8,128)(2,1)} %bitcast.9, bf16[4,4,528,128]{3,2,1,0:T(8,128)(2,1)} %bitcast.10, ...), custom_call_target="tpu_custom_call" | custom-call | flops 536870912 | bytes 5242880 | tf_op jit(solution)/shard_map/input_gradient/pallas_call | solution.py:484
  152.2 8.6 %all-to-all-done.6.got_ref = bf16[4,208,128]{2,1,0:T(8,128)(2,1)S(1)} async-done(((bf16[4,208,128]{2,1,0:T(8,128)(2,1)}), bf16[4,208,128]{2,1,0:T(8,128)(2,1)S(1)}, u32[]{:S(2)}, u32[]{:S(2)}) %all-to-all-start.6) | async-done | bytes 213024 | tf_op jit(solution)/shard_map/all_to_all | solution.py:32
  160.8 0.8 keys_zh.1
  162.2 6.6 %all-to-all-start.7 = ((bf16[16,80,128]{2,1,0:T(8,128)(2,1)}), bf16[16,80,128]{2,1,0:T(8,128)(2,1)S(1)}, u32[]{:S(2)}, u32[]{:S(2)}) async-start(bf16[16,80,128]{2,1,0:T(8,128)(2,1)} %get-tuple-element.59), calls=%async_computation.7 | async-start | bytes 655360 | tf_op jit(solution)/shard_map/all_to_all | solution.py:32
  168.8 5.3 %input_gradient.3 = bf16[16,4096]{1,0:T(8,128)(2,1)} custom-call(bf16[16,512]{1,0:T(8,128)(2,1)} %copy-done.16, bf16[16,512]{1,0:T(8,128)(2,1)} %up_ref.9, bf16[16,4096]{1,0:T(8,128)(2,1)} %get-tuple-element.41.down_ref, bf16[4,4,528,128]{3,2,1,0:T(8,128)(2,1)} %bitcast.13, bf16[4,4,528,128]{3,2,1,0:T(8,128)(2,1)} %bitcast.14, ...), custom_call_target="tpu_custom_call" | custom-call | flops 67108864 | bytes 5242880 | tf_op jit(solution)/shard_map/input_gradient/pallas_call | solution.py:484
  174.1 4.7 %all-to-all-done.7.got_ref = bf16[16,80,128]{2,1,0:T(8,128)(2,1)S(1)} async-done(((bf16[16,80,128]{2,1,0:T(8,128)(2,1)}), bf16[16,80,128]{2,1,0:T(8,128)(2,1)S(1)}, u32[]{:S(2)}, u32[]{:S(2)}) %all-to-all-start.7) | async-done | bytes 327712 | tf_op jit(solution)/shard_map/all_to_all | solution.py:32
  (53 shorter events, 2.6 us)
Async XLA Ops:
  0.6 0.9 copy-start
  34.9 7.6 %copy-start.20 = (bf16[16,4096]{1,0:T(8,128)(2,1)S(1)}, bf16[16,4096]{1,0:T(8,128)(2,1)}, u32[]{:S(2)}) copy-start(bf16[16,4096]{1,0:T(8,128)(2,1)} %param.12) | copy-start | bytes 393220
  34.9 7.6 %copy-start.21 = (bf16[16,512]{1,0:T(8,128)(2,1)S(1)}, bf16[16,512]{1,0:T(8,128)(2,1)}, u32[]{:S(2)}) copy-start(bf16[16,512]{1,0:T(8,128)(2,1)} %param.15) | copy-start | bytes 49156
  34.9 39.9 %all-to-all-start.2 = ((bf16[16,528,128]{2,1,0:T(8,128)(2,1)}), bf16[16,528,128]{2,1,0:T(8,128)(2,1)S(1)}, u32[]{:S(2)}, u32[]{:S(2)}) async-start(bf16[16,528,128]{2,1,0:T(8,128)(2,1)} %weight_copies.1), calls=%async_computation.2 | async-start | bytes 4325376 | tf_op jit(solution)/shard_map/all_to_all | solution.py:32
  42.5 34.3 %copy-start.1 = (bf16[16,4608]{1,0:T(8,128)(2,1)}, bf16[16,4608]{1,0:T(8,128)(2,1)S(1)}, u32[]{:S(2)}) copy-start(bf16[16,4608]{1,0:T(8,128)(2,1)S(1)} %pad_maximum_fusion.key_ref.prompt_ref) | copy-start | bytes 442372
  42.5 15.7 %collective-permute-start.1 = (bf16[16,4608]{1,0:T(8,128)(2,1)S(1)}, bf16[16,4608]{1,0:T(8,128)(2,1)S(1)}, u32[]{:S(2)}, u32[]{:S(2)}) collective-permute-start(bf16[16,4608]{1,0:T(8,128)(2,1)S(1)} %pad_maximum_fusion.key_ref.prompt_ref), channel_id=1, source_target_pairs={{0,6},{2,0},{4,2},{6,4},{1,7},{3,1},{5,3},{7,5},{8,14},{10,8},{12,... | collective-permute-start | bytes 442376 | tf_op jit(solution)/shard_map/ppermute | solution.py:535
  45.0 18.3 %collective-permute-start = (bf16[16,4608]{1,0:T(8,128)(2,1)S(1)}, bf16[16,4608]{1,0:T(8,128)(2,1)S(1)}, u32[]{:S(2)}, u32[]{:S(2)}) collective-permute-start(bf16[16,4608]{1,0:T(8,128)(2,1)S(1)} %pad_maximum_fusion.key_ref.prompt_ref), channel_id=1, source_target_pairs={{0,2},{2,4},{4,6},{6,0},{1,3},{3,5},{5,7},{7,1},{8,10},{10,12},{12... | collective-permute-start | bytes 442376 | tf_op jit(solution)/shard_map/ppermute | solution.py:535
  58.2 18.6 %copy-start.3 = (bf16[16,4608]{1,0:T(8,128)(2,1)}, bf16[16,4608]{1,0:T(8,128)(2,1)S(1)}, u32[]{:S(2)}) copy-start(bf16[16,4608]{1,0:T(8,128)(2,1)S(1)} %collective-permute-done.1.key3_ref.prompt3_ref) | copy-start | bytes 442372
  58.2 16.6 %collective-permute-start.2 = (bf16[16,2560]{1,0:T(8,128)(2,1)S(1)}, bf16[16,2560]{1,0:T(8,128)(2,1)S(1)}, u32[]{:S(2)}, u32[]{:S(2)}) collective-permute-start(bf16[16,2560]{1,0:T(8,128)(2,1)S(1)} %slice.8), channel_id=1, source_target_pairs={{0,6},{2,0},{4,2},{6,4},{1,7},{3,1},{5,3},{7,5},{8,14},{10,8},{12,... | collective-permute-start | bytes 245768 | tf_op jit(solution)/shard_map/ppermute | solution.py:535
  63.3 13.5 %copy-start.5 = (bf16[16,4608]{1,0:T(8,128)(2,1)}, bf16[16,4608]{1,0:T(8,128)(2,1)S(1)}, u32[]{:S(2)}) copy-start(bf16[16,4608]{1,0:T(8,128)(2,1)S(1)} %collective-permute-done.key1_ref.prompt1_ref) | copy-start | bytes 442372
  63.3 11.5 %collective-permute-start.3 = (bf16[16,2048]{1,0:T(8,128)(2,1)S(1)}, bf16[16,2048]{1,0:T(8,128)(2,1)S(1)}, u32[]{:S(2)}, u32[]{:S(2)}) collective-permute-start(bf16[16,2048]{1,0:T(8,128)(2,1)S(1)} %slice.9), channel_id=1, source_target_pairs={{0,2},{2,4},{4,6},{6,0},{1,3},{3,5},{5,7},{7,1},{8,10},{10,12},{12... | collective-permute-start | bytes 196616 | tf_op jit(solution)/shard_map/ppermute | solution.py:535
  74.8 8.5 %copy-start.11 = (bf16[16,2048]{1,0:T(8,128)(2,1)}, bf16[16,2048]{1,0:T(8,128)(2,1)S(1)}, u32[]{:S(2)}) copy-start(bf16[16,2048]{1,0:T(8,128)(2,1)S(1)} %collective-permute-done.3.far_ref) | copy-start | bytes 196612
  74.8 2.0 %copy-start.8 = (bf16[16,2560]{1,0:T(8,128)(2,1)}, bf16[16,2560]{1,0:T(8,128)(2,1)S(1)}, u32[]{:S(2)}) copy-start(bf16[16,2560]{1,0:T(8,128)(2,1)S(1)} %collective-permute-done.2.key2_ref.far_rest_ref) | copy-start | bytes 245764
  74.8 8.5 %copy-start.17 = (bf16[16,528,128]{2,1,0:T(8,128)(2,1)}, bf16[16,528,128]{2,1,0:T(8,128)(2,1)S(1)}, u32[]{:S(2)}) copy-start(bf16[16,528,128]{2,1,0:T(8,128)(2,1)S(1)} %all-to-all-done.2) | copy-start | bytes 6488068
  74.8 8.5 %collective-permute-start.4 = (bf16[16,528,128]{2,1,0:T(8,128)(2,1)S(1)}, bf16[16,528,128]{2,1,0:T(8,128)(2,1)}, u32[]{:S(2)}, u32[]{:S(2)}) collective-permute-start(bf16[16,528,128]{2,1,0:T(8,128)(2,1)S(1)} %all-to-all-done.2), channel_id=1, source_target_pairs={{0,1},{1,0},{2,3},{3,2},{4,5},{5,4},{6,7},{7,6},{8,9},{9,8},{10,11... | collective-permute-start | bytes 6488072 | tf_op jit(solution)/shard_map/ppermute | solution.py:565
  78.4 13.8 %all-to-all-start.1 = ((bf16[8,64,512]{2,1,0:T(8,128)(2,1)}), bf16[8,64,512]{2,1,0:T(8,128)(2,1)S(1)}, u32[]{:S(2)}, u32[]{:S(2)}) async-start(bf16[8,64,512]{2,1,0:T(8,128)(2,1)} %key_copies.1), calls=%async_computation.1 | async-start | bytes 1048576 | tf_op jit(solution)/shard_map/all_to_all | solution.py:32
  92.2 4.9 %copy-start.18 = (bf16[8,64,512]{2,1,0:T(8,128)(2,1)}, bf16[8,64,512]{2,1,0:T(8,128)(2,1)S(1)}, u32[]{:S(2)}) copy-start(bf16[8,64,512]{2,1,0:T(8,128)(2,1)S(1)} %all-to-all-done.1.key_ref) | copy-start | bytes 1572868
  92.2 13.8 %all-to-all-start.3 = ((bf16[8,64,512]{2,1,0:T(8,128)(2,1)}), bf16[8,64,512]{2,1,0:T(8,128)(2,1)S(1)}, u32[]{:S(2)}, u32[]{:S(2)}) async-start(bf16[8,64,512]{2,1,0:T(8,128)(2,1)} %get-tuple-element.44), calls=%async_computation.3 | async-start | bytes 1048576 | tf_op jit(solution)/shard_map/all_to_all | solution.py:32
  106.0 4.9 %copy-start.19 = (bf16[8,64,512]{2,1,0:T(8,128)(2,1)}, bf16[8,64,512]{2,1,0:T(8,128)(2,1)S(1)}, u32[]{:S(2)}) copy-start(bf16[8,64,512]{2,1,0:T(8,128)(2,1)S(1)} %all-to-all-done.3.value_ref) | copy-start | bytes 1572868
  106.0 13.8 %all-to-all-start.4 = ((bf16[8,64,512]{2,1,0:T(8,128)(2,1)}), bf16[8,64,512]{2,1,0:T(8,128)(2,1)S(1)}, u32[]{:S(2)}, u32[]{:S(2)}) async-start(bf16[8,64,512]{2,1,0:T(8,128)(2,1)} %get-tuple-element.48), calls=%async_computation.4 | async-start | bytes 1048576 | tf_op jit(solution)/shard_map/all_to_all | solution.py:32
  110.8 8.9 %copy-start.2 = (bf16[16,4608]{1,0:T(8,128)(2,1)S(1)}, bf16[16,4608]{1,0:T(8,128)(2,1)}, u32[]{:S(2)}) copy-start(bf16[16,4608]{1,0:T(8,128)(2,1)} %copy-done.1) | copy-start | bytes 442372
  110.8 8.9 %copy-start.4 = (bf16[16,4608]{1,0:T(8,128)(2,1)S(1)}, bf16[16,4608]{1,0:T(8,128)(2,1)}, u32[]{:S(2)}) copy-start(bf16[16,4608]{1,0:T(8,128)(2,1)} %copy-done.3) | copy-start | bytes 442372
  110.9 8.9 %copy-start.6 = (bf16[16,4608]{1,0:T(8,128)(2,1)S(1)}, bf16[16,4608]{1,0:T(8,128)(2,1)}, u32[]{:S(2)}) copy-start(bf16[16,4608]{1,0:T(8,128)(2,1)} %copy-done.5) | copy-start | bytes 442372
  110.9 8.9 %copy-start.7 = (bf16[16,4096]{1,0:T(8,128)(2,1)S(1)}, bf16[16,4096]{1,0:T(8,128)(2,1)}, u32[]{:S(2)}) copy-start(bf16[16,4096]{1,0:T(8,128)(2,1)} %get-tuple-element.41.down_ref) | copy-start | bytes 393220
  110.9 8.9 %copy-start.9 = (bf16[16,2560]{1,0:T(8,128)(2,1)S(1)}, bf16[16,2560]{1,0:T(8,128)(2,1)}, u32[]{:S(2)}) copy-start(bf16[16,2560]{1,0:T(8,128)(2,1)} %copy-done.8) | copy-start | bytes 245764
  110.9 8.9 %copy-start.12 = (bf16[16,2048]{1,0:T(8,128)(2,1)S(1)}, bf16[16,2048]{1,0:T(8,128)(2,1)}, u32[]{:S(2)}) copy-start(bf16[16,2048]{1,0:T(8,128)(2,1)} %copy-done.11) | copy-start | bytes 196612
  110.9 8.9 %copy-start.13 = (f32[16,4096]{1,0:T(8,128)S(1)}, f32[16,4096]{1,0:T(8,128)}, u32[]{:S(2)}) copy-start(f32[16,4096]{1,0:T(8,128)} %get-tuple-element.49.grad_ref) | copy-start | bytes 786436
  110.9 8.9 %copy-start.14 = (bf16[16,512]{1,0:T(8,128)(2,1)S(1)}, bf16[16,512]{1,0:T(8,128)(2,1)}, u32[]{:S(2)}) copy-start(bf16[16,512]{1,0:T(8,128)(2,1)} %up_ref.9) | copy-start | bytes 49156
  110.9 8.9 %copy-start.15 = (f32[16,512]{1,0:T(8,128)S(1)}, f32[16,512]{1,0:T(8,128)}, u32[]{:S(2)}) copy-start(f32[16,512]{1,0:T(8,128)} %get-tuple-element.50.second_ref) | copy-start | bytes 98308
  119.8 1.0 copy-start.10
  138.0 22.8 %all-to-all-start.6 = ((bf16[4,208,128]{2,1,0:T(8,128)(2,1)}), bf16[4,208,128]{2,1,0:T(8,128)(2,1)S(1)}, u32[]{:S(2)}, u32[]{:S(2)}) async-start(bf16[4,208,128]{2,1,0:T(8,128)(2,1)} %keys_y.1), calls=%async_computation.6 | async-start | bytes 425984 | tf_op jit(solution)/shard_map/all_to_all | solution.py:32
  162.2 16.6 %all-to-all-start.7 = ((bf16[16,80,128]{2,1,0:T(8,128)(2,1)}), bf16[16,80,128]{2,1,0:T(8,128)(2,1)S(1)}, u32[]{:S(2)}, u32[]{:S(2)}) async-start(bf16[16,80,128]{2,1,0:T(8,128)(2,1)} %get-tuple-element.59), calls=%async_computation.7 | async-start | bytes 655360 | tf_op jit(solution)/shard_map/all_to_all | solution.py:32
  (1 other events, 0.6 us)

commit v6 on v4

--- a/solution.py
+++ b/solution.py
@@ -53,6 +53,24 @@
     return jnp.concatenate([jnp.where(chosen == p, rows, zero) for p in range(PROMPTS)], axis=1)
 
 
+def chosen_of(segment_ref, choice_ref, chosen_ref):
+    segment = segment_ref[...]
+    prompt = jnp.zeros_like(segment)
+    for i in range(choice_ref.shape[1]):
+        prompt = jnp.where(segment == i, choice_ref[0, i], prompt)
+    chosen_ref[...] = jnp.broadcast_to(
+        jnp.concatenate([prompt, prompt], axis=1), (HEAD_DIM, PAIR)
+    ).T
+
+
+def own_bias(segment_ref):
+    segment = jnp.broadcast_to(segment_ref[...], (TOKENS, TOKENS))
+    row = lax.broadcasted_iota(jnp.int32, (TOKENS, TOKENS), 0)
+    column = lax.broadcasted_iota(jnp.int32, (TOKENS, TOKENS), 1)
+    bias = jnp.where((segment.T == segment) & (row <= column), 0.0, -1e30).astype(F32)
+    return jnp.concatenate([bias, bias], axis=1)
+
+
 def pair_rows(ref, pair):
     first = 2 * pair * HEAD_DIM
     return jnp.concatenate(
@@ -109,15 +127,21 @@
 
 
 def forward_kernel(
-    q_ref, cot_ref, key_ref, own_key_ref, chosen_ref, bias_ref, x_ref, up_ref, down_ref,
+    choice_ref, q_ref, cot_ref, key_ref, own_key_ref, segment_ref, x_ref, up_ref, down_ref,
     send_ref, low_ref, back_ref, grad_ref, second_ref, softmax_ref,
-    probs, own_probs, cots, back, first,
+    probs, own_probs, cots, back, first, chosen_rows, bias_rows,
 ):
     k = pl.program_id(0)
     key_cat = prompt_block(key_ref)
     own_key = own_key_ref[...]
-    chosen = chosen_ref[...]
-    bias = bias_ref[...]
+
+    @pl.when(k == 0)
+    def _():
+        chosen_of(segment_ref, choice_ref, chosen_rows)
+        bias_rows[...] = own_bias(segment_ref)
+
+    chosen = chosen_rows[...]
+    bias = bias_rows[...]
     for pair in range(GROUP_SIZE // 2):
         rows = pair_rows(q_ref, pair)
         seen, own = softmax_pair(key_cat, own_key, expand(rows, chosen), rows, bias)
@@ -147,12 +171,25 @@
         grad_ref[...] = nn(back_ref[...], x_ref[...])
 
 
+def weight_copies_kernel(start_ref, send_ref, part, sems):
+    for zh in range(4):
+        part[zh * 128 : (zh + 1) * 128, :] = start_ref[zh, :128, :]
+    part[512:, :] = start_ref[lax.axis_index("x"), 128:144, :]
+    copies = [
+        pltpu.make_async_copy(part, send_ref.at[i], sems.at[i]) for i in range(send_ref.shape[0])
+    ]
+    for copy in copies:
+        copy.start()
+    for copy in copies:
+        copy.wait()
+
+
 def place_before(place, step):
     return lax.rem(place + (4 - step), 4)
 
 
 def adapter_kernel(
-    place_ref, keys_ref, got_ref, grad_ref, second_ref, up_ref, down_ref,
+    keys_ref, got_ref, grad_ref, second_ref, up_ref, down_ref,
     prompt_ref, prompt1_ref, prompt2_ref, prompt3_ref,
     part_ref, send_ref,
     total,
@@ -168,7 +205,7 @@
     prompt_back = jnp.zeros((RANK, 64), F32)
     for k in range(KV_HEADS):
         at = slice(k * HEAD_DIM, (k + 1) * HEAD_DIM)
-        starts = [place_before(place_ref[2], step) * 64 + k * 16 for step in range(4)]
+        starts = [place_before(lax.axis_index("zh"), step) * 64 + k * 16 for step in range(4)]
         low = jnp.concatenate(
             [total[pl.ds(pl.multiple_of(row, 16), 16), :] for row in starts], axis=0
         )
@@ -184,8 +221,8 @@
 
 
 def project_kernel(
-    place_ref, x_ref, prompt_ref, prompt1_ref, prompt2_ref, prompt3_ref,
-    weight_ref, other_ref, up_ref,
+    x_ref, prompt_ref, prompt1_ref, prompt2_ref, prompt3_ref,
+    weight_ref, other_ref, up_ref, factor_ref, other_factor_ref,
     values_ref, send_ref, weight_out_ref, down_ref,
     rows, first,
 ):
@@ -198,21 +235,21 @@
             rows[TOKENS + step * 16 : TOKENS + (step + 1) * 16, :] = ref[...]
         for y in range(4):
             for zh in range(4):
-                for ref, c in ((weight_ref, place_ref[3]), (other_ref, 1 - place_ref[3])):
+                for ref, c in ((factor_ref, lax.axis_index("c")), (other_factor_ref, 1 - lax.axis_index("c"))):
                     at = pl.multiple_of(((y * 4 + zh) * 2 + c) * 128, 128)
-                    down_ref[:, pl.ds(at, 128)] = ref[0, y, zh, 128:, :]
+                    down_ref[:, pl.ds(at, 128)] = ref[zh, y]
         first[...] = nt(rows[...], down_ref[...]).astype(BF16)
 
     for y in range(4):
         for zh in range(4):
-            for ref, c in ((weight_ref, place_ref[3]), (other_ref, 1 - place_ref[3])):
+            for ref, c in ((weight_ref, lax.axis_index("c")), (other_ref, 1 - lax.axis_index("c"))):
                 row = pl.multiple_of(((y * 4 + zh) * 2 + c) * 128, 128)
-                weight_out_ref[pl.ds(row, 128), :] = ref[0, y, zh, :128, :]
+                weight_out_ref[pl.ds(row, 128), :] = ref[0, y, zh * 128 : (zh + 1) * 128, :]
     values = nn(rows[...], weight_out_ref[...]) + ADAPTER_SCALE * nn(first[...], up_ref[...])
     values = values.astype(BF16)
     values_ref[...] = values[:TOKENS]
     for step in range(4):
-        row = place_before(place_ref[2], step) * 64 + k * 16
+        row = place_before(lax.axis_index("zh"), step) * 64 + k * 16
         part = values[TOKENS + step * 16 : TOKENS + (step + 1) * 16]
         for owner in range(8):
             send_ref[owner, pl.ds(pl.multiple_of(row, 16), 16), :] = part
@@ -279,14 +316,19 @@
 
 
 def backward_kernel(
-    q_ref, cot_ref, softmax_ref, value_ref, own_value_ref, chosen_ref,
+    choice_ref, q_ref, cot_ref, softmax_ref, value_ref, own_value_ref, segment_ref,
     send_ref, own_ref,
-    grads, own_grads, queries,
+    grads, own_grads, queries, chosen_rows,
 ):
     k = pl.program_id(0)
     value_cat = value_block(value_ref, k)
     own_value = own_value_ref[...]
-    chosen = chosen_ref[...]
+
+    @pl.when(k == 0)
+    def _():
+        chosen_of(segment_ref, choice_ref, chosen_rows)
+
+    chosen = chosen_rows[...]
     for pair in range(GROUP_SIZE // 2):
         rows = pair_rows(q_ref, pair)
         at = pl.ds(pair * PAIR, PAIR)
@@ -322,17 +364,17 @@
 PARAMS = pltpu.CompilerParams(vmem_limit_bytes=56 << 20, dimension_semantics=("arbitrary",))
 
 
-def attend_forward(queries, cotangent, keys, own_keys, chosen, bias, rows, up, down):
+def attend_forward(choice, queries, cotangent, keys, own_keys, segments, rows, up, down):
     return pl.pallas_call(
         forward_kernel,
         grid=(KV_HEADS,),
         in_specs=[
+            pl.BlockSpec(memory_space=pltpu.SMEM),
             heads_of(TOKENS, WIDE),
             heads_of(TOKENS, WIDE),
             PROMPT_SPEC,
             heads_of(TOKENS, HEAD_DIM),
-            whole((PAIR, HEAD_DIM)),
-            whole((TOKENS, PAIR)),
+            whole((1, TOKENS)),
             whole((TOKENS, D)),
             heads_of(RANK, HEAD_DIM),
             whole((RANK, D)),
@@ -359,66 +401,79 @@
             pltpu.VMEM((ROWS, (PROMPTS + 1) * HEAD_DIM), BF16),
             pltpu.VMEM((RANK, TOKENS), F32),
             pltpu.VMEM((TOKENS, RANK), BF16),
+            pltpu.VMEM((PAIR, HEAD_DIM), jnp.int32),
+            pltpu.VMEM((TOKENS, PAIR), F32),
         ],
         compiler_params=PARAMS,
         cost_estimate=pl.CostEstimate(
             flops=2_000_000_000, bytes_accessed=5 << 20, transcendentals=1 << 20
         ),
         name="attend_forward",
-    )(queries, cotangent, keys, own_keys, chosen, bias, rows, up, down)
-
-
-def adapter_terms(place, keys, got, grad, second, up, down, prompts):
+    )(choice, queries, cotangent, keys, own_keys, segments, rows, up, down)
+
+
+def adapter_terms(keys, got, grad, second, up, down, prompts):
     vmem = pl.BlockSpec(memory_space=pltpu.VMEM)
     return pl.pallas_call(
         adapter_kernel,
-        in_specs=[pl.BlockSpec(memory_space=pltpu.SMEM)] + [vmem] * 10,
+        in_specs=[vmem] * 10,
         out_specs=[vmem] * 2,
         out_shape=[sent(4, 64, HEAD_DIM), sent(8, 384, HEAD_DIM)],
         scratch_shapes=[pltpu.VMEM((256, HEAD_DIM), BF16)],
         compiler_params=pltpu.CompilerParams(vmem_limit_bytes=24 << 20),
         name="adapter_terms",
-    )(place, keys, got, grad, second, up, down, *prompts)
-
-
-def project(place, rows, prompts, weight, other, up):
+    )(keys, got, grad, second, up, down, *prompts)
+
+
+def weight_copies(start):
+    return pl.pallas_call(
+        weight_copies_kernel,
+        in_specs=[pl.BlockSpec(memory_space=pltpu.VMEM)],
+        out_specs=pl.BlockSpec(memory_space=pl.ANY),
+        out_shape=sent(16, 528, HEAD_DIM),
+        scratch_shapes=[pltpu.VMEM((528, HEAD_DIM), BF16), pltpu.SemaphoreType.DMA((16,))],
+        name="weight_copies",
+    )(start)
+
+
+def project(rows, prompts, weight, other, up):
     width = KV_HEADS * HEAD_DIM
 
     def const(*shape):
-        return pl.BlockSpec(shape, lambda k, place: (0,) * len(shape))
+        return pl.BlockSpec(shape, lambda k: (0,) * len(shape))
 
     def head(rows):
-        return pl.BlockSpec((rows, HEAD_DIM), lambda k, place: (0, k))
-
-    block = pl.BlockSpec((1, 4, 4, 144, HEAD_DIM), lambda k, place: (k, 0, 0, 0, 0))
+        return pl.BlockSpec((rows, HEAD_DIM), lambda k: (0, k))
+
+    block = pl.BlockSpec((1, 4, 512, HEAD_DIM), lambda k: (k, 0, 0, 0))
+    factor = pl.BlockSpec((4, 4, RANK, HEAD_DIM), lambda k: (0, 0, 512 // RANK, 0))
     return pl.pallas_call(
         project_kernel,
-        grid_spec=pltpu.PrefetchScalarGridSpec(
-            num_scalar_prefetch=1,
-            grid=(KV_HEADS,),
-            in_specs=[
-                const(TOKENS, D),
-                const(16, D),
-                const(16, D),
-                const(16, D),
-                const(16, D),
-                block,
-                block,
-                head(RANK),
-            ],
-            out_specs=[head(TOKENS), const(8, 256, HEAD_DIM), head(D), const(RANK, D)],
-            scratch_shapes=[
-                pltpu.VMEM((TOKENS + 64, D), BF16),
-                pltpu.VMEM((TOKENS + 64, RANK), BF16),
-            ],
-        ),
+        grid=(KV_HEADS,),
+        in_specs=[
+            const(TOKENS, D),
+            const(16, D),
+            const(16, D),
+            const(16, D),
+            const(16, D),
+            block,
+            block,
+            head(RANK),
+            factor,
+            factor,
+        ],
+        out_specs=[head(TOKENS), const(8, 256, HEAD_DIM), head(D), const(RANK, D)],
+        scratch_shapes=[
+            pltpu.VMEM((TOKENS + 64, D), BF16),
+            pltpu.VMEM((TOKENS + 64, RANK), BF16),
+        ],
         out_shape=[sent(TOKENS, width), sent(8, 256, HEAD_DIM), sent(D, width), sent(RANK, D)],
         compiler_params=PARAMS,
         cost_estimate=pl.CostEstimate(
             flops=600_000_000, bytes_accessed=10 << 20, transcendentals=0
         ),
         name="project",
-    )(place, rows, *prompts, weight, other, up)
+    )(rows, *prompts, weight, other, up, weight, other)
 
 
 def prompt_gradient(low, up, down, weight):
@@ -440,17 +495,18 @@
     )(low, up, down, weight)
 
 
-def attend_backward(queries, cotangent, softmax, values, own_values, chosen):
+def attend_backward(choice, queries, cotangent, softmax, values, own_values, segments):
     return pl.pallas_call(
         backward_kernel,
         grid=(KV_HEADS,),
         in_specs=[
+            pl.BlockSpec(memory_space=pltpu.SMEM),
             heads_of(TOKENS, WIDE),
             heads_of(TOKENS, WIDE),
             pl.BlockSpec((1, 2 * TOKENS, ROWS), lambda k: (k, 0, 0)),
             whole((8, 256, HEAD_DIM)),
             heads_of(TOKENS, HEAD_DIM),
-            whole((PAIR, HEAD_DIM)),
+            whole((1, TOKENS)),
         ],
         out_specs=[whole((8, 256, HEAD_DIM)), heads_of(TOKENS, HEAD_DIM)],
         out_shape=[sent(8, 256, HEAD_DIM), sent(TOKENS, KV_HEADS * HEAD_DIM)],
@@ -458,13 +514,14 @@
             pltpu.VMEM((TOKENS, ROWS), BF16),
             pltpu.VMEM((TOKENS, ROWS), BF16),
             pltpu.VMEM((ROWS, (PROMPTS + 1) * HEAD_DIM), BF16),
+            pltpu.VMEM((PAIR, HEAD_DIM), jnp.int32),
         ],
         compiler_params=PARAMS,
         cost_estimate=pl.CostEstimate(
             flops=3_000_000_000, bytes_accessed=9 << 20, transcendentals=0
         ),
         name="attend_backward",
-    )(queries, cotangent, softmax, values, own_values, chosen)
+    )(choice, queries, cotangent, softmax, values, own_values, segments)
 
 
 def heads_first(rows):
@@ -492,22 +549,13 @@
     value_adapter_down,
     value_adapter_up,
 ):
-    segments = segment_index.reshape(TOKENS)
-    onehot = (segments[:, None] == jnp.arange(8, dtype=jnp.int32)[None, :]).astype(jnp.int32)
-    token_prompt = jnp.sum(onehot * prompt_choice.reshape(1, 8), axis=1)
-    chosen = jnp.broadcast_to(jnp.tile(token_prompt, 2)[:, None], (PAIR, HEAD_DIM))
-    position = jnp.arange(TOKENS, dtype=jnp.int32)
-    own_seen = (segments[:, None] == segments[None, :]) & (position[:, None] <= position[None, :])
-    bias = jnp.tile(jnp.where(own_seen, 0.0, -1e30).astype(F32), (1, 2))
-
     own_columns = lax.dynamic_slice_in_dim(
         frozen_value_weight, lax.axis_index("x") * HEAD_DIM, HEAD_DIM, 1
     )
     start = gather(
         jnp.concatenate([own_columns, value_adapter_down.T, heads_first(prompt_keys)], axis=0), "zh"
     )
-    place = jnp.stack([lax.axis_index(axis) for axis in ("x", "y", "zh", "c")]).astype(jnp.int32)
-    weight = gather(start[:, :144], ("x", "y")).reshape(4, 4, 4, 144, HEAD_DIM)
+    weight = swap(weight_copies(start), ("x", "y")).reshape(4, 4, 528, HEAD_DIM)
     before, behind = lax.optimization_barrier((prompt_rows, prompt_rows, start))[:2]
     before, behind = move(before, "zh", 1), move(behind, "zh", 3)
     prompts = [prompt_rows, before, move(before, "zh", 1), behind]
@@ -515,19 +563,19 @@
     key_all = gather(after(start[:, 144:], weight), OWNERS).reshape(4, 2, 4, 64, HEAD_DIM)
 
     values, part, weight, down = project(
-        place, response_rows, prompts, weight, other, value_adapter_up
+        response_rows, prompts, weight, other, value_adapter_up
     )
     value_all = swap(after(part, key_all), OWNERS)
     send, low, back, token_grad, token_second, softmax = attend_forward(
-        queries, cotangent, key_all, response_keys, chosen, bias, response_rows, value_adapter_up,
-        down,
+        prompt_choice, queries, cotangent, key_all, response_keys, segment_index, response_rows,
+        value_adapter_up, down,
     )
     got = swap(after(send, value_all), OWNERS)
     key_send, own_key_grad = attend_backward(
-        queries, cotangent, softmax, value_all, values, chosen
+        prompt_choice, queries, cotangent, softmax, value_all, values, segment_index
     )
     value_part, key_send = adapter_terms(
-        place, key_send, got, token_grad, token_second, value_adapter_up, down, prompts
+        key_send, got, token_grad, token_second, value_adapter_up, down, prompts
     )
     part = in_vmem(keys_y_kernel, 2, sent(4, 208, HEAD_DIM), "keys_y")(
         swap(key_send, OWNERS), value_part

time: 181 us -> 178 us (0.983); the launches traced: 178 us -> 177 us
  waiting for transfers between devices: 25.7 us -> 30.9 us
  local copies, waits for them, and re-layouts: 6.95 us -> 3.58 us
  starting transfers between devices: 61.6 us -> 58.9 us
    all_to_all x6, waiting for transfers between devices: 16.4 us -> 21.6 us  [swap(): return lax.all_to_all(array, axis, 0, 0, tiled=True)]
    all_to_all x6, starting transfers between devices: 31.8 us -> 28.8 us  [swap(): return lax.all_to_all(array, axis, 0, 0, tiled=True)]
    broadcast_in_dim x3 -> x2, local copies, waits for them, and re-layouts: 2.82 us -> 0.94 us  [gather(): return swap(jnp.broadcast_to(array[None], (n,) + array.shape), axis)]
    pallas_call x4 -> x5, Pallas kernels: 24.7 us -> 25.9 us  [the longest x1 8.63 us: attend_forward(): pl.pallas_call(forward_kernel, grid=(KV_HEADS,), in_specs=[pl.BlockSpec(m...]
  transfers between devices with their start and end apart: 10 -> 10, of which waited for: 7 -> 7; matrix products, arithmetic and copies ran while one was open for 5% -> 3% of each run, Pallas kernels for 16% -> 15%
where the time goes in v6:
time: 178 us; the launch traced here: 177 us
  starting transfers between devices  58.9 us (33%)
  blocking collectives  44.3 us (25%)
  Pallas kernels  32.9 us (18%)
  waiting for transfers between devices  30.9 us (17%)
  matrix products  5.1 us (3%)
  local copies, waits for them, and re-layouts  3.58 us (2%)
    all_to_all x2, blocking collectives, swap(): return lax.all_to_all(array, axis, 0, 0, tiled=True)  44.3 us
    all_to_all x6, starting transfers between devices, swap(): return lax.all_to_all(array, axis, 0, 0, tiled=True)  28.8 us
    all_to_all x6, waiting for transfers between devices, swap(): return lax.all_to_all(array, axis, 0, 0, tiled=True)  21.6 us
    ppermute x3, starting transfers between devices, move(): return lax.ppermute(part, axis, [(i, (i + step) % 4) for i in range(4)])  16.1 us
    ppermute x1, starting transfers between devices, on_device(): other = lax.ppermute(after(weight, *prompts), 'c', [(0, 1), (1, 0)])  14.1 us
    ppermute x3, waiting for transfers between devices, move(): return lax.ppermute(part, axis, [(i, (i + step) % 4) for i in range(4)])  9.3 us
    pallas_call x1, Pallas kernels, attend_forward(): pl.pallas_call(forward_kernel, grid=(KV_HEADS,), in_specs=[pl.BlockSpec(m...  8.63 us
    pallas_call x1, Pallas kernels, attend_backward(): pl.pallas_call(backward_kernel, grid=(KV_HEADS,), in_specs=[pl.BlockSpec(...  7.16 us
  transfers between devices with their start and end apart: 10, of which 7 were waited for; matrix products, arithmetic and copies ran while one was open for 3% of the time, Pallas kernels for 15%

profile of v6, /device:TPU:1, one launch (start us, length us, event | category | flops | bytes accessed | tf_op | source)
XLA Modules:
  0.0 177.2 jit_solution(15622582530820802662)
XLA Ops:
  0.7 0.8 copy_bitcast_fusion
  1.6 0.7 pad_maximum_fusion
  2.3 28.8 %all_to_all.40.start_ref = bf16[4,208,128]{2,1,0:T(8,128)(2,1)} all-to-all(bf16[4,208,128]{2,1,0:T(8,128)(2,1)S(1)} %broadcast_in_dim.4), channel_id=1, replica_groups=mesh['x'=4,'zl'=4,'y'=4,'zh'=4,'c'=2] {'zh'}, dimensions={0} | all-to-all | bytes 425984 | tf_op jit(solution)/shard_map/all_to_all | solution.py:31
  31.1 2.4 %weight_copies.1 = bf16[16,528,128]{2,1,0:T(8,128)(2,1)} custom-call(bf16[4,208,128]{2,1,0:T(8,128)(2,1)} %all_to_all.40.start_ref), custom_call_target="tpu_custom_call" | custom-call | tf_op jit(solution)/shard_map/weight_copies/pallas_call | solution.py:429
  33.5 6.9 %all-to-all-start.1 = ((bf16[16,528,128]{2,1,0:T(8,128)(2,1)}), bf16[16,528,128]{2,1,0:T(8,128)(2,1)S(1)}, u32[]{:S(2)}, u32[]{:S(2)}) async-start(bf16[16,528,128]{2,1,0:T(8,128)(2,1)} %weight_copies.1), calls=%async_computation.1 | async-start | bytes 4325376 | tf_op jit(solution)/shard_map/all_to_all | solution.py:31
  40.5 5.5 %collective-permute-start = (bf16[16,4096]{1,0:T(8,128)(2,1)S(1)}, bf16[16,4096]{1,0:T(8,128)(2,1)S(1)}, u32[]{:S(2)}, u32[]{:S(2)}) collective-permute-start(bf16[16,4096]{1,0:T(8,128)(2,1)S(1)} %copy-done.2), channel_id=1, source_target_pairs={{0,2},{2,4},{4,6},{6,0},{1,3},{3,5},{5,7},{7,1},{8,10},{10,12},{12... | collective-permute-start | bytes 393224 | tf_op jit(solution)/shard_map/ppermute | solution.py:532
  45.9 3.7 %collective-permute-start.2 = (bf16[16,4096]{1,0:T(8,128)(2,1)S(1)}, bf16[16,4096]{1,0:T(8,128)(2,1)S(1)}, u32[]{:S(2)}, u32[]{:S(2)}) collective-permute-start(bf16[16,4096]{1,0:T(8,128)(2,1)S(1)} %copy-done.2), channel_id=1, source_target_pairs={{0,6},{2,0},{4,2},{6,4},{1,7},{3,1},{5,3},{7,5},{8,14},{10,8},{12,... | collective-permute-start | bytes 393224 | tf_op jit(solution)/shard_map/ppermute | solution.py:532
  50.2 6.9 %collective-permute-start.1 = (bf16[16,4096]{1,0:T(8,128)(2,1)S(1)}, bf16[16,4096]{1,0:T(8,128)(2,1)S(1)}, u32[]{:S(2)}, u32[]{:S(2)}) collective-permute-start(bf16[16,4096]{1,0:T(8,128)(2,1)S(1)} %collective-permute-done.prompt1_ref), channel_id=1, source_target_pairs={{0,2},{2,4},{4,6},{6,0},{1,3},{3,5},{5,7},{7,1},{8,10},{10,12},{12... | collective-permute-start | bytes 393224 | tf_op jit(solution)/shard_map/ppermute | solution.py:532
  57.1 8.8 %collective-permute-done.1.prompt2_ref = bf16[16,4096]{1,0:T(8,128)(2,1)S(1)} collective-permute-done((bf16[16,4096]{1,0:T(8,128)(2,1)S(1)}, bf16[16,4096]{1,0:T(8,128)(2,1)S(1)}, u32[]{:S(2)}, u32[]{:S(2)}) %collective-permute-start.1) | collective-permute-done | bytes 131104 | tf_op jit(solution)/shard_map/ppermute | solution.py:532
  65.9 14.1 %collective-permute-start.3 = (bf16[4,4,528,128]{3,2,1,0:T(8,128)(2,1)S(1)}, bf16[4,4,528,128]{3,2,1,0:T(8,128)(2,1)}, u32[]{:S(2)}, u32[]{:S(2)}) collective-permute-start(bf16[4,4,528,128]{3,2,1,0:T(8,128)(2,1)S(1)} %bitcast.16), channel_id=1, source_target_pairs={{0,1},{1,0},{2,3},{3,2},{4,5},{5,4},{6,7},{7,6},{8,9},{9,8},{10,11... | collective-permute-start | bytes 6488072 | tf_op jit(solution)/shard_map/ppermute | solution.py:562
  80.0 0.9 broadcast_in_dim.5
  80.9 4.0 %all-to-all-start.2 = ((bf16[8,4,64,128]{3,2,1,0:T(8,128)(2,1)}), bf16[8,4,64,128]{3,2,1,0:T(8,128)(2,1)S(1)}, u32[]{:S(2)}, u32[]{:S(2)}) async-start(bf16[8,4,64,128]{3,2,1,0:T(8,128)(2,1)} %broadcast_in_dim.5), calls=%async_computation.2 | async-start | bytes 1048576 | tf_op jit(solution)/shard_map/all_to_all | solution.py:31
  84.9 6.8 %project.1 = (bf16[128,512]{1,0:T(8,128)(2,1)}, bf16[8,256,128]{2,1,0:T(8,128)(2,1)}, bf16[4096,512]{1,0:T(8,128)(2,1)}, bf16[16,4096]{1,0:T(8,128)(2,1)}) custom-call(bf16[128,4096]{1,0:T(8,128)(2,1)} %x_ref.3, bf16[16,4096]{1,0:T(8,128)(2,1)} %prompt_ref.3, bf16[16,4096]{1,0:T(8,128)(2,1)} %copy-done.4, bf16[16,4096]{1,0:T(8,128)(2,1)} %copy-done.8, ...), custom_call_target="tpu_custom_call" | custom-call | flops 600000000 | bytes 10485760 | tf_op jit(solution)/shard_map/project/pallas_call | solution.py:450
  91.7 2.6 %all-to-all-done.2 = bf16[8,4,64,128]{3,2,1,0:T(8,128)(2,1)S(1)} async-done(((bf16[8,4,64,128]{3,2,1,0:T(8,128)(2,1)}), bf16[8,4,64,128]{3,2,1,0:T(8,128)(2,1)S(1)}, u32[]{:S(2)}, u32[]{:S(2)}) %all-to-all-start.2) | async-done | bytes 524320 | tf_op jit(solution)/shard_map/all_to_all | solution.py:31
  94.3 4.3 %all-to-all-start.3 = ((bf16[8,256,128]{2,1,0:T(8,128)(2,1)}), bf16[8,256,128]{2,1,0:T(8,128)(2,1)S(1)}, u32[]{:S(2)}, u32[]{:S(2)}) async-start(bf16[8,256,128]{2,1,0:T(8,128)(2,1)} %get-tuple-element.40), calls=%async_computation.3 | async-start | bytes 1048576 | tf_op jit(solution)/shard_map/all_to_all | solution.py:31
  98.6 8.6 %attend_forward.1 = (bf16[8,256,128]{2,1,0:T(8,128)(2,1)}, bf16[128,512]{1,0:T(8,128)(2,1)}, bf16[16,128]{1,0:T(8,128)(2,1)}, f32[16,4096]{1,0:T(8,128)}, f32[16,512]{1,0:T(8,128)}, /*index=5*/f32[4,256,1024]{2,1,0:T(8,128)}) custom-call(s32[1,8]{1,0:T(1,128)} %choice_ref.3, bf16[128,4096]{1,0:T(8,128)(2,1)} %q_ref.3, bf16[128,4096]{1,0:T(8,128)(2,1)} %cot_ref.3, ...), custom_call_target="tpu_custom_call" | custom-call | flops 2000000000 | bytes 5242880 | tf_op jit(solution)/shard_map/attend_forward/pallas_call | solution.py:368
  107.2 0.9 all-to-all-done.3.value_ref
  108.1 4.3 %all-to-all-start.4 = ((bf16[8,256,128]{2,1,0:T(8,128)(2,1)}), bf16[8,256,128]{2,1,0:T(8,128)(2,1)S(1)}, u32[]{:S(2)}, u32[]{:S(2)}) async-start(bf16[8,256,128]{2,1,0:T(8,128)(2,1)} %get-tuple-element.44), calls=%async_computation.4 | async-start | bytes 1048576 | tf_op jit(solution)/shard_map/all_to_all | solution.py:31
  112.5 7.2 %attend_backward.1 = (bf16[8,256,128]{2,1,0:T(8,128)(2,1)}, bf16[128,512]{1,0:T(8,128)(2,1)}) custom-call(s32[1,8]{1,0:T(1,128)} %choice_ref.3, bf16[128,4096]{1,0:T(8,128)(2,1)} %q_ref.3, bf16[128,4096]{1,0:T(8,128)(2,1)} %cot_ref.3, f32[4,256,1024]{2,1,0:T(8,128)} %get-tuple-element.38.softmax_ref, bf16[8,256,128]{2,1,0:T(8,128)(2,1)} %copy-done.17, ...), custom_call_target="tpu_custom_call" | custom-call | flops 3000000000 | bytes 9437184 | tf_op jit(solution)/shard_map/attend_backward/pallas_call | solution.py:499
  119.6 2.3 %all-to-all-done.4.got_ref = bf16[8,256,128]{2,1,0:T(8,128)(2,1)S(1)} async-done(((bf16[8,256,128]{2,1,0:T(8,128)(2,1)}), bf16[8,256,128]{2,1,0:T(8,128)(2,1)S(1)}, u32[]{:S(2)}, u32[]{:S(2)}) %all-to-all-start.4) | async-done | bytes 524320 | tf_op jit(solution)/shard_map/all_to_all | solution.py:31
  121.9 1.0 copy-done.10
  123.0 0.9 adapter_terms.1
  123.8 15.5 %all_to_all.41.got_ref = bf16[8,384,128]{2,1,0:T(8,128)(2,1)S(1)} all-to-all(bf16[8,384,128]{2,1,0:T(8,128)(2,1)S(1)} %get-tuple-element.47), channel_id=1, replica_groups=mesh['x'=4,'zl'=4,'y'=4,'zh'=4,'c'=2] {'y','c'}, dimensions={0} | all-to-all | bytes 1572864 | tf_op jit(solution)/shard_map/all_to_all | solution.py:31
  139.3 0.8 keys_y.1
  140.1 5.8 %all-to-all-start.6 = ((bf16[4,208,128]{2,1,0:T(8,128)(2,1)}), bf16[4,208,128]{2,1,0:T(8,128)(2,1)S(1)}, u32[]{:S(2)}, u32[]{:S(2)}) async-start(bf16[4,208,128]{2,1,0:T(8,128)(2,1)} %keys_y.1), calls=%async_computation.6 | async-start | bytes 425984 | tf_op jit(solution)/shard_map/all_to_all | solution.py:31
  146.4 4.6 %fusion = bf16[128,4096]{1,0:T(8,128)(2,1)} fusion(f32[128,4096]{1,0:T(8,128)S(1)} %convolution_multiply_fusion, bf16[128,512]{1,0:T(8,128)(2,1)S(1)} %copy-done.18, bf16[4096,512]{1,0:T(8,128)(2,1)} %get-tuple-element.50.weight_ref), kind=kOutput, calls=%fused_computation.2 | convolution fusion | flops 537919488 | bytes 7471104 | tf_op jit(solution)/shard_map/dot_general | solution.py:40
  151.1 9.7 %all-to-all-done.6.got_ref = bf16[4,208,128]{2,1,0:T(8,128)(2,1)S(1)} async-done(((bf16[4,208,128]{2,1,0:T(8,128)(2,1)}), bf16[4,208,128]{2,1,0:T(8,128)(2,1)S(1)}, u32[]{:S(2)}, u32[]{:S(2)}) %all-to-all-start.6) | async-done | bytes 213024 | tf_op jit(solution)/shard_map/all_to_all | solution.py:31
  160.7 0.8 keys_zh.1
  162.1 3.5 %all-to-all-start.7 = ((bf16[16,80,128]{2,1,0:T(8,128)(2,1)}), bf16[16,80,128]{2,1,0:T(8,128)(2,1)S(1)}, u32[]{:S(2)}, u32[]{:S(2)}) async-start(bf16[16,80,128]{2,1,0:T(8,128)(2,1)} %get-tuple-element.57), calls=%async_computation.7 | async-start | bytes 655360 | tf_op jit(solution)/shard_map/all_to_all | solution.py:31
  165.6 4.8 %prompt_gradient.1 = bf16[16,4096]{1,0:T(8,128)(2,1)} custom-call(bf16[16,512]{1,0:T(8,128)(2,1)} %copy-done.14, bf16[16,512]{1,0:T(8,128)(2,1)} %up_ref.7, bf16[16,4096]{1,0:T(8,128)(2,1)} %get-tuple-element.37.down_ref, bf16[4096,512]{1,0:T(8,128)(2,1)} %get-tuple-element.50.weight_ref), custom_call_target="tpu_custom_call" | custom-call | tf_op jit(solution)/shard_map/prompt_gradient/pallas_call | solution.py:481
  170.4 6.2 %all-to-all-done.7.got_ref = bf16[16,80,128]{2,1,0:T(8,128)(2,1)S(1)} async-done(((bf16[16,80,128]{2,1,0:T(8,128)(2,1)}), bf16[16,80,128]{2,1,0:T(8,128)(2,1)S(1)}, u32[]{:S(2)}, u32[]{:S(2)}) %all-to-all-start.7) | async-done | bytes 327712 | tf_op jit(solution)/shard_map/all_to_all | solution.py:31
  176.6 0.7 over_group.1
  (48 shorter events, 1.8 us)
Async XLA Ops:
  0.6 0.9 copy-start
  33.5 6.9 %copy-start.2 = (bf16[16,4096]{1,0:T(8,128)(2,1)S(1)}, bf16[16,4096]{1,0:T(8,128)(2,1)}, u32[]{:S(2)}) copy-start(bf16[16,4096]{1,0:T(8,128)(2,1)} %prompt_ref.3) | copy-start | bytes 393220
  33.5 46.4 %slice-start = ((bf16[4,208,128]{2,1,0:T(8,128)(2,1)}), bf16[4,64,128]{2,1,0:T(8,128)(2,1)S(1)}, s32[]{:S(2)}) async-start(bf16[4,208,128]{2,1,0:T(8,128)(2,1)} %all_to_all.40.start_ref), calls=%async_computation.8 | async-start | bytes 131072 | tf_op jit(solution)/shard_map/slice | solution.py:563
  33.5 32.3 %all-to-all-start.1 = ((bf16[16,528,128]{2,1,0:T(8,128)(2,1)}), bf16[16,528,128]{2,1,0:T(8,128)(2,1)S(1)}, u32[]{:S(2)}, u32[]{:S(2)}) async-start(bf16[16,528,128]{2,1,0:T(8,128)(2,1)} %weight_copies.1), calls=%async_computation.1 | async-start | bytes 4325376 | tf_op jit(solution)/shard_map/all_to_all | solution.py:31
  40.5 9.7 %collective-permute-start = (bf16[16,4096]{1,0:T(8,128)(2,1)S(1)}, bf16[16,4096]{1,0:T(8,128)(2,1)S(1)}, u32[]{:S(2)}, u32[]{:S(2)}) collective-permute-start(bf16[16,4096]{1,0:T(8,128)(2,1)S(1)} %copy-done.2), channel_id=1, source_target_pairs={{0,2},{2,4},{4,6},{6,0},{1,3},{3,5},{5,7},{7,1},{8,10},{10,12},{12... | collective-permute-start | bytes 393224 | tf_op jit(solution)/shard_map/ppermute | solution.py:532
  45.9 11.1 %collective-permute-start.2 = (bf16[16,4096]{1,0:T(8,128)(2,1)S(1)}, bf16[16,4096]{1,0:T(8,128)(2,1)S(1)}, u32[]{:S(2)}, u32[]{:S(2)}) collective-permute-start(bf16[16,4096]{1,0:T(8,128)(2,1)S(1)} %copy-done.2), channel_id=1, source_target_pairs={{0,6},{2,0},{4,2},{6,4},{1,7},{3,1},{5,3},{7,5},{8,14},{10,8},{12,... | collective-permute-start | bytes 393224 | tf_op jit(solution)/shard_map/ppermute | solution.py:532
  50.2 34.7 %copy-start.4 = (bf16[16,4096]{1,0:T(8,128)(2,1)}, bf16[16,4096]{1,0:T(8,128)(2,1)S(1)}, u32[]{:S(2)}) copy-start(bf16[16,4096]{1,0:T(8,128)(2,1)S(1)} %collective-permute-done.prompt1_ref) | copy-start | bytes 393220
  50.2 15.7 %collective-permute-start.1 = (bf16[16,4096]{1,0:T(8,128)(2,1)S(1)}, bf16[16,4096]{1,0:T(8,128)(2,1)S(1)}, u32[]{:S(2)}, u32[]{:S(2)}) collective-permute-start(bf16[16,4096]{1,0:T(8,128)(2,1)S(1)} %collective-permute-done.prompt1_ref), channel_id=1, source_target_pairs={{0,2},{2,4},{4,6},{6,0},{1,3},{3,5},{5,7},{7,1},{8,10},{10,12},{12... | collective-permute-start | bytes 393224 | tf_op jit(solution)/shard_map/ppermute | solution.py:532
  57.1 27.8 %copy-start.6 = (bf16[16,4096]{1,0:T(8,128)(2,1)}, bf16[16,4096]{1,0:T(8,128)(2,1)S(1)}, u32[]{:S(2)}) copy-start(bf16[16,4096]{1,0:T(8,128)(2,1)S(1)} %collective-permute-done.2.prompt3_ref) | copy-start | bytes 393220
  65.9 19.0 %copy-start.8 = (bf16[16,4096]{1,0:T(8,128)(2,1)}, bf16[16,4096]{1,0:T(8,128)(2,1)S(1)}, u32[]{:S(2)}) copy-start(bf16[16,4096]{1,0:T(8,128)(2,1)S(1)} %collective-permute-done.1.prompt2_ref) | copy-start | bytes 393220
  65.9 19.0 %copy-start.15 = (bf16[16,528,128]{2,1,0:T(8,128)(2,1)}, bf16[16,528,128]{2,1,0:T(8,128)(2,1)S(1)}, u32[]{:S(2)}) copy-start(bf16[16,528,128]{2,1,0:T(8,128)(2,1)S(1)} %all-to-all-done.1) | copy-start | bytes 6488068
  65.9 19.0 %collective-permute-start.3 = (bf16[4,4,528,128]{3,2,1,0:T(8,128)(2,1)S(1)}, bf16[4,4,528,128]{3,2,1,0:T(8,128)(2,1)}, u32[]{:S(2)}, u32[]{:S(2)}) collective-permute-start(bf16[4,4,528,128]{3,2,1,0:T(8,128)(2,1)S(1)} %bitcast.16), channel_id=1, source_target_pairs={{0,1},{1,0},{2,3},{3,2},{4,5},{5,4},{6,7},{7,6},{8,9},{9,8},{10,11... | collective-permute-start | bytes 6488072 | tf_op jit(solution)/shard_map/ppermute | solution.py:562
  80.9 13.5 %all-to-all-start.2 = ((bf16[8,4,64,128]{3,2,1,0:T(8,128)(2,1)}), bf16[8,4,64,128]{3,2,1,0:T(8,128)(2,1)S(1)}, u32[]{:S(2)}, u32[]{:S(2)}) async-start(bf16[8,4,64,128]{3,2,1,0:T(8,128)(2,1)} %broadcast_in_dim.5), calls=%async_computation.2 | async-start | bytes 1048576 | tf_op jit(solution)/shard_map/all_to_all | solution.py:31
  94.3 4.3 %copy-start.16 = (bf16[8,4,64,128]{3,2,1,0:T(8,128)(2,1)}, bf16[8,4,64,128]{3,2,1,0:T(8,128)(2,1)S(1)}, u32[]{:S(2)}) copy-start(bf16[8,4,64,128]{3,2,1,0:T(8,128)(2,1)S(1)} %all-to-all-done.2) | copy-start | bytes 1572868
  94.3 13.8 %all-to-all-start.3 = ((bf16[8,256,128]{2,1,0:T(8,128)(2,1)}), bf16[8,256,128]{2,1,0:T(8,128)(2,1)S(1)}, u32[]{:S(2)}, u32[]{:S(2)}) async-start(bf16[8,256,128]{2,1,0:T(8,128)(2,1)} %get-tuple-element.40), calls=%async_computation.3 | async-start | bytes 1048576 | tf_op jit(solution)/shard_map/all_to_all | solution.py:31
  108.1 4.3 %copy-start.17 = (bf16[8,256,128]{2,1,0:T(8,128)(2,1)}, bf16[8,256,128]{2,1,0:T(8,128)(2,1)S(1)}, u32[]{:S(2)}) copy-start(bf16[8,256,128]{2,1,0:T(8,128)(2,1)S(1)} %all-to-all-done.3.value_ref) | copy-start | bytes 1572868
  108.1 13.8 %all-to-all-start.4 = ((bf16[8,256,128]{2,1,0:T(8,128)(2,1)}), bf16[8,256,128]{2,1,0:T(8,128)(2,1)S(1)}, u32[]{:S(2)}, u32[]{:S(2)}) async-start(bf16[8,256,128]{2,1,0:T(8,128)(2,1)} %get-tuple-element.44), calls=%async_computation.4 | async-start | bytes 1048576 | tf_op jit(solution)/shard_map/all_to_all | solution.py:31
  112.4 9.5 %copy-start.1 = (bf16[16,4096]{1,0:T(8,128)(2,1)S(1)}, bf16[16,4096]{1,0:T(8,128)(2,1)}, u32[]{:S(2)}) copy-start(bf16[16,4096]{1,0:T(8,128)(2,1)} %get-tuple-element.37.down_ref) | copy-start | bytes 393220
  112.4 9.5 %copy-start.3 = (bf16[16,4096]{1,0:T(8,128)(2,1)S(1)}, bf16[16,4096]{1,0:T(8,128)(2,1)}, u32[]{:S(2)}) copy-start(bf16[16,4096]{1,0:T(8,128)(2,1)} %prompt_ref.3) | copy-start | bytes 393220
  112.4 9.5 %copy-start.5 = (bf16[16,4096]{1,0:T(8,128)(2,1)S(1)}, bf16[16,4096]{1,0:T(8,128)(2,1)}, u32[]{:S(2)}) copy-start(bf16[16,4096]{1,0:T(8,128)(2,1)} %copy-done.4) | copy-start | bytes 393220
  112.4 9.5 %copy-start.7 = (bf16[16,4096]{1,0:T(8,128)(2,1)S(1)}, bf16[16,4096]{1,0:T(8,128)(2,1)}, u32[]{:S(2)}) copy-start(bf16[16,4096]{1,0:T(8,128)(2,1)} %copy-done.6) | copy-start | bytes 393220
  112.4 9.5 %copy-start.9 = (bf16[16,4096]{1,0:T(8,128)(2,1)S(1)}, bf16[16,4096]{1,0:T(8,128)(2,1)}, u32[]{:S(2)}) copy-start(bf16[16,4096]{1,0:T(8,128)(2,1)} %copy-done.8) | copy-start | bytes 393220
  112.4 9.5 %copy-start.11 = (f32[16,4096]{1,0:T(8,128)S(1)}, f32[16,4096]{1,0:T(8,128)}, u32[]{:S(2)}) copy-start(f32[16,4096]{1,0:T(8,128)} %get-tuple-element.45.grad_ref) | copy-start | bytes 786436
  112.4 9.5 %copy-start.12 = (bf16[16,512]{1,0:T(8,128)(2,1)S(1)}, bf16[16,512]{1,0:T(8,128)(2,1)}, u32[]{:S(2)}) copy-start(bf16[16,512]{1,0:T(8,128)(2,1)} %up_ref.7) | copy-start | bytes 49156
  112.4 9.5 %copy-start.13 = (f32[16,512]{1,0:T(8,128)S(1)}, f32[16,512]{1,0:T(8,128)}, u32[]{:S(2)}) copy-start(f32[16,512]{1,0:T(8,128)} %get-tuple-element.46.second_ref) | copy-start | bytes 98308
  121.9 1.0 copy-start.10
  123.0 23.0 %copy-start.19 = (bf16[16,128]{1,0:T(8,128)(2,1)S(1)}, bf16[16,128]{1,0:T(8,128)(2,1)}, u32[]{:S(2)}) copy-start(bf16[16,128]{1,0:T(8,128)(2,1)} %get-tuple-element.51) | copy-start | bytes 12292
  139.3 7.1 %copy-start.18 = (bf16[128,512]{1,0:T(8,128)(2,1)S(1)}, bf16[128,512]{1,0:T(8,128)(2,1)}, u32[]{:S(2)}) copy-start(bf16[128,512]{1,0:T(8,128)(2,1)} %get-tuple-element.49) | copy-start | bytes 393220
  140.1 20.6 %all-to-all-start.6 = ((bf16[4,208,128]{2,1,0:T(8,128)(2,1)}), bf16[4,208,128]{2,1,0:T(8,128)(2,1)S(1)}, u32[]{:S(2)}, u32[]{:S(2)}) async-start(bf16[4,208,128]{2,1,0:T(8,128)(2,1)} %keys_y.1), calls=%async_computation.6 | async-start | bytes 425984 | tf_op jit(solution)/shard_map/all_to_all | solution.py:31
  161.5 0.6 copy-start.14
  162.1 14.5 %all-to-all-start.7 = ((bf16[16,80,128]{2,1,0:T(8,128)(2,1)}), bf16[16,80,128]{2,1,0:T(8,128)(2,1)S(1)}, u32[]{:S(2)}, u32[]{:S(2)}) async-start(bf16[16,80,128]{2,1,0:T(8,128)(2,1)} %get-tuple-element.57), calls=%async_computation.7 | async-start | bytes 655360 | tf_op jit(solution)/shard_map/all_to_all | solution.py:31

commit v7 on v6

--- a/solution.py
+++ b/solution.py
@@ -560,7 +560,8 @@
     before, behind = move(before, "zh", 1), move(behind, "zh", 3)
     prompts = [prompt_rows, before, move(before, "zh", 1), behind]
     other = lax.ppermute(after(weight, *prompts), "c", [(0, 1), (1, 0)])
-    key_all = gather(after(start[:, 144:], weight), OWNERS).reshape(4, 2, 4, 64, HEAD_DIM)
+    key_copies = jnp.broadcast_to(start[None, :, 144:], (8, 4, 64, HEAD_DIM))
+    key_all = swap(after(key_copies, weight), OWNERS).reshape(4, 2, 4, 64, HEAD_DIM)
 
     values, part, weight, down = project(
         response_rows, prompts, weight, other, value_adapter_up

time: 178 us -> 178 us (level)
  no operation moved by 1% of the time
where the time goes in v7:
time: 178 us; the launch traced here: 177 us
  starting transfers between devices  58.9 us (33%)
  blocking collectives  44.3 us (25%)
  Pallas kernels  32.9 us (18%)
  waiting for transfers between devices  30.9 us (17%)
  matrix products  5.1 us (3%)
  local copies, waits for them, and re-layouts  3.58 us (2%)
    all_to_all x2, blocking collectives, swap(): return lax.all_to_all(array, axis, 0, 0, tiled=True)  44.3 us
    all_to_all x6, starting transfers between devices, swap(): return lax.all_to_all(array, axis, 0, 0, tiled=True)  28.8 us
    all_to_all x6, waiting for transfers between devices, swap(): return lax.all_to_all(array, axis, 0, 0, tiled=True)  21.6 us
    ppermute x3, starting transfers between devices, move(): return lax.ppermute(part, axis, [(i, (i + step) % 4) for i in range(4)])  16.1 us
    ppermute x1, starting transfers between devices, on_device(): other = lax.ppermute(after(weight, *prompts), 'c', [(0, 1), (1, 0)])  14.1 us
    ppermute x3, waiting for transfers between devices, move(): return lax.ppermute(part, axis, [(i, (i + step) % 4) for i in range(4)])  9.3 us
    pallas_call x1, Pallas kernels, attend_forward(): pl.pallas_call(forward_kernel, grid=(KV_HEADS,), in_specs=[pl.BlockSpec(m...  8.63 us
    pallas_call x1, Pallas kernels, attend_backward(): pl.pallas_call(backward_kernel, grid=(KV_HEADS,), in_specs=[pl.BlockSpec(...  7.16 us
  transfers between devices with their start and end apart: 10, of which 7 were waited for; matrix products, arithmetic and copies ran while one was open for 3% of the time, Pallas kernels for 15%

profile of v7, /device:TPU:1, one launch (start us, length us, event | category | flops | bytes accessed | tf_op | source)
XLA Modules:
  0.0 177.2 jit_solution(15622582530820802662)
XLA Ops:
  0.7 0.8 copy_bitcast_fusion
  1.6 0.7 pad_maximum_fusion
  2.3 28.8 %all_to_all.40.start_ref = bf16[4,208,128]{2,1,0:T(8,128)(2,1)} all-to-all(bf16[4,208,128]{2,1,0:T(8,128)(2,1)S(1)} %broadcast_in_dim.4), channel_id=1, replica_groups=mesh['x'=4,'zl'=4,'y'=4,'zh'=4,'c'=2] {'zh'}, dimensions={0} | all-to-all | bytes 425984 | tf_op jit(solution)/shard_map/all_to_all | solution.py:31
  31.1 2.4 %weight_copies.1 = bf16[16,528,128]{2,1,0:T(8,128)(2,1)} custom-call(bf16[4,208,128]{2,1,0:T(8,128)(2,1)} %all_to_all.40.start_ref), custom_call_target="tpu_custom_call" | custom-call | tf_op jit(solution)/shard_map/weight_copies/pallas_call | solution.py:429
  33.5 6.9 %all-to-all-start.1 = ((bf16[16,528,128]{2,1,0:T(8,128)(2,1)}), bf16[16,528,128]{2,1,0:T(8,128)(2,1)S(1)}, u32[]{:S(2)}, u32[]{:S(2)}) async-start(bf16[16,528,128]{2,1,0:T(8,128)(2,1)} %weight_copies.1), calls=%async_computation.1 | async-start | bytes 4325376 | tf_op jit(solution)/shard_map/all_to_all | solution.py:31
  40.5 5.5 %collective-permute-start = (bf16[16,4096]{1,0:T(8,128)(2,1)S(1)}, bf16[16,4096]{1,0:T(8,128)(2,1)S(1)}, u32[]{:S(2)}, u32[]{:S(2)}) collective-permute-start(bf16[16,4096]{1,0:T(8,128)(2,1)S(1)} %copy-done.2), channel_id=1, source_target_pairs={{0,2},{2,4},{4,6},{6,0},{1,3},{3,5},{5,7},{7,1},{8,10},{10,12},{12... | collective-permute-start | bytes 393224 | tf_op jit(solution)/shard_map/ppermute | solution.py:532
  45.9 3.7 %collective-permute-start.2 = (bf16[16,4096]{1,0:T(8,128)(2,1)S(1)}, bf16[16,4096]{1,0:T(8,128)(2,1)S(1)}, u32[]{:S(2)}, u32[]{:S(2)}) collective-permute-start(bf16[16,4096]{1,0:T(8,128)(2,1)S(1)} %copy-done.2), channel_id=1, source_target_pairs={{0,6},{2,0},{4,2},{6,4},{1,7},{3,1},{5,3},{7,5},{8,14},{10,8},{12,... | collective-permute-start | bytes 393224 | tf_op jit(solution)/shard_map/ppermute | solution.py:532
  50.2 6.9 %collective-permute-start.1 = (bf16[16,4096]{1,0:T(8,128)(2,1)S(1)}, bf16[16,4096]{1,0:T(8,128)(2,1)S(1)}, u32[]{:S(2)}, u32[]{:S(2)}) collective-permute-start(bf16[16,4096]{1,0:T(8,128)(2,1)S(1)} %collective-permute-done.prompt1_ref), channel_id=1, source_target_pairs={{0,2},{2,4},{4,6},{6,0},{1,3},{3,5},{5,7},{7,1},{8,10},{10,12},{12... | collective-permute-start | bytes 393224 | tf_op jit(solution)/shard_map/ppermute | solution.py:532
  57.1 8.8 %collective-permute-done.1.prompt2_ref = bf16[16,4096]{1,0:T(8,128)(2,1)S(1)} collective-permute-done((bf16[16,4096]{1,0:T(8,128)(2,1)S(1)}, bf16[16,4096]{1,0:T(8,128)(2,1)S(1)}, u32[]{:S(2)}, u32[]{:S(2)}) %collective-permute-start.1) | collective-permute-done | bytes 131104 | tf_op jit(solution)/shard_map/ppermute | solution.py:532
  65.9 14.1 %collective-permute-start.3 = (bf16[4,4,528,128]{3,2,1,0:T(8,128)(2,1)S(1)}, bf16[4,4,528,128]{3,2,1,0:T(8,128)(2,1)}, u32[]{:S(2)}, u32[]{:S(2)}) collective-permute-start(bf16[4,4,528,128]{3,2,1,0:T(8,128)(2,1)S(1)} %bitcast.16), channel_id=1, source_target_pairs={{0,1},{1,0},{2,3},{3,2},{4,5},{5,4},{6,7},{7,6},{8,9},{9,8},{10,11... | collective-permute-start | bytes 6488072 | tf_op jit(solution)/shard_map/ppermute | solution.py:562
  80.0 0.9 broadcast_in_dim.5
  80.9 4.0 %all-to-all-start.2 = ((bf16[8,4,64,128]{3,2,1,0:T(8,128)(2,1)}), bf16[8,4,64,128]{3,2,1,0:T(8,128)(2,1)S(1)}, u32[]{:S(2)}, u32[]{:S(2)}) async-start(bf16[8,4,64,128]{3,2,1,0:T(8,128)(2,1)} %broadcast_in_dim.5), calls=%async_computation.2 | async-start | bytes 1048576 | tf_op jit(solution)/shard_map/all_to_all | solution.py:31
  84.9 6.8 %project.1 = (bf16[128,512]{1,0:T(8,128)(2,1)}, bf16[8,256,128]{2,1,0:T(8,128)(2,1)}, bf16[4096,512]{1,0:T(8,128)(2,1)}, bf16[16,4096]{1,0:T(8,128)(2,1)}) custom-call(bf16[128,4096]{1,0:T(8,128)(2,1)} %x_ref.3, bf16[16,4096]{1,0:T(8,128)(2,1)} %prompt_ref.3, bf16[16,4096]{1,0:T(8,128)(2,1)} %copy-done.4, bf16[16,4096]{1,0:T(8,128)(2,1)} %copy-done.8, ...), custom_call_target="tpu_custom_call" | custom-call | flops 600000000 | bytes 10485760 | tf_op jit(solution)/shard_map/project/pallas_call | solution.py:450
  91.7 2.6 %all-to-all-done.2 = bf16[8,4,64,128]{3,2,1,0:T(8,128)(2,1)S(1)} async-done(((bf16[8,4,64,128]{3,2,1,0:T(8,128)(2,1)}), bf16[8,4,64,128]{3,2,1,0:T(8,128)(2,1)S(1)}, u32[]{:S(2)}, u32[]{:S(2)}) %all-to-all-start.2) | async-done | bytes 524320 | tf_op jit(solution)/shard_map/all_to_all | solution.py:31
  94.3 4.3 %all-to-all-start.3 = ((bf16[8,256,128]{2,1,0:T(8,128)(2,1)}), bf16[8,256,128]{2,1,0:T(8,128)(2,1)S(1)}, u32[]{:S(2)}, u32[]{:S(2)}) async-start(bf16[8,256,128]{2,1,0:T(8,128)(2,1)} %get-tuple-element.40), calls=%async_computation.3 | async-start | bytes 1048576 | tf_op jit(solution)/shard_map/all_to_all | solution.py:31
  98.6 8.6 %attend_forward.1 = (bf16[8,256,128]{2,1,0:T(8,128)(2,1)}, bf16[128,512]{1,0:T(8,128)(2,1)}, bf16[16,128]{1,0:T(8,128)(2,1)}, f32[16,4096]{1,0:T(8,128)}, f32[16,512]{1,0:T(8,128)}, /*index=5*/f32[4,256,1024]{2,1,0:T(8,128)}) custom-call(s32[1,8]{1,0:T(1,128)} %choice_ref.3, bf16[128,4096]{1,0:T(8,128)(2,1)} %q_ref.3, bf16[128,4096]{1,0:T(8,128)(2,1)} %cot_ref.3, ...), custom_call_target="tpu_custom_call" | custom-call | flops 2000000000 | bytes 5242880 | tf_op jit(solution)/shard_map/attend_forward/pallas_call | solution.py:368
  107.2 0.9 all-to-all-done.3.value_ref
  108.1 4.3 %all-to-all-start.4 = ((bf16[8,256,128]{2,1,0:T(8,128)(2,1)}), bf16[8,256,128]{2,1,0:T(8,128)(2,1)S(1)}, u32[]{:S(2)}, u32[]{:S(2)}) async-start(bf16[8,256,128]{2,1,0:T(8,128)(2,1)} %get-tuple-element.44), calls=%async_computation.4 | async-start | bytes 1048576 | tf_op jit(solution)/shard_map/all_to_all | solution.py:31
  112.5 7.2 %attend_backward.1 = (bf16[8,256,128]{2,1,0:T(8,128)(2,1)}, bf16[128,512]{1,0:T(8,128)(2,1)}) custom-call(s32[1,8]{1,0:T(1,128)} %choice_ref.3, bf16[128,4096]{1,0:T(8,128)(2,1)} %q_ref.3, bf16[128,4096]{1,0:T(8,128)(2,1)} %cot_ref.3, f32[4,256,1024]{2,1,0:T(8,128)} %get-tuple-element.38.softmax_ref, bf16[8,256,128]{2,1,0:T(8,128)(2,1)} %copy-done.17, ...), custom_call_target="tpu_custom_call" | custom-call | flops 3000000000 | bytes 9437184 | tf_op jit(solution)/shard_map/attend_backward/pallas_call | solution.py:499
  119.6 2.3 %all-to-all-done.4.got_ref = bf16[8,256,128]{2,1,0:T(8,128)(2,1)S(1)} async-done(((bf16[8,256,128]{2,1,0:T(8,128)(2,1)}), bf16[8,256,128]{2,1,0:T(8,128)(2,1)S(1)}, u32[]{:S(2)}, u32[]{:S(2)}) %all-to-all-start.4) | async-done | bytes 524320 | tf_op jit(solution)/shard_map/all_to_all | solution.py:31
  121.9 1.0 copy-done.10
  123.0 0.9 adapter_terms.1
  123.8 15.5 %all_to_all.41.got_ref = bf16[8,384,128]{2,1,0:T(8,128)(2,1)S(1)} all-to-all(bf16[8,384,128]{2,1,0:T(8,128)(2,1)S(1)} %get-tuple-element.47), channel_id=1, replica_groups=mesh['x'=4,'zl'=4,'y'=4,'zh'=4,'c'=2] {'y','c'}, dimensions={0} | all-to-all | bytes 1572864 | tf_op jit(solution)/shard_map/all_to_all | solution.py:31
  139.3 0.8 keys_y.1
  140.1 5.8 %all-to-all-start.6 = ((bf16[4,208,128]{2,1,0:T(8,128)(2,1)}), bf16[4,208,128]{2,1,0:T(8,128)(2,1)S(1)}, u32[]{:S(2)}, u32[]{:S(2)}) async-start(bf16[4,208,128]{2,1,0:T(8,128)(2,1)} %keys_y.1), calls=%async_computation.6 | async-start | bytes 425984 | tf_op jit(solution)/shard_map/all_to_all | solution.py:31
  146.4 4.6 %fusion = bf16[128,4096]{1,0:T(8,128)(2,1)} fusion(f32[128,4096]{1,0:T(8,128)S(1)} %convolution_multiply_fusion, bf16[128,512]{1,0:T(8,128)(2,1)S(1)} %copy-done.18, bf16[4096,512]{1,0:T(8,128)(2,1)} %get-tuple-element.50.weight_ref), kind=kOutput, calls=%fused_computation.2 | convolution fusion | flops 537919488 | bytes 7471104 | tf_op jit(solution)/shard_map/dot_general | solution.py:40
  151.1 9.7 %all-to-all-done.6.got_ref = bf16[4,208,128]{2,1,0:T(8,128)(2,1)S(1)} async-done(((bf16[4,208,128]{2,1,0:T(8,128)(2,1)}), bf16[4,208,128]{2,1,0:T(8,128)(2,1)S(1)}, u32[]{:S(2)}, u32[]{:S(2)}) %all-to-all-start.6) | async-done | bytes 213024 | tf_op jit(solution)/shard_map/all_to_all | solution.py:31
  160.7 0.8 keys_zh.1
  162.1 3.5 %all-to-all-start.7 = ((bf16[16,80,128]{2,1,0:T(8,128)(2,1)}), bf16[16,80,128]{2,1,0:T(8,128)(2,1)S(1)}, u32[]{:S(2)}, u32[]{:S(2)}) async-start(bf16[16,80,128]{2,1,0:T(8,128)(2,1)} %get-tuple-element.57), calls=%async_computation.7 | async-start | bytes 655360 | tf_op jit(solution)/shard_map/all_to_all | solution.py:31
  165.6 4.8 %prompt_gradient.1 = bf16[16,4096]{1,0:T(8,128)(2,1)} custom-call(bf16[16,512]{1,0:T(8,128)(2,1)} %copy-done.14, bf16[16,512]{1,0:T(8,128)(2,1)} %up_ref.7, bf16[16,4096]{1,0:T(8,128)(2,1)} %get-tuple-element.37.down_ref, bf16[4096,512]{1,0:T(8,128)(2,1)} %get-tuple-element.50.weight_ref), custom_call_target="tpu_custom_call" | custom-call | tf_op jit(solution)/shard_map/prompt_gradient/pallas_call | solution.py:481
  170.4 6.2 %all-to-all-done.7.got_ref = bf16[16,80,128]{2,1,0:T(8,128)(2,1)S(1)} async-done(((bf16[16,80,128]{2,1,0:T(8,128)(2,1)}), bf16[16,80,128]{2,1,0:T(8,128)(2,1)S(1)}, u32[]{:S(2)}, u32[]{:S(2)}) %all-to-all-start.7) | async-done | bytes 327712 | tf_op jit(solution)/shard_map/all_to_all | solution.py:31
  176.6 0.7 over_group.1
  (48 shorter events, 1.8 us)
Async XLA Ops:
  0.6 0.9 copy-start
  33.5 6.9 %copy-start.2 = (bf16[16,4096]{1,0:T(8,128)(2,1)S(1)}, bf16[16,4096]{1,0:T(8,128)(2,1)}, u32[]{:S(2)}) copy-start(bf16[16,4096]{1,0:T(8,128)(2,1)} %prompt_ref.3) | copy-start | bytes 393220
  33.5 46.4 %slice-start = ((bf16[4,208,128]{2,1,0:T(8,128)(2,1)}), bf16[4,64,128]{2,1,0:T(8,128)(2,1)S(1)}, s32[]{:S(2)}) async-start(bf16[4,208,128]{2,1,0:T(8,128)(2,1)} %all_to_all.40.start_ref), calls=%async_computation.8 | async-start | bytes 131072 | tf_op jit(solution)/shard_map/slice | solution.py:563
  33.5 32.3 %all-to-all-start.1 = ((bf16[16,528,128]{2,1,0:T(8,128)(2,1)}), bf16[16,528,128]{2,1,0:T(8,128)(2,1)S(1)}, u32[]{:S(2)}, u32[]{:S(2)}) async-start(bf16[16,528,128]{2,1,0:T(8,128)(2,1)} %weight_copies.1), calls=%async_computation.1 | async-start | bytes 4325376 | tf_op jit(solution)/shard_map/all_to_all | solution.py:31
  40.5 9.7 %collective-permute-start = (bf16[16,4096]{1,0:T(8,128)(2,1)S(1)}, bf16[16,4096]{1,0:T(8,128)(2,1)S(1)}, u32[]{:S(2)}, u32[]{:S(2)}) collective-permute-start(bf16[16,4096]{1,0:T(8,128)(2,1)S(1)} %copy-done.2), channel_id=1, source_target_pairs={{0,2},{2,4},{4,6},{6,0},{1,3},{3,5},{5,7},{7,1},{8,10},{10,12},{12... | collective-permute-start | bytes 393224 | tf_op jit(solution)/shard_map/ppermute | solution.py:532
  45.9 11.1 %collective-permute-start.2 = (bf16[16,4096]{1,0:T(8,128)(2,1)S(1)}, bf16[16,4096]{1,0:T(8,128)(2,1)S(1)}, u32[]{:S(2)}, u32[]{:S(2)}) collective-permute-start(bf16[16,4096]{1,0:T(8,128)(2,1)S(1)} %copy-done.2), channel_id=1, source_target_pairs={{0,6},{2,0},{4,2},{6,4},{1,7},{3,1},{5,3},{7,5},{8,14},{10,8},{12,... | collective-permute-start | bytes 393224 | tf_op jit(solution)/shard_map/ppermute | solution.py:532
  50.2 34.7 %copy-start.4 = (bf16[16,4096]{1,0:T(8,128)(2,1)}, bf16[16,4096]{1,0:T(8,128)(2,1)S(1)}, u32[]{:S(2)}) copy-start(bf16[16,4096]{1,0:T(8,128)(2,1)S(1)} %collective-permute-done.prompt1_ref) | copy-start | bytes 393220
  50.2 15.7 %collective-permute-start.1 = (bf16[16,4096]{1,0:T(8,128)(2,1)S(1)}, bf16[16,4096]{1,0:T(8,128)(2,1)S(1)}, u32[]{:S(2)}, u32[]{:S(2)}) collective-permute-start(bf16[16,4096]{1,0:T(8,128)(2,1)S(1)} %collective-permute-done.prompt1_ref), channel_id=1, source_target_pairs={{0,2},{2,4},{4,6},{6,0},{1,3},{3,5},{5,7},{7,1},{8,10},{10,12},{12... | collective-permute-start | bytes 393224 | tf_op jit(solution)/shard_map/ppermute | solution.py:532
  57.1 27.8 %copy-start.6 = (bf16[16,4096]{1,0:T(8,128)(2,1)}, bf16[16,4096]{1,0:T(8,128)(2,1)S(1)}, u32[]{:S(2)}) copy-start(bf16[16,4096]{1,0:T(8,128)(2,1)S(1)} %collective-permute-done.2.prompt3_ref) | copy-start | bytes 393220
  65.9 19.0 %copy-start.8 = (bf16[16,4096]{1,0:T(8,128)(2,1)}, bf16[16,4096]{1,0:T(8,128)(2,1)S(1)}, u32[]{:S(2)}) copy-start(bf16[16,4096]{1,0:T(8,128)(2,1)S(1)} %collective-permute-done.1.prompt2_ref) | copy-start | bytes 393220
  65.9 19.0 %copy-start.15 = (bf16[16,528,128]{2,1,0:T(8,128)(2,1)}, bf16[16,528,128]{2,1,0:T(8,128)(2,1)S(1)}, u32[]{:S(2)}) copy-start(bf16[16,528,128]{2,1,0:T(8,128)(2,1)S(1)} %all-to-all-done.1) | copy-start | bytes 6488068
  65.9 19.0 %collective-permute-start.3 = (bf16[4,4,528,128]{3,2,1,0:T(8,128)(2,1)S(1)}, bf16[4,4,528,128]{3,2,1,0:T(8,128)(2,1)}, u32[]{:S(2)}, u32[]{:S(2)}) collective-permute-start(bf16[4,4,528,128]{3,2,1,0:T(8,128)(2,1)S(1)} %bitcast.16), channel_id=1, source_target_pairs={{0,1},{1,0},{2,3},{3,2},{4,5},{5,4},{6,7},{7,6},{8,9},{9,8},{10,11... | collective-permute-start | bytes 6488072 | tf_op jit(solution)/shard_map/ppermute | solution.py:562
  80.9 13.5 %all-to-all-start.2 = ((bf16[8,4,64,128]{3,2,1,0:T(8,128)(2,1)}), bf16[8,4,64,128]{3,2,1,0:T(8,128)(2,1)S(1)}, u32[]{:S(2)}, u32[]{:S(2)}) async-start(bf16[8,4,64,128]{3,2,1,0:T(8,128)(2,1)} %broadcast_in_dim.5), calls=%async_computation.2 | async-start | bytes 1048576 | tf_op jit(solution)/shard_map/all_to_all | solution.py:31
  94.3 4.3 %copy-start.16 = (bf16[8,4,64,128]{3,2,1,0:T(8,128)(2,1)}, bf16[8,4,64,128]{3,2,1,0:T(8,128)(2,1)S(1)}, u32[]{:S(2)}) copy-start(bf16[8,4,64,128]{3,2,1,0:T(8,128)(2,1)S(1)} %all-to-all-done.2) | copy-start | bytes 1572868
  94.3 13.8 %all-to-all-start.3 = ((bf16[8,256,128]{2,1,0:T(8,128)(2,1)}), bf16[8,256,128]{2,1,0:T(8,128)(2,1)S(1)}, u32[]{:S(2)}, u32[]{:S(2)}) async-start(bf16[8,256,128]{2,1,0:T(8,128)(2,1)} %get-tuple-element.40), calls=%async_computation.3 | async-start | bytes 1048576 | tf_op jit(solution)/shard_map/all_to_all | solution.py:31
  108.1 4.3 %copy-start.17 = (bf16[8,256,128]{2,1,0:T(8,128)(2,1)}, bf16[8,256,128]{2,1,0:T(8,128)(2,1)S(1)}, u32[]{:S(2)}) copy-start(bf16[8,256,128]{2,1,0:T(8,128)(2,1)S(1)} %all-to-all-done.3.value_ref) | copy-start | bytes 1572868
  108.1 13.8 %all-to-all-start.4 = ((bf16[8,256,128]{2,1,0:T(8,128)(2,1)}), bf16[8,256,128]{2,1,0:T(8,128)(2,1)S(1)}, u32[]{:S(2)}, u32[]{:S(2)}) async-start(bf16[8,256,128]{2,1,0:T(8,128)(2,1)} %get-tuple-element.44), calls=%async_computation.4 | async-start | bytes 1048576 | tf_op jit(solution)/shard_map/all_to_all | solution.py:31
  112.4 9.5 %copy-start.1 = (bf16[16,4096]{1,0:T(8,128)(2,1)S(1)}, bf16[16,4096]{1,0:T(8,128)(2,1)}, u32[]{:S(2)}) copy-start(bf16[16,4096]{1,0:T(8,128)(2,1)} %get-tuple-element.37.down_ref) | copy-start | bytes 393220
  112.4 9.5 %copy-start.3 = (bf16[16,4096]{1,0:T(8,128)(2,1)S(1)}, bf16[16,4096]{1,0:T(8,128)(2,1)}, u32[]{:S(2)}) copy-start(bf16[16,4096]{1,0:T(8,128)(2,1)} %prompt_ref.3) | copy-start | bytes 393220
  112.4 9.5 %copy-start.5 = (bf16[16,4096]{1,0:T(8,128)(2,1)S(1)}, bf16[16,4096]{1,0:T(8,128)(2,1)}, u32[]{:S(2)}) copy-start(bf16[16,4096]{1,0:T(8,128)(2,1)} %copy-done.4) | copy-start | bytes 393220
  112.4 9.5 %copy-start.7 = (bf16[16,4096]{1,0:T(8,128)(2,1)S(1)}, bf16[16,4096]{1,0:T(8,128)(2,1)}, u32[]{:S(2)}) copy-start(bf16[16,4096]{1,0:T(8,128)(2,1)} %copy-done.6) | copy-start | bytes 393220
  112.4 9.5 %copy-start.9 = (bf16[16,4096]{1,0:T(8,128)(2,1)S(1)}, bf16[16,4096]{1,0:T(8,128)(2,1)}, u32[]{:S(2)}) copy-start(bf16[16,4096]{1,0:T(8,128)(2,1)} %copy-done.8) | copy-start | bytes 393220
  112.4 9.5 %copy-start.11 = (f32[16,4096]{1,0:T(8,128)S(1)}, f32[16,4096]{1,0:T(8,128)}, u32[]{:S(2)}) copy-start(f32[16,4096]{1,0:T(8,128)} %get-tuple-element.45.grad_ref) | copy-start | bytes 786436
  112.4 9.5 %copy-start.12 = (bf16[16,512]{1,0:T(8,128)(2,1)S(1)}, bf16[16,512]{1,0:T(8,128)(2,1)}, u32[]{:S(2)}) copy-start(bf16[16,512]{1,0:T(8,128)(2,1)} %up_ref.7) | copy-start | bytes 49156
  112.4 9.5 %copy-start.13 = (f32[16,512]{1,0:T(8,128)S(1)}, f32[16,512]{1,0:T(8,128)}, u32[]{:S(2)}) copy-start(f32[16,512]{1,0:T(8,128)} %get-tuple-element.46.second_ref) | copy-start | bytes 98308
  121.9 1.0 copy-start.10
  123.0 23.0 %copy-start.19 = (bf16[16,128]{1,0:T(8,128)(2,1)S(1)}, bf16[16,128]{1,0:T(8,128)(2,1)}, u32[]{:S(2)}) copy-start(bf16[16,128]{1,0:T(8,128)(2,1)} %get-tuple-element.51) | copy-start | bytes 12292
  139.3 7.1 %copy-start.18 = (bf16[128,512]{1,0:T(8,128)(2,1)S(1)}, bf16[128,512]{1,0:T(8,128)(2,1)}, u32[]{:S(2)}) copy-start(bf16[128,512]{1,0:T(8,128)(2,1)} %get-tuple-element.49) | copy-start | bytes 393220
  140.1 20.6 %all-to-all-start.6 = ((bf16[4,208,128]{2,1,0:T(8,128)(2,1)}), bf16[4,208,128]{2,1,0:T(8,128)(2,1)S(1)}, u32[]{:S(2)}, u32[]{:S(2)}) async-start(bf16[4,208,128]{2,1,0:T(8,128)(2,1)} %keys_y.1), calls=%async_computation.6 | async-start | bytes 425984 | tf_op jit(solution)/shard_map/all_to_all | solution.py:31
  161.5 0.6 copy-start.14
  162.1 14.5 %all-to-all-start.7 = ((bf16[16,80,128]{2,1,0:T(8,128)(2,1)}), bf16[16,80,128]{2,1,0:T(8,128)(2,1)S(1)}, u32[]{:S(2)}, u32[]{:S(2)}) async-start(bf16[16,80,128]{2,1,0:T(8,128)(2,1)} %get-tuple-element.57), calls=%async_computation.7 | async-start | bytes 655360 | tf_op jit(solution)/shard_map/all_to_all | solution.py:31

commit v8 on v7

--- a/solution.py
+++ b/solution.py
@@ -129,7 +129,7 @@
 def forward_kernel(
     choice_ref, q_ref, cot_ref, key_ref, own_key_ref, segment_ref, x_ref, up_ref, down_ref,
     send_ref, low_ref, back_ref, grad_ref, second_ref, softmax_ref,
-    probs, own_probs, cots, back, first, chosen_rows, bias_rows,
+    cots, back, first, chosen_rows, bias_rows,
 ):
     k = pl.program_id(0)
     key_cat = prompt_block(key_ref)
@@ -146,15 +146,13 @@
         rows = pair_rows(q_ref, pair)
         seen, own = softmax_pair(key_cat, own_key, expand(rows, chosen), rows, bias)
         at = pl.ds(pair * PAIR, PAIR)
-        softmax_ref[0, :TOKENS, at] = seen
-        softmax_ref[0, TOKENS:, at] = own
-        probs[:, at] = seen.astype(BF16)
-        own_probs[:, at] = own.astype(BF16)
+        softmax_ref[0, :TOKENS, at] = seen.astype(BF16)
+        softmax_ref[0, TOKENS:, at] = own.astype(BF16)
         cot = pair_rows(cot_ref, pair)
         cots[at, : PROMPTS * HEAD_DIM] = expand(cot, chosen)
         cots[at, PROMPTS * HEAD_DIM :] = cot
-    spread(send_ref, k, nn(probs[...], cots[:, : PROMPTS * HEAD_DIM]))
-    low = nn(own_probs[...], cots[:, PROMPTS * HEAD_DIM :]).astype(BF16)
+    spread(send_ref, k, nn(softmax_ref[0, :TOKENS, :], cots[:, : PROMPTS * HEAD_DIM]))
+    low = nn(softmax_ref[0, TOKENS:, :], cots[:, PROMPTS * HEAD_DIM :]).astype(BF16)
     low_ref[...] = low
 
     @pl.when(k == 0)
@@ -334,13 +332,13 @@
         at = pl.ds(pair * PAIR, PAIR)
         queries[at, : PROMPTS * HEAD_DIM] = expand(rows, chosen)
         queries[at, PROMPTS * HEAD_DIM :] = rows
-        seen = softmax_ref[0, :TOKENS, at]
-        own = softmax_ref[0, TOKENS:, at]
+        seen = softmax_ref[0, :TOKENS, at].astype(F32)
+        own = softmax_ref[0, TOKENS:, at].astype(F32)
         cot = pair_rows(cot_ref, pair)
         seen_grad = nt(value_cat, expand(cot, chosen))
         own_grad = nt(own_value, cot)
-        delta = jnp.sum(seen.astype(BF16).astype(F32) * seen_grad, axis=0, keepdims=True) + jnp.sum(
-            own.astype(BF16).astype(F32) * own_grad, axis=0, keepdims=True
+        delta = jnp.sum(seen * seen_grad, axis=0, keepdims=True) + jnp.sum(
+            own * own_grad, axis=0, keepdims=True
         )
         grads[:, at] = (seen * (seen_grad - delta)).astype(BF16)
         own_grads[:, at] = (own * (own_grad - delta)).astype(BF16)
@@ -393,11 +391,9 @@
             sent(RANK, TOKENS),
             jax.ShapeDtypeStruct((RANK, D), F32),
             jax.ShapeDtypeStruct((RANK, KV_HEADS * HEAD_DIM), F32),
-            jax.ShapeDtypeStruct((KV_HEADS, 2 * TOKENS, ROWS), F32),
+            sent(KV_HEADS, 2 * TOKENS, ROWS),
         ],
         scratch_shapes=[
-            pltpu.VMEM((TOKENS, ROWS), BF16),
-            pltpu.VMEM((TOKENS, ROWS), BF16),
             pltpu.VMEM((ROWS, (PROMPTS + 1) * HEAD_DIM), BF16),
             pltpu.VMEM((RANK, TOKENS), F32),
             pltpu.VMEM((TOKENS, RANK), BF16),

time: 178 us -> 178 us (level)
  no operation moved by 1% of the time
where the time goes in v8:
time: 178 us; the launch traced here: 177 us
  starting transfers between devices  58.9 us (33%)
  blocking collectives  44.3 us (25%)
  Pallas kernels  32.2 us (18%)
  waiting for transfers between devices  31.6 us (18%)
  matrix products  5.1 us (3%)
  local copies, waits for them, and re-layouts  3.58 us (2%)
    all_to_all x2, blocking collectives, swap(): return lax.all_to_all(array, axis, 0, 0, tiled=True)  44.3 us
    all_to_all x6, starting transfers between devices, swap(): return lax.all_to_all(array, axis, 0, 0, tiled=True)  28.8 us
    all_to_all x6, waiting for transfers between devices, swap(): return lax.all_to_all(array, axis, 0, 0, tiled=True)  22.3 us
    ppermute x3, starting transfers between devices, move(): return lax.ppermute(part, axis, [(i, (i + step) % 4) for i in range(4)])  16.1 us
    ppermute x1, starting transfers between devices, on_device(): other = lax.ppermute(after(weight, *prompts), 'c', [(0, 1), (1, 0)])  14.1 us
    ppermute x3, waiting for transfers between devices, move(): return lax.ppermute(part, axis, [(i, (i + step) % 4) for i in range(4)])  9.3 us
    pallas_call x1, Pallas kernels, attend_forward(): pl.pallas_call(forward_kernel, grid=(KV_HEADS,), in_specs=[pl.BlockSpec(m...  8.37 us
    pallas_call x1, Pallas kernels, project(): pl.pallas_call(project_kernel, grid=(KV_HEADS,), in_specs=[const(TOKENS,...  6.84 us
  transfers between devices with their start and end apart: 10, of which 7 were waited for; matrix products, arithmetic and copies ran while one was open for 3% of the time, Pallas kernels for 15%

profile of v8, /device:TPU:1, one launch (start us, length us, event | category | flops | bytes accessed | tf_op | source)
XLA Modules:
  0.0 177.2 jit_solution(17803462880043084779)
XLA Ops:
  0.7 0.8 copy_bitcast_fusion
  1.6 0.7 pad_maximum_fusion
  2.3 28.8 %all_to_all.40.start_ref = bf16[4,208,128]{2,1,0:T(8,128)(2,1)} all-to-all(bf16[4,208,128]{2,1,0:T(8,128)(2,1)S(1)} %broadcast_in_dim.4), channel_id=1, replica_groups=mesh['x'=4,'zl'=4,'y'=4,'zh'=4,'c'=2] {'zh'}, dimensions={0} | all-to-all | bytes 425984 | tf_op jit(solution)/shard_map/all_to_all | solution.py:31
  31.1 2.4 %weight_copies.1 = bf16[16,528,128]{2,1,0:T(8,128)(2,1)} custom-call(bf16[4,208,128]{2,1,0:T(8,128)(2,1)} %all_to_all.40.start_ref), custom_call_target="tpu_custom_call" | custom-call | tf_op jit(solution)/shard_map/weight_copies/pallas_call | solution.py:425
  33.5 6.9 %all-to-all-start.1 = ((bf16[16,528,128]{2,1,0:T(8,128)(2,1)}), bf16[16,528,128]{2,1,0:T(8,128)(2,1)S(1)}, u32[]{:S(2)}, u32[]{:S(2)}) async-start(bf16[16,528,128]{2,1,0:T(8,128)(2,1)} %weight_copies.1), calls=%async_computation.1 | async-start | bytes 4325376 | tf_op jit(solution)/shard_map/all_to_all | solution.py:31
  40.5 5.5 %collective-permute-start = (bf16[16,4096]{1,0:T(8,128)(2,1)S(1)}, bf16[16,4096]{1,0:T(8,128)(2,1)S(1)}, u32[]{:S(2)}, u32[]{:S(2)}) collective-permute-start(bf16[16,4096]{1,0:T(8,128)(2,1)S(1)} %copy-done.2), channel_id=1, source_target_pairs={{0,2},{2,4},{4,6},{6,0},{1,3},{3,5},{5,7},{7,1},{8,10},{10,12},{12... | collective-permute-start | bytes 393224 | tf_op jit(solution)/shard_map/ppermute | solution.py:528
  45.9 3.7 %collective-permute-start.2 = (bf16[16,4096]{1,0:T(8,128)(2,1)S(1)}, bf16[16,4096]{1,0:T(8,128)(2,1)S(1)}, u32[]{:S(2)}, u32[]{:S(2)}) collective-permute-start(bf16[16,4096]{1,0:T(8,128)(2,1)S(1)} %copy-done.2), channel_id=1, source_target_pairs={{0,6},{2,0},{4,2},{6,4},{1,7},{3,1},{5,3},{7,5},{8,14},{10,8},{12,... | collective-permute-start | bytes 393224 | tf_op jit(solution)/shard_map/ppermute | solution.py:528
  50.2 6.9 %collective-permute-start.1 = (bf16[16,4096]{1,0:T(8,128)(2,1)S(1)}, bf16[16,4096]{1,0:T(8,128)(2,1)S(1)}, u32[]{:S(2)}, u32[]{:S(2)}) collective-permute-start(bf16[16,4096]{1,0:T(8,128)(2,1)S(1)} %collective-permute-done.prompt1_ref), channel_id=1, source_target_pairs={{0,2},{2,4},{4,6},{6,0},{1,3},{3,5},{5,7},{7,1},{8,10},{10,12},{12... | collective-permute-start | bytes 393224 | tf_op jit(solution)/shard_map/ppermute | solution.py:528
  57.1 8.8 %collective-permute-done.1.prompt2_ref = bf16[16,4096]{1,0:T(8,128)(2,1)S(1)} collective-permute-done((bf16[16,4096]{1,0:T(8,128)(2,1)S(1)}, bf16[16,4096]{1,0:T(8,128)(2,1)S(1)}, u32[]{:S(2)}, u32[]{:S(2)}) %collective-permute-start.1) | collective-permute-done | bytes 131104 | tf_op jit(solution)/shard_map/ppermute | solution.py:528
  65.9 14.1 %collective-permute-start.3 = (bf16[4,4,528,128]{3,2,1,0:T(8,128)(2,1)S(1)}, bf16[4,4,528,128]{3,2,1,0:T(8,128)(2,1)}, u32[]{:S(2)}, u32[]{:S(2)}) collective-permute-start(bf16[4,4,528,128]{3,2,1,0:T(8,128)(2,1)S(1)} %bitcast.16), channel_id=1, source_target_pairs={{0,1},{1,0},{2,3},{3,2},{4,5},{5,4},{6,7},{7,6},{8,9},{9,8},{10,11... | collective-permute-start | bytes 6488072 | tf_op jit(solution)/shard_map/ppermute | solution.py:558
  80.0 0.9 broadcast_in_dim.5
  80.9 4.0 %all-to-all-start.2 = ((bf16[8,4,64,128]{3,2,1,0:T(8,128)(2,1)}), bf16[8,4,64,128]{3,2,1,0:T(8,128)(2,1)S(1)}, u32[]{:S(2)}, u32[]{:S(2)}) async-start(bf16[8,4,64,128]{3,2,1,0:T(8,128)(2,1)} %broadcast_in_dim.5), calls=%async_computation.2 | async-start | bytes 1048576 | tf_op jit(solution)/shard_map/all_to_all | solution.py:31
  84.9 6.8 %project.1 = (bf16[128,512]{1,0:T(8,128)(2,1)}, bf16[8,256,128]{2,1,0:T(8,128)(2,1)}, bf16[4096,512]{1,0:T(8,128)(2,1)}, bf16[16,4096]{1,0:T(8,128)(2,1)}) custom-call(bf16[128,4096]{1,0:T(8,128)(2,1)} %x_ref.3, bf16[16,4096]{1,0:T(8,128)(2,1)} %prompt_ref.3, bf16[16,4096]{1,0:T(8,128)(2,1)} %copy-done.4, bf16[16,4096]{1,0:T(8,128)(2,1)} %copy-done.8, ...), custom_call_target="tpu_custom_call" | custom-call | flops 600000000 | bytes 10485760 | tf_op jit(solution)/shard_map/project/pallas_call | solution.py:446
  91.7 2.6 %all-to-all-done.2 = bf16[8,4,64,128]{3,2,1,0:T(8,128)(2,1)S(1)} async-done(((bf16[8,4,64,128]{3,2,1,0:T(8,128)(2,1)}), bf16[8,4,64,128]{3,2,1,0:T(8,128)(2,1)S(1)}, u32[]{:S(2)}, u32[]{:S(2)}) %all-to-all-start.2) | async-done | bytes 524320 | tf_op jit(solution)/shard_map/all_to_all | solution.py:31
  94.3 4.3 %all-to-all-start.3 = ((bf16[8,256,128]{2,1,0:T(8,128)(2,1)}), bf16[8,256,128]{2,1,0:T(8,128)(2,1)S(1)}, u32[]{:S(2)}, u32[]{:S(2)}) async-start(bf16[8,256,128]{2,1,0:T(8,128)(2,1)} %get-tuple-element.40), calls=%async_computation.3 | async-start | bytes 1048576 | tf_op jit(solution)/shard_map/all_to_all | solution.py:31
  98.6 8.4 %attend_forward.1 = (bf16[8,256,128]{2,1,0:T(8,128)(2,1)}, bf16[128,512]{1,0:T(8,128)(2,1)}, bf16[16,128]{1,0:T(8,128)(2,1)}, f32[16,4096]{1,0:T(8,128)}, f32[16...) custom-call(s32[1,8]{1,0:T(1,128)} %choice_ref.3, bf16[128,4096]{1,0:T(8,128)(2,1)} %q_ref.3, bf16[128,4096]{1,0:T(8,128)(2,1)} %cot_ref.3, ...), custom_call_target="tpu_custom_call" | custom-call | flops 2000000000 | bytes 5242880 | tf_op jit(solution)/shard_map/attend_forward/pallas_call | solution.py:366
  107.0 1.1 all-to-all-done.3.value_ref
  108.1 4.3 %all-to-all-start.4 = ((bf16[8,256,128]{2,1,0:T(8,128)(2,1)}), bf16[8,256,128]{2,1,0:T(8,128)(2,1)S(1)}, u32[]{:S(2)}, u32[]{:S(2)}) async-start(bf16[8,256,128]{2,1,0:T(8,128)(2,1)} %get-tuple-element.44), calls=%async_computation.4 | async-start | bytes 1048576 | tf_op jit(solution)/shard_map/all_to_all | solution.py:31
  112.5 6.7 %attend_backward.1 = (bf16[8,256,128]{2,1,0:T(8,128)(2,1)}, bf16[128,512]{1,0:T(8,128)(2,1)}) custom-call(s32[1,8]{1,0:T(1,128)} %choice_ref.3, bf16[128,4096]{1,0:T(8,128)(2,1)} %q_ref.3, bf16[128,4096]{1,0:T(8,128)(2,1)} %cot_ref.3, bf16[4,256,1024]{2,1,0:T(8,128)(2,1)} %get-tuple-element.38.softmax_ref, bf16[8,256,128]{2,1,0:T(8,128)(2,1)} %copy-done.17, ...), custom_call_target="tpu_custom_call" | custom-call | flops 3000000000 | bytes 9437184 | tf_op jit(solution)/shard_map/attend_backward/pallas_call | solution.py:495
  119.1 2.8 %all-to-all-done.4.got_ref = bf16[8,256,128]{2,1,0:T(8,128)(2,1)S(1)} async-done(((bf16[8,256,128]{2,1,0:T(8,128)(2,1)}), bf16[8,256,128]{2,1,0:T(8,128)(2,1)S(1)}, u32[]{:S(2)}, u32[]{:S(2)}) %all-to-all-start.4) | async-done | bytes 524320 | tf_op jit(solution)/shard_map/all_to_all | solution.py:31
  121.9 1.0 copy-done.10
  123.0 0.9 adapter_terms.1
  123.8 15.5 %all_to_all.41.got_ref = bf16[8,384,128]{2,1,0:T(8,128)(2,1)S(1)} all-to-all(bf16[8,384,128]{2,1,0:T(8,128)(2,1)S(1)} %get-tuple-element.47), channel_id=1, replica_groups=mesh['x'=4,'zl'=4,'y'=4,'zh'=4,'c'=2] {'y','c'}, dimensions={0} | all-to-all | bytes 1572864 | tf_op jit(solution)/shard_map/all_to_all | solution.py:31
  139.3 0.8 keys_y.1
  140.1 5.8 %all-to-all-start.6 = ((bf16[4,208,128]{2,1,0:T(8,128)(2,1)}), bf16[4,208,128]{2,1,0:T(8,128)(2,1)S(1)}, u32[]{:S(2)}, u32[]{:S(2)}) async-start(bf16[4,208,128]{2,1,0:T(8,128)(2,1)} %keys_y.1), calls=%async_computation.6 | async-start | bytes 425984 | tf_op jit(solution)/shard_map/all_to_all | solution.py:31
  146.4 4.6 %fusion = bf16[128,4096]{1,0:T(8,128)(2,1)} fusion(f32[128,4096]{1,0:T(8,128)S(1)} %convolution_multiply_fusion, bf16[128,512]{1,0:T(8,128)(2,1)S(1)} %copy-done.18, bf16[4096,512]{1,0:T(8,128)(2,1)} %get-tuple-element.50.weight_ref), kind=kOutput, calls=%fused_computation.2 | convolution fusion | flops 537919488 | bytes 7471104 | tf_op jit(solution)/shard_map/dot_general | solution.py:40
  151.1 9.7 %all-to-all-done.6.got_ref = bf16[4,208,128]{2,1,0:T(8,128)(2,1)S(1)} async-done(((bf16[4,208,128]{2,1,0:T(8,128)(2,1)}), bf16[4,208,128]{2,1,0:T(8,128)(2,1)S(1)}, u32[]{:S(2)}, u32[]{:S(2)}) %all-to-all-start.6) | async-done | bytes 213024 | tf_op jit(solution)/shard_map/all_to_all | solution.py:31
  160.7 0.8 keys_zh.1
  162.1 3.5 %all-to-all-start.7 = ((bf16[16,80,128]{2,1,0:T(8,128)(2,1)}), bf16[16,80,128]{2,1,0:T(8,128)(2,1)S(1)}, u32[]{:S(2)}, u32[]{:S(2)}) async-start(bf16[16,80,128]{2,1,0:T(8,128)(2,1)} %get-tuple-element.57), calls=%async_computation.7 | async-start | bytes 655360 | tf_op jit(solution)/shard_map/all_to_all | solution.py:31
  165.7 4.8 %prompt_gradient.1 = bf16[16,4096]{1,0:T(8,128)(2,1)} custom-call(bf16[16,512]{1,0:T(8,128)(2,1)} %copy-done.14, bf16[16,512]{1,0:T(8,128)(2,1)} %up_ref.7, bf16[16,4096]{1,0:T(8,128)(2,1)} %get-tuple-element.37.down_ref, bf16[4096,512]{1,0:T(8,128)(2,1)} %get-tuple-element.50.weight_ref), custom_call_target="tpu_custom_call" | custom-call | tf_op jit(solution)/shard_map/prompt_gradient/pallas_call | solution.py:477
  170.4 6.2 %all-to-all-done.7.got_ref = bf16[16,80,128]{2,1,0:T(8,128)(2,1)S(1)} async-done(((bf16[16,80,128]{2,1,0:T(8,128)(2,1)}), bf16[16,80,128]{2,1,0:T(8,128)(2,1)S(1)}, u32[]{:S(2)}, u32[]{:S(2)}) %all-to-all-start.7) | async-done | bytes 327712 | tf_op jit(solution)/shard_map/all_to_all | solution.py:31
  176.6 0.7 over_group.1
  (48 shorter events, 1.8 us)
Async XLA Ops:
  0.6 0.9 copy-start
  33.5 6.9 %copy-start.2 = (bf16[16,4096]{1,0:T(8,128)(2,1)S(1)}, bf16[16,4096]{1,0:T(8,128)(2,1)}, u32[]{:S(2)}) copy-start(bf16[16,4096]{1,0:T(8,128)(2,1)} %prompt_ref.3) | copy-start | bytes 393220
  33.5 46.4 %slice-start = ((bf16[4,208,128]{2,1,0:T(8,128)(2,1)}), bf16[4,64,128]{2,1,0:T(8,128)(2,1)S(1)}, s32[]{:S(2)}) async-start(bf16[4,208,128]{2,1,0:T(8,128)(2,1)} %all_to_all.40.start_ref), calls=%async_computation.8 | async-start | bytes 131072 | tf_op jit(solution)/shard_map/slice | solution.py:559
  33.5 32.3 %all-to-all-start.1 = ((bf16[16,528,128]{2,1,0:T(8,128)(2,1)}), bf16[16,528,128]{2,1,0:T(8,128)(2,1)S(1)}, u32[]{:S(2)}, u32[]{:S(2)}) async-start(bf16[16,528,128]{2,1,0:T(8,128)(2,1)} %weight_copies.1), calls=%async_computation.1 | async-start | bytes 4325376 | tf_op jit(solution)/shard_map/all_to_all | solution.py:31
  40.5 9.7 %collective-permute-start = (bf16[16,4096]{1,0:T(8,128)(2,1)S(1)}, bf16[16,4096]{1,0:T(8,128)(2,1)S(1)}, u32[]{:S(2)}, u32[]{:S(2)}) collective-permute-start(bf16[16,4096]{1,0:T(8,128)(2,1)S(1)} %copy-done.2), channel_id=1, source_target_pairs={{0,2},{2,4},{4,6},{6,0},{1,3},{3,5},{5,7},{7,1},{8,10},{10,12},{12... | collective-permute-start | bytes 393224 | tf_op jit(solution)/shard_map/ppermute | solution.py:528
  45.9 11.1 %collective-permute-start.2 = (bf16[16,4096]{1,0:T(8,128)(2,1)S(1)}, bf16[16,4096]{1,0:T(8,128)(2,1)S(1)}, u32[]{:S(2)}, u32[]{:S(2)}) collective-permute-start(bf16[16,4096]{1,0:T(8,128)(2,1)S(1)} %copy-done.2), channel_id=1, source_target_pairs={{0,6},{2,0},{4,2},{6,4},{1,7},{3,1},{5,3},{7,5},{8,14},{10,8},{12,... | collective-permute-start | bytes 393224 | tf_op jit(solution)/shard_map/ppermute | solution.py:528
  50.2 34.7 %copy-start.4 = (bf16[16,4096]{1,0:T(8,128)(2,1)}, bf16[16,4096]{1,0:T(8,128)(2,1)S(1)}, u32[]{:S(2)}) copy-start(bf16[16,4096]{1,0:T(8,128)(2,1)S(1)} %collective-permute-done.prompt1_ref) | copy-start | bytes 393220
  50.2 15.7 %collective-permute-start.1 = (bf16[16,4096]{1,0:T(8,128)(2,1)S(1)}, bf16[16,4096]{1,0:T(8,128)(2,1)S(1)}, u32[]{:S(2)}, u32[]{:S(2)}) collective-permute-start(bf16[16,4096]{1,0:T(8,128)(2,1)S(1)} %collective-permute-done.prompt1_ref), channel_id=1, source_target_pairs={{0,2},{2,4},{4,6},{6,0},{1,3},{3,5},{5,7},{7,1},{8,10},{10,12},{12... | collective-permute-start | bytes 393224 | tf_op jit(solution)/shard_map/ppermute | solution.py:528
  57.1 27.8 %copy-start.6 = (bf16[16,4096]{1,0:T(8,128)(2,1)}, bf16[16,4096]{1,0:T(8,128)(2,1)S(1)}, u32[]{:S(2)}) copy-start(bf16[16,4096]{1,0:T(8,128)(2,1)S(1)} %collective-permute-done.2.prompt3_ref) | copy-start | bytes 393220
  65.9 19.0 %copy-start.8 = (bf16[16,4096]{1,0:T(8,128)(2,1)}, bf16[16,4096]{1,0:T(8,128)(2,1)S(1)}, u32[]{:S(2)}) copy-start(bf16[16,4096]{1,0:T(8,128)(2,1)S(1)} %collective-permute-done.1.prompt2_ref) | copy-start | bytes 393220
  65.9 19.0 %copy-start.15 = (bf16[16,528,128]{2,1,0:T(8,128)(2,1)}, bf16[16,528,128]{2,1,0:T(8,128)(2,1)S(1)}, u32[]{:S(2)}) copy-start(bf16[16,528,128]{2,1,0:T(8,128)(2,1)S(1)} %all-to-all-done.1) | copy-start | bytes 6488068
  65.9 19.0 %collective-permute-start.3 = (bf16[4,4,528,128]{3,2,1,0:T(8,128)(2,1)S(1)}, bf16[4,4,528,128]{3,2,1,0:T(8,128)(2,1)}, u32[]{:S(2)}, u32[]{:S(2)}) collective-permute-start(bf16[4,4,528,128]{3,2,1,0:T(8,128)(2,1)S(1)} %bitcast.16), channel_id=1, source_target_pairs={{0,1},{1,0},{2,3},{3,2},{4,5},{5,4},{6,7},{7,6},{8,9},{9,8},{10,11... | collective-permute-start | bytes 6488072 | tf_op jit(solution)/shard_map/ppermute | solution.py:558
  80.9 13.5 %all-to-all-start.2 = ((bf16[8,4,64,128]{3,2,1,0:T(8,128)(2,1)}), bf16[8,4,64,128]{3,2,1,0:T(8,128)(2,1)S(1)}, u32[]{:S(2)}, u32[]{:S(2)}) async-start(bf16[8,4,64,128]{3,2,1,0:T(8,128)(2,1)} %broadcast_in_dim.5), calls=%async_computation.2 | async-start | bytes 1048576 | tf_op jit(solution)/shard_map/all_to_all | solution.py:31
  94.3 4.3 %copy-start.16 = (bf16[8,4,64,128]{3,2,1,0:T(8,128)(2,1)}, bf16[8,4,64,128]{3,2,1,0:T(8,128)(2,1)S(1)}, u32[]{:S(2)}) copy-start(bf16[8,4,64,128]{3,2,1,0:T(8,128)(2,1)S(1)} %all-to-all-done.2) | copy-start | bytes 1572868
  94.3 13.8 %all-to-all-start.3 = ((bf16[8,256,128]{2,1,0:T(8,128)(2,1)}), bf16[8,256,128]{2,1,0:T(8,128)(2,1)S(1)}, u32[]{:S(2)}, u32[]{:S(2)}) async-start(bf16[8,256,128]{2,1,0:T(8,128)(2,1)} %get-tuple-element.40), calls=%async_computation.3 | async-start | bytes 1048576 | tf_op jit(solution)/shard_map/all_to_all | solution.py:31
  108.1 4.3 %copy-start.17 = (bf16[8,256,128]{2,1,0:T(8,128)(2,1)}, bf16[8,256,128]{2,1,0:T(8,128)(2,1)S(1)}, u32[]{:S(2)}) copy-start(bf16[8,256,128]{2,1,0:T(8,128)(2,1)S(1)} %all-to-all-done.3.value_ref) | copy-start | bytes 1572868
  108.1 13.8 %all-to-all-start.4 = ((bf16[8,256,128]{2,1,0:T(8,128)(2,1)}), bf16[8,256,128]{2,1,0:T(8,128)(2,1)S(1)}, u32[]{:S(2)}, u32[]{:S(2)}) async-start(bf16[8,256,128]{2,1,0:T(8,128)(2,1)} %get-tuple-element.44), calls=%async_computation.4 | async-start | bytes 1048576 | tf_op jit(solution)/shard_map/all_to_all | solution.py:31
  112.4 9.5 %copy-start.1 = (bf16[16,4096]{1,0:T(8,128)(2,1)S(1)}, bf16[16,4096]{1,0:T(8,128)(2,1)}, u32[]{:S(2)}) copy-start(bf16[16,4096]{1,0:T(8,128)(2,1)} %get-tuple-element.37.down_ref) | copy-start | bytes 393220
  112.4 9.5 %copy-start.3 = (bf16[16,4096]{1,0:T(8,128)(2,1)S(1)}, bf16[16,4096]{1,0:T(8,128)(2,1)}, u32[]{:S(2)}) copy-start(bf16[16,4096]{1,0:T(8,128)(2,1)} %prompt_ref.3) | copy-start | bytes 393220
  112.4 9.5 %copy-start.5 = (bf16[16,4096]{1,0:T(8,128)(2,1)S(1)}, bf16[16,4096]{1,0:T(8,128)(2,1)}, u32[]{:S(2)}) copy-start(bf16[16,4096]{1,0:T(8,128)(2,1)} %copy-done.4) | copy-start | bytes 393220
  112.4 9.5 %copy-start.7 = (bf16[16,4096]{1,0:T(8,128)(2,1)S(1)}, bf16[16,4096]{1,0:T(8,128)(2,1)}, u32[]{:S(2)}) copy-start(bf16[16,4096]{1,0:T(8,128)(2,1)} %copy-done.6) | copy-start | bytes 393220
  112.4 9.5 %copy-start.9 = (bf16[16,4096]{1,0:T(8,128)(2,1)S(1)}, bf16[16,4096]{1,0:T(8,128)(2,1)}, u32[]{:S(2)}) copy-start(bf16[16,4096]{1,0:T(8,128)(2,1)} %copy-done.8) | copy-start | bytes 393220
  112.4 9.5 %copy-start.11 = (f32[16,4096]{1,0:T(8,128)S(1)}, f32[16,4096]{1,0:T(8,128)}, u32[]{:S(2)}) copy-start(f32[16,4096]{1,0:T(8,128)} %get-tuple-element.45.grad_ref) | copy-start | bytes 786436
  112.4 9.5 %copy-start.12 = (bf16[16,512]{1,0:T(8,128)(2,1)S(1)}, bf16[16,512]{1,0:T(8,128)(2,1)}, u32[]{:S(2)}) copy-start(bf16[16,512]{1,0:T(8,128)(2,1)} %up_ref.7) | copy-start | bytes 49156
  112.4 9.5 %copy-start.13 = (f32[16,512]{1,0:T(8,128)S(1)}, f32[16,512]{1,0:T(8,128)}, u32[]{:S(2)}) copy-start(f32[16,512]{1,0:T(8,128)} %get-tuple-element.46.second_ref) | copy-start | bytes 98308
  121.9 1.0 copy-start.10
  123.0 23.0 %copy-start.19 = (bf16[16,128]{1,0:T(8,128)(2,1)S(1)}, bf16[16,128]{1,0:T(8,128)(2,1)}, u32[]{:S(2)}) copy-start(bf16[16,128]{1,0:T(8,128)(2,1)} %get-tuple-element.51) | copy-start | bytes 12292
  139.3 7.1 %copy-start.18 = (bf16[128,512]{1,0:T(8,128)(2,1)S(1)}, bf16[128,512]{1,0:T(8,128)(2,1)}, u32[]{:S(2)}) copy-start(bf16[128,512]{1,0:T(8,128)(2,1)} %get-tuple-element.49) | copy-start | bytes 393220
  140.1 20.6 %all-to-all-start.6 = ((bf16[4,208,128]{2,1,0:T(8,128)(2,1)}), bf16[4,208,128]{2,1,0:T(8,128)(2,1)S(1)}, u32[]{:S(2)}, u32[]{:S(2)}) async-start(bf16[4,208,128]{2,1,0:T(8,128)(2,1)} %keys_y.1), calls=%async_computation.6 | async-start | bytes 425984 | tf_op jit(solution)/shard_map/all_to_all | solution.py:31
  161.5 0.6 copy-start.14
  162.1 14.5 %all-to-all-start.7 = ((bf16[16,80,128]{2,1,0:T(8,128)(2,1)}), bf16[16,80,128]{2,1,0:T(8,128)(2,1)S(1)}, u32[]{:S(2)}, u32[]{:S(2)}) async-start(bf16[16,80,128]{2,1,0:T(8,128)(2,1)} %get-tuple-element.57), calls=%async_computation.7 | async-start | bytes 655360 | tf_op jit(solution)/shard_map/all_to_all | solution.py:31
